TPU v7x, 32 devices: a whole 2x2x4 slice. The times are simulated.
32 devices in a mesh: tm: 32 (over z, y, x, core).
Axes of the slice: x: 2, y: 2, z: 4, core: 2. Of those that a mesh axis runs over, the one named last changes fastest.
Arguments:
- diag_blocks: float32 [128, 512, 512], P('tm'), as said below
- lower_blocks: float32 [128, 512, 512], P('tm')
- arrow_blocks: float32 [128, 64, 512], P('tm')
- tip_block: float32 [64, 64], replicated, as said below
Outputs:
- pair_fronts: float32 [17408, 1088], P('tm')
- tip_schur: float32 [64, 64], replicated
Inputs may be any that keep to these rules, and one draw needn't show every extreme that they name: `diag_blocks`: every block is symmetric, and the matrix that Q forms over all time blocks is positive definite. `tip_block`: symmetric.
All inputs are finite; a program needn't handle non-finite values.
Results may differ from a plain program's by a relative error of at most 0.0003.
Values sent between devices are 32-bit elements; how exact they have to be, the bound alone decides.
No kernel may reach another device: no remote copies, remote signals or barrier semaphores. Data moves between devices by JAX's collectives and lax.ppermute only.
A program may use at most 128 MiB of HBM per device.

v0:
```python
import jax
import jax.numpy as jnp
from jax import lax
from jax.sharding import PartitionSpec as P

highest = lax.Precision.HIGHEST


def shifted(value, axis, steps):
    count = lax.axis_size(axis)
    first, last = (max(0, -steps), min(count, count - steps))
    return lax.ppermute(value, axis, [(source, source + steps) for source in range(first, last)])


def factor_and_scale(pivot_block, coupling):
    factor = jnp.linalg.cholesky(pivot_block)
    return lax.linalg.triangular_solve(factor, coupling, left_side=True, lower=True)


def eliminate(pivot_block, coupling, outer_block):
    scaled = factor_and_scale(pivot_block, coupling)
    return outer_block - jnp.dot(
        scaled.T, scaled, precision=highest, preferred_element_type=jnp.float32
    )


def partition_front(diag_part, lower_part, arrow_part):
    count = diag_part.shape[0]
    width = diag_part.shape[1]
    tip_width = arrow_part.shape[1]
    square_zero = jnp.zeros((width, width), jnp.float32)
    front = jnp.block(
        [
            [diag_part[0], lower_part[0].T, arrow_part[0].T],
            [lower_part[0], diag_part[1], arrow_part[1].T],
            [arrow_part[0], arrow_part[1], jnp.zeros((tip_width, tip_width), jnp.float32)],
        ]
    )
    for index in range(1, count - 1):
        current = front[width : 2 * width]
        coupling = jnp.concatenate(
            [current[:, :width], lower_part[index].T, current[:, 2 * width :]], axis=1
        )
        outer_block = jnp.block(
            [
                [front[:width, :width], square_zero, front[:width, 2 * width :]],
                [square_zero, diag_part[index + 1], arrow_part[index + 1].T],
                [
                    front[2 * width :, :width],
                    arrow_part[index + 1],
                    front[2 * width :, 2 * width :],
                ],
            ]
        )
        front = eliminate(current[:, width : 2 * width], coupling, outer_block)
    return front


def condense(front, link):
    width = link.shape[0]
    tip_width = front.shape[0] - 2 * width
    square_zero = jnp.zeros((width, width), jnp.float32)
    side_zero = jnp.zeros((width, tip_width), jnp.float32)
    right_rows = front[width : 2 * width]
    coupling = jnp.concatenate([right_rows[:, :width], link.T, right_rows[:, 2 * width :]], axis=1)
    outer_block = jnp.block(
        [
            [front[:width, :width], square_zero, front[:width, 2 * width :]],
            [square_zero, square_zero, side_zero],
            [front[2 * width :, :width], side_zero.T, front[2 * width :, 2 * width :]],
        ]
    )
    return eliminate(right_rows[:, width : 2 * width], coupling, outer_block)


def joined_system(condensed, right_front, width):
    double = 2 * width
    square_zero = jnp.zeros((width, width), jnp.float32)
    pivot_block = condensed[width:double, width:double] + right_front[:width, :width]
    coupling = jnp.concatenate(
        [
            condensed[width:double, :width],
            right_front[:width, width:double],
            condensed[width:double, double:] + right_front[:width, double:],
        ],
        axis=1,
    )
    outer_block = jnp.block(
        [
            [condensed[:width, :width], square_zero, condensed[:width, double:]],
            [
                square_zero,
                right_front[width:double, width:double],
                right_front[width:double, double:],
            ],
            [
                condensed[double:, :width],
                right_front[double:, width:double],
                condensed[double:, double:] + right_front[double:, double:],
            ],
        ]
    )
    return (pivot_block, coupling, outer_block)


def merge_front(condensed, right_front, width):
    pivot_block, coupling, outer_block = joined_system(condensed, right_front, width)
    return eliminate(pivot_block, coupling, outer_block)


def local(diag_blocks, lower_blocks, arrow_blocks, tip_block):
    width = diag_blocks.shape[1]
    front = partition_front(diag_blocks, lower_blocks, arrow_blocks)
    half = front.shape[0] // 2
    parity = lax.axis_index("tm") % 2
    is_left = parity == 0
    outgoing = lax.cond(is_left, lambda: condense(front, lower_blocks[-1]), lambda: front)
    received = shifted(outgoing, "tm", 1)
    merged = lax.cond(
        is_left, lambda: jnp.zeros_like(front), lambda: merge_front(received, front, width)
    )
    returned = shifted(merged[:half], "tm", -1)
    mine = jnp.where(is_left, returned, merged[half:])
    tip_rows = mine[2 * width - half :, 2 * width :]
    contribution = jnp.where(is_left, jnp.zeros_like(tip_rows), tip_rows)
    tip_schur = tip_block + lax.psum(contribution, "tm")
    return (mine, tip_schur)


def solution(mesh):
    placed = (P("tm", None, None), P("tm", None, None), P("tm", None, None), P())
    return jax.shard_map(
        local, mesh=mesh, in_specs=placed, out_specs=(P("tm", None), P()), check_vma=False
    )
```

profile of v0, /device:TPU:0, one launch (start us, length us, event | category | flops | bytes accessed | tf_op | source)
XLA Modules:
  0.0 915.0 jit_solution(6667492256306219521)
XLA Ops:
  18.7 11.7 %cholesky.606 = f32[128,128]{1,0:T(8,128)S(1)} custom-call(f32[128,128]{1,0:T(8,128)S(1)} %cholesky.772), custom_call_target="Cholesky" | custom-call | tf_op jit(solution)/shard_map/jit(cholesky)/cholesky | solution.py:16
  43.6 12.8 %cholesky.625 = f32[128,128]{1,0:T(8,128)S(1)} custom-call(f32[128,128]{1,0:T(8,128)} %cholesky.776), custom_call_target="Cholesky" | custom-call | tf_op jit(solution)/shard_map/jit(cholesky)/cholesky | solution.py:16
  69.2 11.7 %cholesky.646 = f32[128,128]{1,0:T(8,128)S(1)} custom-call(f32[128,128]{1,0:T(8,128)S(1)} %cholesky.781), custom_call_target="Cholesky" | custom-call | tf_op jit(solution)/shard_map/jit(cholesky)/cholesky | solution.py:16
  92.2 23.1 %cholesky.663 = f32[128,128]{1,0:T(8,128)S(1)} custom-call(f32[128,128]{1,0:T(8,128)S(1)} %convolution_subtract_fusion.27), custom_call_target="Cholesky" | custom-call | tf_op jit(solution)/shard_map/jit(cholesky)/cholesky | solution.py:16
  121.2 12.0 %while.10 = (s32[]{:T(128)}, f32[512,512]{1,0:T(8,128)}, s32[4,2]{0,1:T(2,128)S(1)}, f32[4,128,128]{2,1,0:T(8,128)S(1)}, s32[]{:T(128)}) while((s32[]{:T(128)}, f32[512,512]{1,0:T(8,128)}, s32[4,2]{0,1:T(2,128)S(1)}, f32[4,128,128]{2,1,0:T(8,128)S(1)}, s32[]{:T(128)}) %tuple.139), condition=%wide.while_cond.clone.1, body=%wide.while_body.clone.1.sunk | while | flops 2 | bytes 131189 | solution.py:17
  133.1 39.3 %custom-call.46 = f32[4,128,128]{1,2,0:T(8,128)S(1)} custom-call(f32[4,128,128]{2,1,0:T(8,128)S(1)} %get-tuple-element.51), custom_call_target="InvertDiagBlocksLowerTriangular" | custom-call | tf_op jit(solution)/shard_map/triangular_solve/custom-call.3 | solution.py:17
  203.7 11.7 %cholesky.678 = f32[128,128]{1,0:T(8,128)S(1)} custom-call(f32[128,128]{1,0:T(8,128)S(1)} %cholesky.785), custom_call_target="Cholesky" | custom-call | tf_op jit(solution)/shard_map/jit(cholesky)/cholesky | solution.py:16
  228.5 12.7 %cholesky.697 = f32[128,128]{1,0:T(8,128)S(1)} custom-call(f32[128,128]{1,0:T(8,128)} %cholesky.789), custom_call_target="Cholesky" | custom-call | tf_op jit(solution)/shard_map/jit(cholesky)/cholesky | solution.py:16
  254.1 11.7 %cholesky.718 = f32[128,128]{1,0:T(8,128)S(1)} custom-call(f32[128,128]{1,0:T(8,128)S(1)} %cholesky.794), custom_call_target="Cholesky" | custom-call | tf_op jit(solution)/shard_map/jit(cholesky)/cholesky | solution.py:16
  277.1 11.9 %cholesky.735 = f32[128,128]{1,0:T(8,128)S(1)} custom-call(f32[128,128]{1,0:T(8,128)S(1)} %convolution_subtract_fusion.26), custom_call_target="Cholesky" | custom-call | tf_op jit(solution)/shard_map/jit(cholesky)/cholesky | solution.py:16
  295.6 11.7 %while.11 = (s32[]{:T(128)}, f32[512,512]{1,0:T(8,128)}, s32[4,2]{0,1:T(2,128)S(1)}, f32[4,128,128]{2,1,0:T(8,128)S(1)}, s32[]{:T(128)}) while((s32[]{:T(128)}, f32[512,512]{1,0:T(8,128)}, s32[4,2]{0,1:T(2,128)S(1)}, f32[4,128,128]{2,1,0:T(8,128)S(1)}, s32[]{:T(128)}) %tuple.149), condition=%wide.while_cond.clone.2, body=%wide.while_body.clone.2.sunk | while | flops 2 | bytes 131189 | solution.py:17
  307.3 39.3 %custom-call.50 = f32[4,128,128]{1,2,0:T(8,128)S(1)} custom-call(f32[4,128,128]{2,1,0:T(8,128)S(1)} %get-tuple-element.52), custom_call_target="InvertDiagBlocksLowerTriangular" | custom-call | tf_op jit(solution)/shard_map/triangular_solve/custom-call.3 | solution.py:17
  355.5 14.8 %convolution_subtract_fusion.14 = f32[1088,1088]{0,1:T(8,128)} fusion(f32[512,512]{0,1:T(8,128)S(1)} %copy-done.8, f32[64,64]{0,1:T(8,128)S(1)} %copy-done.31, f32[64,512]{0,1:T(8,128)S(1)} %bitcast.237, f32[64,512]{0,1:T(8,128)S(1)} %copy-done.19, f32[512,64]{0,1:T(8,128)S(1)} %copy-done.26, f32[512,512]{0,1:T(8,128)S(1)} %bitcast.234, ...), kind=kOutput, calls=%fused_computation.163 | convolution fusion | flops 7285248000 | bytes 10649600 | tf_op jit(solution)/shard_map/dot_general | solution.py:22
  370.3 195.4 %conditional.2 = (f32[1088,1088]{0,1:T(8,128)}) conditional(s32[]{:T(128)} %convert_element_type.4, f32[1088,1088]{0,1:T(8,128)} %convolution_subtract_fusion.14, (f32[1088,1088]{0,1:T(8,128)}, f32[4,512,512]{2,1,0:T(8,128)}) %tuple.22), branch_computations={%region_8.11_spmd, %region_9.12_spmd} | conditional | flops 9831608320 | bytes 77271448 | solution.py:117
  393.2 11.7 %cholesky.462 = f32[128,128]{1,0:T(8,128)S(1)} custom-call(f32[128,128]{1,0:T(8,128)S(1)} %cholesky.746), custom_call_target="Cholesky" | custom-call | tf_op jit(solution)/shard_map/cond/branch_1_fun/jit(cholesky)/cholesky | solution.py:16
  418.0 12.5 %cholesky.481 = f32[128,128]{1,0:T(8,128)S(1)} custom-call(f32[128,128]{1,0:T(8,128)} %cholesky.750), custom_call_target="Cholesky" | custom-call | tf_op jit(solution)/shard_map/cond/branch_1_fun/jit(cholesky)/cholesky | solution.py:16
  431.2 10.8 %custom-call.36 = f32[1,128,128]{1,2,0:T(8,128)S(1)} custom-call(f32[1,128,128]{2,1,0:T(8,128)} %get-tuple-element.99), custom_call_target="InvertDiagBlocksLowerTriangular" | custom-call | tf_op jit(solution)/shard_map/cond/branch_1_fun/jit(cholesky)/cholesky | solution.py:16
  443.6 11.7 %cholesky.502 = f32[128,128]{1,0:T(8,128)S(1)} custom-call(f32[128,128]{1,0:T(8,128)S(1)} %cholesky.755), custom_call_target="Cholesky" | custom-call | tf_op jit(solution)/shard_map/cond/branch_1_fun/jit(cholesky)/cholesky | solution.py:16
  466.6 12.1 %cholesky.519 = f32[128,128]{1,0:T(8,128)S(1)} custom-call(f32[128,128]{1,0:T(8,128)S(1)} %convolution_subtract_fusion.6), custom_call_target="Cholesky" | custom-call | tf_op jit(solution)/shard_map/cond/branch_1_fun/jit(cholesky)/cholesky | solution.py:16
  484.0 11.7 %while.8 = (s32[]{:T(128)}, f32[512,512]{1,0:T(8,128)}, s32[4,2]{0,1:T(2,128)S(1)}, f32[4,128,128]{2,1,0:T(8,128)S(1)}, s32[]{:T(128)}) while((s32[]{:T(128)}, f32[512,512]{1,0:T(8,128)}, s32[4,2]{0,1:T(2,128)S(1)}, f32[4,128,128]{2,1,0:T(8,128)S(1)}, s32[]{:T(128)}) %tuple.136), condition=%wide.while_cond, body=%wide.while_body.sunk | while | flops 2 | bytes 131189 | solution.py:17
  495.7 39.3 %custom-call.38 = f32[4,128,128]{1,2,0:T(8,128)S(1)} custom-call(f32[4,128,128]{2,1,0:T(8,128)S(1)} %get-tuple-element.49), custom_call_target="InvertDiagBlocksLowerTriangular" | custom-call | tf_op jit(solution)/shard_map/cond/branch_1_fun/triangular_solve/custom-call.3 | solution.py:17
  543.9 14.9 %convolution_subtract_fusion = f32[1088,1088]{1,0:T(8,128)} fusion(f32[64,64]{1,0:T(8,128)S(1)} %copy-done.32, f32[64,512]{1,0:T(8,128)S(1)} %broadcast.146, f32[64,512]{1,0:T(8,128)S(1)} %copy-done.23, f32[512,64]{1,0:T(8,128)S(1)} %broadcast.145, f32[512,512]{1,0:T(8,128)S(1)} %broadcast.144, f32[512,64]{1,0:T(8,128)S(1)} %copy-done.20, ...), kind=kOutput, calls=%fused_computation.2 | convolution fusion | flops 7285248000 | bytes 9601024 | tf_op jit(solution)/shard_map/cond/branch_1_fun/dot_general | solution.py:22
  586.8 253.6 %collective-permute-done.1 = f32[544,1088]{1,0:T(8,128)S(1)} collective-permute-done((f32[544,1088]{1,0:T(8,128)}, f32[544,1088]{1,0:T(8,128)S(1)}, u32[]{:S(2)}, u32[]{:S(2)}) %collective-permute-start.1) | collective-permute-done | bytes 2367520 | tf_op jit(solution)/shard_map/ppermute | solution.py:12
  848.4 65.4 %psum.7 = f32[64,64]{0,1:T(8,128)S(1)} all-reduce(f32[64,64]{0,1:T(8,128)S(1)} %slice_select_fusion.1), channel_id=1, replica_groups=mesh['tm'=32] {'tm'}, use_global_device_ids=true, to_apply=%region_12.15 | all-reduce | flops 4096 | bytes 32768 | tf_op jit(solution)/shard_map/psum | solution.py:126
  (231 shorter events, 274.6 us)
Async XLA Ops:
  179.1 3.6 copy-start.11
  179.2 3.6 copy-start.12
  179.2 3.6 copy-start.16
  179.2 3.6 copy-start.17
  179.2 3.6 copy-start.27
  179.2 3.6 copy-start.28
  182.7 10.4 %copy-start.7 = (f32[512,512]{0,1:T(8,128)}, f32[512,512]{0,1:T(8,128)S(1)}, u32[]{:S(2)}) copy-start(f32[512,512]{0,1:T(8,128)S(1)} %broadcast.152) | copy-start | bytes 3145732
  193.1 2.5 copy-start
  195.7 2.7 copy-start.1
  352.1 3.4 copy-start.8
  352.1 3.4 copy-start.13
  352.1 3.4 copy-start.14
  352.1 3.4 copy-start.18
  352.1 3.4 copy-start.19
  352.1 3.4 copy-start.25
  352.1 3.4 copy-start.26
  352.2 3.4 copy-start.31
  540.3 3.6 copy-start.9
  540.3 3.5 copy-start.20
  540.3 3.5 copy-start.23
  540.3 3.5 copy-start.32
  565.7 9.6 %collective-permute-start = (f32[1088,1088]{0,1:T(8,128)}, f32[1088,1088]{0,1:T(8,128)}, u32[]{:S(2)}, u32[]{:S(2)}) collective-permute-start(f32[1088,1088]{0,1:T(8,128)} %get-tuple-element.351), channel_id=1, source_target_pairs={{0,1},{1,2},{2,3},{3,4},{4,5},{5,6},{6,7},{7,8},{8,9},{9,10},{10,1... | collective-permute-start | bytes 14204936 | tf_op jit(solution)/shard_map/ppermute | solution.py:12
  583.2 3.5 copy-start.30
  585.4 255.0 %collective-permute-start.1 = (f32[544,1088]{1,0:T(8,128)}, f32[544,1088]{1,0:T(8,128)S(1)}, u32[]{:S(2)}, u32[]{:S(2)}) collective-permute-start(f32[544,1088]{1,0:T(8,128)} %copy.81), channel_id=1, source_target_pairs={{1,0},{2,1},{3,2},{4,3},{5,4},{6,5},{7,6},{8,7},{9,8},{10,9},{11,1... | collective-permute-start | bytes 7102472 | tf_op jit(solution)/shard_map/ppermute | solution.py:12
  (4 other events, 4.8 us)
where the time goes:
time: 926 us; the launch traced here: 915 us
  other arithmetic  386 us (42%)
  waiting for transfers between devices  260 us (28%)
  local copies, waits for them, and re-layouts  103 us (11%)
  matrix products  82 us (9%)
  blocking collectives  65.4 us (7%)
    ppermute x2, waiting for transfers between devices, shifted(): lax.ppermute(value, axis, [(source, source + steps) for source in range(f...  260 us
    another operation x43, other arithmetic, factor_and_scale(): factor = jnp.linalg.cholesky(pivot_block)  255 us
    another operation x9, other arithmetic, factor_and_scale(): lax.linalg.triangular_solve(factor, coupling, left_side=True, lower=True)  121 us
    psum x1, blocking collectives, local(): tip_schur = tip_block + lax.psum(contribution, 'tm')  65.4 us
    dot_general x3, matrix products, eliminate(): jnp.dot(scaled.T, scaled, precision=highest, preferred_element_type=jnp.f...  40 us
    another operation x40, local copies, waits for them, and re-layouts, factor_and_scale(): lax.linalg.triangular_solve(factor, coupling, left_side=True, lower=True)  35.2 us
    another operation x21, matrix products, factor_and_scale(): lax.linalg.triangular_solve(factor, coupling, left_side=True, lower=True)  25.6 us
  transfers between devices with their start and end apart: 2, of which 2 were waited for; matrix products, arithmetic and copies ran while one was open for 0% of the time, Pallas kernels for 0%

commit v1 on v0

v1 whole, which is shorter than its diff:
```python
import functools

import jax
import jax.numpy as jnp
from jax import lax
from jax.experimental import pallas as pl
from jax.experimental.pallas import tpu as pltpu
from jax.sharding import PartitionSpec as P

F32 = jnp.float32
BF16 = jnp.bfloat16
SUB = 8
LANES = 128
HALF = 256
NN = (((1,), (0,)), ((), ()))
NT = (((1,), (1,)), ((), ()))


def split(value):
    high = value.astype(BF16)
    return high, (value - high.astype(F32)).astype(BF16)


def dot3(left, right, dims=NN):
    one = functools.partial(lax.dot_general, dimension_numbers=dims, preferred_element_type=F32)
    return one(left[0], right[0]) + (one(left[0], right[1]) + one(left[1], right[0]))


def row_of(value, index):
    return jnp.broadcast_to(value[index : index + 1, :], (SUB, LANES))


def column_of(value, index):
    return jnp.broadcast_to(value[:, index : index + 1], (SUB, LANES))


def panel_step(state):
    rows, columns = list(state[:16]), list(state[16:])
    sub = lax.broadcasted_iota(jnp.int32, (SUB, LANES), 0)
    lane = lax.broadcasted_iota(jnp.int32, (SUB, LANES), 1)
    panel = lane < SUB
    top = jnp.where(panel, jnp.where(lane == sub, 1.0, 0.0).astype(F32), rows[0])
    for pivot in range(SUB):
        inverse = pl.reciprocal(row_of(columns[pivot], pivot))
        here = sub == pivot
        for index in range(pivot + 1, SUB):
            scaled = row_of(columns[index], pivot) * inverse
            columns[index] = jnp.where(here, scaled, columns[index] - columns[pivot] * scaled)
        scaled = row_of(top, pivot) * inverse
        top = jnp.where(here, scaled, top - columns[pivot] * scaled)
    top_rows = [row_of(top, index) for index in range(SUB)]
    fresh = []
    for index in range(1, 16):
        terms = [column_of(rows[index], k) * top_rows[k] for k in range(SUB)]
        while len(terms) > 1:
            terms = [terms[k] + terms[k + 1] for k in range(0, len(terms), 2)]
        fresh.append(jnp.where(panel, 0.0, rows[index]) - terms[0])
    columns = [column_of(fresh[0], SUB + k) for k in range(SUB)]
    fresh.append(top)
    rows = [pltpu.roll(value, LANES - SUB, 1) for value in fresh]
    return tuple(rows + columns)


def invert_128(blocks):
    states = []
    for block in blocks:
        rows = [block[SUB * k : SUB * (k + 1), :] for k in range(16)]
        states.append(tuple(rows + [column_of(rows[0], k) for k in range(SUB)]))
    states = lax.fori_loop(0, 16, lambda _, carry: tuple(panel_step(s) for s in carry), tuple(states))
    return [jnp.concatenate(state[:16], axis=0) for state in states]


def invert_256(blocks):
    firsts = invert_128([block[0] for block in blocks])
    seconds, sides = [], []
    for first, (_, right, below, last) in zip(firsts, blocks):
        first, right, below = split(first), split(right), split(below)
        low = split(dot3(below, first))
        seconds.append(last - dot3(low, right))
        sides.append((low, split(dot3(first, right))))
    results = []
    for first, second, (low, high) in zip(firsts, invert_128(seconds), sides):
        corner = split(second)
        below = dot3(corner, low)
        top = jnp.concatenate([first + dot3(high, split(below)), -dot3(high, corner)], axis=1)
        bottom = jnp.concatenate([-below, second], axis=1)
        results.append(jnp.concatenate([top, bottom], axis=0))
    return results


def quarters(value):
    return (
        value[:LANES, :LANES],
        value[:LANES, LANES:],
        value[LANES:, :LANES],
        value[LANES:, LANES:],
    )


def chunks(count):
    return [(start, min(HALF, count - start)) for start in range(0, count, HALF)]


def eliminate(systems):
    upper = [split(x) for x in invert_256([quarters(s[0][:HALF, :HALF]) for s in systems])]
    lower = []
    for (pivot, g, gh, gl, zh, zl), inverse in zip(systems, upper):
        right = split(pivot[:HALF, HALF:])
        low = split(dot3(split(pivot[HALF:, :HALF]), inverse))
        lower.append(pivot[HALF:, HALF:] - dot3(low, right))
        for start, size in chunks(g.shape[0]):
            rows = pl.ds(start, size)
            part = split(g[rows, :HALF])
            gh[rows, :HALF], gl[rows, :HALF] = part
            solved = split(dot3(part, inverse))
            zh[rows, :HALF], zl[rows, :HALF] = solved
            part = split(g[rows, HALF:] - dot3(solved, right))
            gh[rows, HALF:], gl[rows, HALF:] = part
    lower = [split(x) for x in invert_256([quarters(value) for value in lower])]
    for (pivot, g, gh, gl, zh, zl), inverse in zip(systems, lower):
        for start, size in chunks(g.shape[0]):
            rows = pl.ds(start, size)
            solved = split(dot3((gh[rows, HALF:], gl[rows, HALF:]), inverse))
            zh[rows, HALF:], zl[rows, HALF:] = solved


def update(system, row, rows, column, columns):
    _, _, gh, gl, zh, zl = system
    row, column = pl.ds(row, rows), pl.ds(column, columns)
    return dot3((zh[row, :], zl[row, :]), (gh[column, :], gl[column, :]), NT)


def transpose_into(target, row, source):
    width = source.shape[1]
    for i in range(0, width, LANES):
        for j in range(0, source.shape[0], LANES):
            target[row + i : row + i + LANES, j : j + LANES] = source[
                j : j + LANES, i : i + LANES
            ].T


def front_kernel(
    side, diag, lower, arrow, pivot_out, pack_out, outer_out,
    dv, lv, av, ga, gah, gal, zah, zal, gb, gbh, gbl, zbh, zbl, pivot, sems,
):
    width, tip = diag.shape[1], arrow.shape[1]
    two = 2 * width
    order = [
        (diag, dv, 1), (diag, dv, 3), (lower, lv, 0), (lower, lv, 1), (lower, lv, 2), (lower, lv, 3),
        (arrow, av, 1), (arrow, av, 3), (diag, dv, 2), (arrow, av, 2), (diag, dv, 0), (arrow, av, 0),
    ]
    copies = [
        pltpu.make_async_copy(source.at[k], target.at[k], sems.at[n])
        for n, (source, target, k) in enumerate(order)
    ]
    for copy in copies:
        copy.start()
    for copy in copies:
        copy.wait()
    is_left = side[0] == 0

    transpose_into(ga, 0, lv.at[0])
    ga[width:two, :] = lv[1]
    ga[two:, :] = av[1]
    gb[:width, :] = lv[3]
    transpose_into(gb, width, lv.at[2])
    gb[two:, :] = av[3]
    first = (dv.at[1], ga, gah, gal, zah, zal)
    third = (dv.at[3], gb, gbh, gbl, zbh, zbl)
    eliminate([first, third])

    def pick(left, right):
        return jnp.where(is_left, left, right)

    def drop(value):
        return jnp.where(is_left, value, jnp.zeros_like(value))

    for start, size in chunks(width):
        rows = pl.ds(start, size)
        shared = pl.ds(width + start, size)
        e = (width + start, size, width, width)
        pivot[rows, :] = dv[2, rows, :] - update(first, *e) - drop(update(third, *e))
        fe = (start, size, width, width)
        near = -update(first, *fe)
        far = -update(third, *fe)
        ga[rows, :] = pick(near, lv[2, rows, :])
        ga[shared, :] = pick(far, near)
        ff = (start, size, 0, width)
        near = dv[0, rows, :] - update(first, *ff)
        far = -update(third, *ff)
        pivot_out[rows, :] = pick(far, near)
        outer_out[rows, :] = pick(near, dv[3, rows, :])
    te = (two, tip, width, width)
    ga[two:, :] = av[2] - update(first, *te) - drop(update(third, *te))
    tf = (two, tip, 0, width)
    near = av[0] - update(first, *tf)
    far = -update(third, *tf)
    tip_pivot = pick(far, near)
    tip_outer = pick(near, av[3])
    tt = (two, tip, two, tip)
    tip_tip = -update(first, *tt) - drop(update(third, *tt))

    second = (pivot, ga, gah, gal, zah, zal)
    eliminate([second])
    for start, size in chunks(width):
        rows = pl.ds(start, size)
        pivot_out[rows, :] = pivot_out[rows, :] - update(second, width + start, size, width, width)
        pack_out[rows, :] = -update(second, start, size, width, width)
        outer_out[rows, :] = outer_out[rows, :] - update(second, start, size, 0, width)
    pack_out[width : width + tip, :] = tip_pivot - update(second, two, tip, width, width)
    pack_out[width + tip : width + 2 * tip, :] = tip_outer - update(second, two, tip, 0, width)
    base = width + 2 * tip
    pack_out[base : base + tip, :] = jnp.zeros((tip, width), F32)
    pack_out[base : base + tip, :tip] = tip_tip - update(second, *tt)
    spill = pack_out.shape[0] - base - tip
    pack_out[base + tip :, :] = outer_out[:spill, :]


def merge_kernel(
    side, pivot_mine, pivot_other, pack_mine, pack_other, outer_mine, merged, tip_out,
    g, gh, gl, zh, zl, pivot,
):
    width = pivot.shape[0]
    tip = tip_out.shape[0]
    two = 2 * width
    base = width + 2 * tip
    half = merged.shape[0]
    spill = half - width
    is_left = side[0] == 0
    pivot[...] = pivot_mine[...] + pivot_other[...]
    for start, size in chunks(width):
        rows = pl.ds(start, size)
        mine, other = pack_mine[rows, :], pack_other[rows, :]
        g[rows, :] = jnp.where(is_left, mine, other)
        g[pl.ds(width + start, size), :] = jnp.where(is_left, other, mine)
    at = pl.ds(width, tip)
    g[two:, :] = pack_mine[at, :] + pack_other[at, :]
    system = (pivot, g, gh, gl, zh, zl)
    eliminate([system])
    at = pl.ds(base, tip)
    tip_tip = pack_mine[at, :tip] + pack_other[at, :tip] - update(system, two, tip, two, tip)
    tip_out[...] = tip_tip
    outer_tip = pl.ds(width + tip, tip)

    @pl.when(is_left)
    def _():
        for start, size in chunks(width):
            rows = pl.ds(start, size)
            merged[rows, :width] = outer_mine[rows, :] - update(system, start, size, 0, width)
            merged[rows, width:two] = -update(system, start, size, width, width)
            mine = pack_mine[outer_tip, start : start + size].T
            merged[rows, two:] = mine - update(system, start, size, two, tip)
        merged[width:, :width] = -update(system, width, spill, 0, width)
        other = pack_other[base + tip :, :]
        merged[width:, width:two] = other - update(system, width, spill, width, width)
        other = pack_other[outer_tip, :LANES].T[:spill, :]
        merged[width:, two:] = other - update(system, width, spill, two, tip)

    @pl.when(jnp.logical_not(is_left))
    def _():
        for start, size in chunks(width):
            skip = spill if start == 0 else 0
            rows = pl.ds(start + skip - spill, size - skip)
            merged[rows, :width] = -update(system, width + start, size, 0, width)[skip:, :]
            mine = outer_mine[pl.ds(start, size), :]
            merged[rows, width:two] = (
                mine - update(system, width + start, size, width, width)
            )[skip:, :]
            mine = pack_mine[outer_tip, start : start + size].T
            merged[rows, two:] = (mine - update(system, width + start, size, two, tip))[skip:, :]
        rows = pl.ds(half - tip, tip)
        merged[rows, :width] = pack_other[outer_tip, :] - update(system, two, tip, 0, width)
        merged[rows, width:two] = pack_mine[outer_tip, :] - update(system, two, tip, width, width)
        merged[rows, two:] = tip_tip


def swapped(value, axis, mask):
    count = lax.axis_size(axis)
    return lax.ppermute(value, axis, [(k, k ^ mask) for k in range(count)])


def sum_over_pairs(value, axis):
    step = 2
    while step < lax.axis_size(axis):
        if 2 * step < lax.axis_size(axis):
            near, far, across = (swapped(value, axis, step * k) for k in (1, 2, 3))
            value = (value + near) + (far + across)
            step *= 4
        else:
            value = value + swapped(value, axis, step)
            step *= 2
    return value


def whole(*shape):
    return pl.BlockSpec(shape, lambda: (0,) * len(shape), memory_space=pltpu.VMEM)


def local(diag_blocks, lower_blocks, arrow_blocks, tip_block):
    count, width = diag_blocks.shape[:2]
    tip = arrow_blocks.shape[1]
    front = 2 * width + tip
    half = front // 2
    spill = half - width
    packed = width + 3 * tip + spill
    side = (lax.axis_index("tm") % 2).astype(jnp.int32).reshape(1)
    smem = pl.BlockSpec(memory_space=pltpu.SMEM)
    system = [pltpu.VMEM((front, width), F32)] + [pltpu.VMEM((front, width), BF16)] * 4
    params = pltpu.CompilerParams(vmem_limit_bytes=56 * 2**20)
    pivot, pack, outer = pl.pallas_call(
        front_kernel,
        out_shape=[
            jax.ShapeDtypeStruct((width, width), F32),
            jax.ShapeDtypeStruct((packed, width), F32),
            jax.ShapeDtypeStruct((width, width), F32),
        ],
        in_specs=[smem] + [pl.BlockSpec(memory_space=pl.ANY)] * 3,
        out_specs=[pl.BlockSpec(memory_space=pltpu.VMEM)] * 3,
        scratch_shapes=[
            pltpu.VMEM((count, width, width), F32),
            pltpu.VMEM((count, width, width), F32),
            pltpu.VMEM((count, tip, width), F32),
        ]
        + system
        + system
        + [pltpu.VMEM((width, width), F32), pltpu.SemaphoreType.DMA((3 * count,))],
        compiler_params=params,
        name="front",
    )(side, diag_blocks, lower_blocks, arrow_blocks)
    pivot_other = swapped(pivot, "tm", 1)
    pack_other = swapped(pack, "tm", 1)
    merged, tip_tip = pl.pallas_call(
        merge_kernel,
        out_shape=[
            jax.ShapeDtypeStruct((half, front), F32),
            jax.ShapeDtypeStruct((tip, tip), F32),
        ],
        in_specs=[smem] + [pl.BlockSpec(memory_space=pltpu.VMEM)] * 5,
        out_specs=[pl.BlockSpec(memory_space=pltpu.VMEM)] * 2,
        scratch_shapes=system + [pltpu.VMEM((width, width), F32)],
        compiler_params=params,
        name="merge",
    )(side, pivot, pivot_other, pack, pack_other, outer)
    return merged, tip_block + sum_over_pairs(tip_tip, "tm")


def solution(mesh):
    placed = (P("tm", None, None), P("tm", None, None), P("tm", None, None), P())
    return jax.shard_map(
        local, mesh=mesh, in_specs=placed, out_specs=(P("tm", None), P()), check_vma=False
    )
```

time: 926 us -> 148 us (0.16); the launches traced: 915 us -> 147 us
  other arithmetic: 386 us -> 1.4 us
  waiting for transfers between devices: 260 us -> 12.7 us
  Pallas kernels: 0 us -> 122 us
  local copies, waits for them, and re-layouts: 103 us -> 1.45 us
  matrix products: 82 us -> 0 us
  blocking collectives: 65.4 us -> 0 us
    another operation x52 -> x0, other arithmetic: 377 us -> none  [the longest x43 255 us: factor_and_scale(): factor = jnp.linalg.cholesky(pivot_block)]
    ppermute x2 -> x8, waiting for transfers between devices: 260 us -> 12.7 us  [swapped(): return lax.ppermute(value, axis, [(k, k ^ mask) for k in range(count)])]
    pallas_call x0 -> x2, Pallas kernels: none -> 122 us  [the longest x1 87.8 us: local(): pl.pallas_call(front_kernel, out_shape=[jax.ShapeDtypeStruct((width, widt...]
    psum x1 -> x0, blocking collectives: 65.4 us -> none  [local(): tip_schur = tip_block + lax.psum(contribution, 'tm')]
    another operation x58 -> x0, local copies, waits for them, and re-layouts: 47.1 us -> none  [the longest x40 35.2 us: factor_and_scale(): lax.linalg.triangular_solve(factor, coupling, left_side=True, lower=True)]
    another operation x39 -> x0, matrix products: 42 us -> none  [the longest x21 25.6 us: factor_and_scale(): lax.linalg.triangular_solve(factor, coupling, left_side=True, lower=True)]
    dot_general x3 -> x0, matrix products: 40 us -> none  [eliminate(): jnp.dot(scaled.T, scaled, precision=highest, preferred_element_type=jnp.f...]
    slice x15 -> x0, local copies, waits for them, and re-layouts: 24 us -> none  [the longest x2 4.27 us: condense(): return eliminate(right_rows[:, width:2 * width], coupling, outer_block)]
  transfers between devices with their start and end apart: 2 -> 8, of which waited for: 2 -> 6; matrix products, arithmetic and copies ran while one was open for 0% -> 0% of each run, Pallas kernels for 0% -> 0%
where the time goes in v1:
time: 148 us; the launch traced here: 147 us
  Pallas kernels  122 us (82%)
  waiting for transfers between devices  12.7 us (9%)
  starting transfers between devices  9.43 us (6%)
    pallas_call x1, Pallas kernels, local(): pl.pallas_call(front_kernel, out_shape=[jax.ShapeDtypeStruct((width, widt...  87.8 us
    pallas_call x1, Pallas kernels, local(): pl.pallas_call(merge_kernel, out_shape=[jax.ShapeDtypeStruct((half, front...  33.9 us
    ppermute x8, waiting for transfers between devices, swapped(): return lax.ppermute(value, axis, [(k, k ^ mask) for k in range(count)])  12.7 us
    ppermute x8, starting transfers between devices, swapped(): return lax.ppermute(value, axis, [(k, k ^ mask) for k in range(count)])  9.43 us
  transfers between devices with their start and end apart: 8, of which 6 were waited for; matrix products, arithmetic and copies ran while one was open for 0% of the time, Pallas kernels for 0%

profile of v1, /device:TPU:0, one launch (start us, length us, event | category | flops | bytes accessed | tf_op | source)
XLA Modules:
  0.0 147.3 jit_solution(8651404952735240152)
XLA Ops:
  0.6 87.8 %front.1 = (f32[512,512]{1,0:T(8,128)}, f32[736,512]{1,0:T(8,128)}, f32[512,512]{1,0:T(8,128)}) custom-call(s32[1]{0:T(128)} %bitcast.side, f32[4,512,512]{2,1,0:T(8,128)} %diag.1, f32[4,512,512]{2,1,0:T(8,128)} %lower.1, f32[4,64,512]{2,1,0:T(8,128)} %arrow.1), custom_call_target="tpu_custom_call" | custom-call | tf_op jit(solution)/shard_map/front/pallas_call | solution.py:310
  88.4 0.5 collective-permute-start.1
  89.0 0.1 collective-permute-start
  89.0 4.6 %collective-permute-done.pivot_other = f32[512,512]{1,0:T(8,128)S(1)} collective-permute-done((f32[512,512]{1,0:T(8,128)}, f32[512,512]{1,0:T(8,128)S(1)}, u32[]{:S(2)}, u32[]{:S(2)}) %collective-permute-start) | collective-permute-done | bytes 1048608 | tf_op jit(solution)/shard_map/ppermute | solution.py:279
  93.6 0.0 copy-start.1
  93.6 0.0 collective-permute-done.1.pack_other
  93.6 1.0 copy-done.1
  94.6 0.4 copy-done
  95.1 33.9 %merge.1 = (f32[544,1088]{1,0:T(8,128)}, f32[64,64]{1,0:T(8,128)}) custom-call(s32[1]{0:T(128)} %bitcast.side, f32[512,512]{1,0:T(8,128)} %get-tuple-element.7.pivot_mine, f32[512,512]{1,0:T(8,128)} %copy-done.1, f32[736,512]{1,0:T(8,128)} %get-tuple-element.8.pack_mine, f32[736,512]{1,0:T(8,128)} %copy-done, f32[512,512]{1,0:T(8,128)} %get-tuple-element.9.outer_mine), custom_call_target="tpu_custom_call" | custom-call | tf_op jit(solution)/shard_map/merge/pallas_call | solution.py:332
  129.0 3.8 %collective-permute-start.4 = (f32[64,64]{1,0:T(8,128)}, f32[64,64]{1,0:T(8,128)S(1)}, u32[]{:S(2)}, u32[]{:S(2)}) collective-permute-start(f32[64,64]{1,0:T(8,128)} %get-tuple-element.11), channel_id=1, source_target_pairs={{0,6},{1,7},{2,4},{3,5},{4,2},{5,3},{6,0},{7,1},{8,14},{9,15},{10,... | collective-permute-start | bytes 49160 | tf_op jit(solution)/shard_map/ppermute | solution.py:279
  132.8 0.5 collective-permute-start.3
  133.3 0.1 collective-permute-start.2
  133.4 1.5 %collective-permute-done.4 = f32[64,64]{1,0:T(8,128)S(1)} collective-permute-done((f32[64,64]{1,0:T(8,128)}, f32[64,64]{1,0:T(8,128)S(1)}, u32[]{:S(2)}, u32[]{:S(2)}) %collective-permute-start.4) | collective-permute-done | bytes 16416 | tf_op jit(solution)/shard_map/ppermute | solution.py:279
  134.9 2.0 %collective-permute-done.3 = f32[64,64]{1,0:T(8,128)S(1)} collective-permute-done((f32[64,64]{1,0:T(8,128)}, f32[64,64]{1,0:T(8,128)S(1)}, u32[]{:S(2)}, u32[]{:S(2)}) %collective-permute-start.3) | collective-permute-done | bytes 16416 | tf_op jit(solution)/shard_map/ppermute | solution.py:279
  137.0 0.5 collective-permute-done.2
  137.5 0.8 add_add_fusion.1
  138.2 3.7 %collective-permute-start.7 = (f32[64,64]{1,0:T(8,128)S(1)}, f32[64,64]{1,0:T(8,128)S(1)}, u32[]{:S(2)}, u32[]{:S(2)}) collective-permute-start(f32[64,64]{1,0:T(8,128)S(1)} %add_add_fusion.1), channel_id=1, source_target_pairs={{0,24},{1,25},{2,26},{3,27},{4,28},{5,29},{6,30},{7,31},{8,16},{9,... | collective-permute-start | bytes 49160 | tf_op jit(solution)/shard_map/ppermute | solution.py:279
  141.9 0.0 collective-permute-start.6
  141.9 0.8 collective-permute-start.5
  142.7 1.4 collective-permute-done.7
  144.1 2.6 %collective-permute-done.6 = f32[64,64]{1,0:T(8,128)S(1)} collective-permute-done((f32[64,64]{1,0:T(8,128)S(1)}, f32[64,64]{1,0:T(8,128)S(1)}, u32[]{:S(2)}, u32[]{:S(2)}) %collective-permute-start.6) | collective-permute-done | bytes 16416 | tf_op jit(solution)/shard_map/ppermute | solution.py:279
  146.7 0.0 collective-permute-done.5
  146.7 0.0 copy-done.2
  146.7 0.6 add_add_fusion
  (2 shorter events, 0.0 us)
Async XLA Ops:
  88.4 5.2 %collective-permute-start.1 = (f32[736,512]{1,0:T(8,128)}, f32[736,512]{1,0:T(8,128)S(1)}, u32[]{:S(2)}, u32[]{:S(2)}) collective-permute-start(f32[736,512]{1,0:T(8,128)} %get-tuple-element.8.pack_mine), channel_id=1, source_target_pairs={{0,1},{1,0},{2,3},{3,2},{4,5},{5,4},{6,7},{7,6},{8,9},{9,8},{10,11... | collective-permute-start | bytes 4521992 | tf_op jit(solution)/shard_map/ppermute | solution.py:279
  89.0 4.7 %collective-permute-start = (f32[512,512]{1,0:T(8,128)}, f32[512,512]{1,0:T(8,128)S(1)}, u32[]{:S(2)}, u32[]{:S(2)}) collective-permute-start(f32[512,512]{1,0:T(8,128)} %get-tuple-element.7.pivot_mine), channel_id=1, source_target_pairs={{0,1},{1,0},{2,3},{3,2},{4,5},{5,4},{6,7},{7,6},{8,9},{9,8},{10,11... | collective-permute-start | bytes 3145736 | tf_op jit(solution)/shard_map/ppermute | solution.py:279
  93.6 1.0 copy-start.1
  93.6 1.4 copy-start
  95.1 51.6 %copy-start.2 = (f32[64,64]{1,0:T(8,128)S(1)}, f32[64,64]{1,0:T(8,128)}, u32[]{:S(2)}) copy-start(f32[64,64]{1,0:T(8,128)} %param.7) | copy-start | bytes 49156
  129.0 5.9 %collective-permute-start.4 = (f32[64,64]{1,0:T(8,128)}, f32[64,64]{1,0:T(8,128)S(1)}, u32[]{:S(2)}, u32[]{:S(2)}) collective-permute-start(f32[64,64]{1,0:T(8,128)} %get-tuple-element.11), channel_id=1, source_target_pairs={{0,6},{1,7},{2,4},{3,5},{4,2},{5,3},{6,0},{7,1},{8,14},{9,15},{10,... | collective-permute-start | bytes 49160 | tf_op jit(solution)/shard_map/ppermute | solution.py:279
  132.8 4.1 %collective-permute-start.3 = (f32[64,64]{1,0:T(8,128)}, f32[64,64]{1,0:T(8,128)S(1)}, u32[]{:S(2)}, u32[]{:S(2)}) collective-permute-start(f32[64,64]{1,0:T(8,128)} %get-tuple-element.11), channel_id=1, source_target_pairs={{0,4},{1,5},{2,6},{3,7},{4,0},{5,1},{6,2},{7,3},{8,12},{9,13},{10,... | collective-permute-start | bytes 49160 | tf_op jit(solution)/shard_map/ppermute | solution.py:279
  133.3 4.1 %collective-permute-start.2 = (f32[64,64]{1,0:T(8,128)}, f32[64,64]{1,0:T(8,128)S(1)}, u32[]{:S(2)}, u32[]{:S(2)}) collective-permute-start(f32[64,64]{1,0:T(8,128)} %get-tuple-element.11), channel_id=1, source_target_pairs={{0,2},{1,3},{2,0},{3,1},{4,6},{5,7},{6,4},{7,5},{8,10},{9,11},{10,... | collective-permute-start | bytes 49160 | tf_op jit(solution)/shard_map/ppermute | solution.py:279
  138.2 5.9 %collective-permute-start.7 = (f32[64,64]{1,0:T(8,128)S(1)}, f32[64,64]{1,0:T(8,128)S(1)}, u32[]{:S(2)}, u32[]{:S(2)}) collective-permute-start(f32[64,64]{1,0:T(8,128)S(1)} %add_add_fusion.1), channel_id=1, source_target_pairs={{0,24},{1,25},{2,26},{3,27},{4,28},{5,29},{6,30},{7,31},{8,16},{9,... | collective-permute-start | bytes 49160 | tf_op jit(solution)/shard_map/ppermute | solution.py:279
  141.9 4.8 %collective-permute-start.6 = (f32[64,64]{1,0:T(8,128)S(1)}, f32[64,64]{1,0:T(8,128)S(1)}, u32[]{:S(2)}, u32[]{:S(2)}) collective-permute-start(f32[64,64]{1,0:T(8,128)S(1)} %add_add_fusion.1), channel_id=1, source_target_pairs={{0,16},{1,17},{2,18},{3,19},{4,20},{5,21},{6,22},{7,23},{8,24},{9,... | collective-permute-start | bytes 49160 | tf_op jit(solution)/shard_map/ppermute | solution.py:279
  141.9 4.8 %collective-permute-start.5 = (f32[64,64]{1,0:T(8,128)S(1)}, f32[64,64]{1,0:T(8,128)S(1)}, u32[]{:S(2)}, u32[]{:S(2)}) collective-permute-start(f32[64,64]{1,0:T(8,128)S(1)} %add_add_fusion.1), channel_id=1, source_target_pairs={{0,8},{1,9},{2,10},{3,11},{4,12},{5,13},{6,14},{7,15},{8,0},{9,1},... | collective-permute-start | bytes 49160 | tf_op jit(solution)/shard_map/ppermute | solution.py:279

commit v2 on v1

--- a/solution.py
+++ b/solution.py
@@ -34,30 +34,45 @@
     return jnp.broadcast_to(value[:, index : index + 1], (SUB, LANES))
 
 
-def panel_step(state):
+def total(terms):
+    while len(terms) > 1:
+        terms = [terms[k] + terms[k + 1] for k in range(0, len(terms), 2)]
+    return terms[0]
+
+
+def cleared(value, start, top):
+    lane = lax.broadcasted_iota(jnp.int32, (SUB, LANES), 1)
+    panel = (lane >= start) & (lane < start + SUB)
+    terms = [column_of(value, start + k) * top[k] for k in range(SUB)]
+    return jnp.where(panel, 0.0, value) - total(terms)
+
+
+def late_update(rows):
+    top = [row_of(rows[15], k) for k in range(SUB)]
+    return rows[:1] + [cleared(value, LANES - SUB, top) for value in rows[1:15]] + rows[15:]
+
+
+def panel_step(state, late):
     rows, columns = list(state[:16]), list(state[16:])
     sub = lax.broadcasted_iota(jnp.int32, (SUB, LANES), 0)
     lane = lax.broadcasted_iota(jnp.int32, (SUB, LANES), 1)
-    panel = lane < SUB
-    top = jnp.where(panel, jnp.where(lane == sub, 1.0, 0.0).astype(F32), rows[0])
+    if late:
+        rows = late_update(rows)
+    top = jnp.where(lane < SUB, jnp.where(lane == sub, 1.0, 0.0).astype(F32), rows[0])
     for pivot in range(SUB):
-        inverse = pl.reciprocal(row_of(columns[pivot], pivot))
+        inverse = pltpu.reciprocal(row_of(columns[pivot], pivot))
         here = sub == pivot
-        for index in range(pivot + 1, SUB):
-            scaled = row_of(columns[index], pivot) * inverse
-            columns[index] = jnp.where(here, scaled, columns[index] - columns[pivot] * scaled)
-        scaled = row_of(top, pivot) * inverse
-        top = jnp.where(here, scaled, top - columns[pivot] * scaled)
-    top_rows = [row_of(top, index) for index in range(SUB)]
-    fresh = []
-    for index in range(1, 16):
-        terms = [column_of(rows[index], k) * top_rows[k] for k in range(SUB)]
-        while len(terms) > 1:
-            terms = [terms[k] + terms[k + 1] for k in range(0, len(terms), 2)]
-        fresh.append(jnp.where(panel, 0.0, rows[index]) - terms[0])
-    columns = [column_of(fresh[0], SUB + k) for k in range(SUB)]
-    fresh.append(top)
-    rows = [pltpu.roll(value, LANES - SUB, 1) for value in fresh]
+
+        def eliminated(value):
+            row = row_of(value, pivot)
+            product = columns[pivot] * row
+            return jnp.where(here, row * inverse, value - product * inverse)
+
+        columns[pivot + 1 :] = [eliminated(value) for value in columns[pivot + 1 :]]
+        top = eliminated(top)
+    following = cleared(rows[1], 0, [row_of(top, k) for k in range(SUB)])
+    columns = [column_of(following, SUB + k) for k in range(SUB)]
+    rows = [pltpu.roll(value, LANES - SUB, 1) for value in [following] + rows[2:] + [top]]
     return tuple(rows + columns)
 
 
@@ -65,9 +80,12 @@
     states = []
     for block in blocks:
         rows = [block[SUB * k : SUB * (k + 1), :] for k in range(16)]
-        states.append(tuple(rows + [column_of(rows[0], k) for k in range(SUB)]))
-    states = lax.fori_loop(0, 16, lambda _, carry: tuple(panel_step(s) for s in carry), tuple(states))
-    return [jnp.concatenate(state[:16], axis=0) for state in states]
+        columns = [column_of(rows[0], k) for k in range(SUB)]
+        states.append(panel_step(tuple(rows + columns), False))
+    states = lax.fori_loop(
+        1, 16, lambda _, carry: tuple(panel_step(s, True) for s in carry), tuple(states)
+    )
+    return [jnp.concatenate(late_update(list(state[:16])), axis=0) for state in states]
 
 
 def invert_256(blocks):
@@ -101,20 +119,38 @@
     return [(start, min(HALF, count - start)) for start in range(0, count, HALF)]
 
 
+def equilibrate(pivot):
+    width = pivot.shape[0]
+    row = lax.broadcasted_iota(jnp.int32, (LANES, LANES), 0)
+    lane = lax.broadcasted_iota(jnp.int32, (LANES, LANES), 1)
+    scales = []
+    for start in range(0, width, LANES):
+        block = pivot[start : start + LANES, start : start + LANES]
+        scales.append(lax.rsqrt(jnp.sum(jnp.where(row == lane, block, 0.0), axis=0, keepdims=True)))
+    for index, scale in enumerate(scales):
+        rows = pl.ds(index * LANES, LANES)
+        down = jnp.broadcast_to(scale, (LANES, LANES)).T
+        for other, across in enumerate(scales):
+            lanes = pl.ds(other * LANES, LANES)
+            pivot[rows, lanes] = pivot[rows, lanes] * down * across
+    return jnp.concatenate(scales, axis=1)
+
+
 def eliminate(systems):
+    scales = [equilibrate(system[0]) for system in systems]
     upper = [split(x) for x in invert_256([quarters(s[0][:HALF, :HALF]) for s in systems])]
     lower = []
-    for (pivot, g, gh, gl, zh, zl), inverse in zip(systems, upper):
+    for (pivot, g, gh, gl, zh, zl), inverse, scale in zip(systems, upper, scales):
         right = split(pivot[:HALF, HALF:])
         low = split(dot3(split(pivot[HALF:, :HALF]), inverse))
         lower.append(pivot[HALF:, HALF:] - dot3(low, right))
         for start, size in chunks(g.shape[0]):
             rows = pl.ds(start, size)
-            part = split(g[rows, :HALF])
+            part = split(g[rows, :HALF] * scale[:, :HALF])
             gh[rows, :HALF], gl[rows, :HALF] = part
             solved = split(dot3(part, inverse))
             zh[rows, :HALF], zl[rows, :HALF] = solved
-            part = split(g[rows, HALF:] - dot3(solved, right))
+            part = split(g[rows, HALF:] * scale[:, HALF:] - dot3(solved, right))
             gh[rows, HALF:], gl[rows, HALF:] = part
     lower = [split(x) for x in invert_256([quarters(value) for value in lower])]
     for (pivot, g, gh, gl, zh, zl), inverse in zip(systems, lower):
@@ -167,6 +203,7 @@
     gb[two:, :] = av[3]
     first = (dv.at[1], ga, gah, gal, zah, zal)
     third = (dv.at[3], gb, gbh, gbl, zbh, zbl)
+    outer_out[...] = dv[3]
     eliminate([first, third])
 
     def pick(left, right):
@@ -189,7 +226,7 @@
         near = dv[0, rows, :] - update(first, *ff)
         far = -update(third, *ff)
         pivot_out[rows, :] = pick(far, near)
-        outer_out[rows, :] = pick(near, dv[3, rows, :])
+        outer_out[rows, :] = pick(near, outer_out[rows, :])
     te = (two, tip, width, width)
     ga[two:, :] = av[2] - update(first, *te) - drop(update(third, *te))
     tf = (two, tip, 0, width)

time: 148 us -> 160 us (1.081)
  Pallas kernels: 122 us -> 134 us
    pallas_call x1, Pallas kernels: 87.8 us -> 97.9 us  [local(): pl.pallas_call(front_kernel, out_shape=[jax.ShapeDtypeStruct((width, widt...]
    pallas_call x1, Pallas kernels: 33.9 us -> 35.9 us  [local(): pl.pallas_call(merge_kernel, out_shape=[jax.ShapeDtypeStruct((half, front...]
where the time goes in v2:
time: 160 us; the launch traced here: 159 us
  Pallas kernels  134 us (84%)
  waiting for transfers between devices  12.7 us (8%)
  starting transfers between devices  9.43 us (6%)
    pallas_call x1, Pallas kernels, local(): pl.pallas_call(front_kernel, out_shape=[jax.ShapeDtypeStruct((width, widt...  97.9 us
    pallas_call x1, Pallas kernels, local(): pl.pallas_call(merge_kernel, out_shape=[jax.ShapeDtypeStruct((half, front...  35.9 us
    ppermute x8, waiting for transfers between devices, swapped(): return lax.ppermute(value, axis, [(k, k ^ mask) for k in range(count)])  12.7 us
    ppermute x8, starting transfers between devices, swapped(): return lax.ppermute(value, axis, [(k, k ^ mask) for k in range(count)])  9.43 us
  transfers between devices with their start and end apart: 8, of which 6 were waited for; matrix products, arithmetic and copies ran while one was open for 0% of the time, Pallas kernels for 0%

profile of v2, /device:TPU:0, one launch (start us, length us, event | category | flops | bytes accessed | tf_op | source)
XLA Modules:
  0.0 159.4 jit_solution(4222381808754981910)
XLA Ops:
  0.6 97.9 %front.1 = (f32[512,512]{1,0:T(8,128)}, f32[736,512]{1,0:T(8,128)}, f32[512,512]{1,0:T(8,128)}) custom-call(s32[1]{0:T(128)} %bitcast.side, f32[4,512,512]{2,1,0:T(8,128)} %diag.1, f32[4,512,512]{2,1,0:T(8,128)} %lower.1, f32[4,64,512]{2,1,0:T(8,128)} %arrow.1), custom_call_target="tpu_custom_call" | custom-call | tf_op jit(solution)/shard_map/front/pallas_call | solution.py:347
  98.5 0.5 collective-permute-start.1
  99.0 0.1 collective-permute-start
  99.1 4.6 %collective-permute-done.pivot_other = f32[512,512]{1,0:T(8,128)S(1)} collective-permute-done((f32[512,512]{1,0:T(8,128)}, f32[512,512]{1,0:T(8,128)S(1)}, u32[]{:S(2)}, u32[]{:S(2)}) %collective-permute-start) | collective-permute-done | bytes 1048608 | tf_op jit(solution)/shard_map/ppermute | solution.py:316
  103.7 0.0 copy-start.1
  103.7 0.0 collective-permute-done.1.pack_other
  103.7 1.0 copy-done.1
  104.7 0.4 copy-done
  105.1 35.9 %merge.1 = (f32[544,1088]{1,0:T(8,128)}, f32[64,64]{1,0:T(8,128)}) custom-call(s32[1]{0:T(128)} %bitcast.side, f32[512,512]{1,0:T(8,128)} %get-tuple-element.7.pivot_mine, f32[512,512]{1,0:T(8,128)} %copy-done.1, f32[736,512]{1,0:T(8,128)} %get-tuple-element.8.pack_mine, f32[736,512]{1,0:T(8,128)} %copy-done, f32[512,512]{1,0:T(8,128)} %get-tuple-element.9.outer_mine), custom_call_target="tpu_custom_call" | custom-call | tf_op jit(solution)/shard_map/merge/pallas_call | solution.py:369
  141.1 3.8 %collective-permute-start.4 = (f32[64,64]{1,0:T(8,128)}, f32[64,64]{1,0:T(8,128)S(1)}, u32[]{:S(2)}, u32[]{:S(2)}) collective-permute-start(f32[64,64]{1,0:T(8,128)} %get-tuple-element.11), channel_id=1, source_target_pairs={{0,6},{1,7},{2,4},{3,5},{4,2},{5,3},{6,0},{7,1},{8,14},{9,15},{10,... | collective-permute-start | bytes 49160 | tf_op jit(solution)/shard_map/ppermute | solution.py:316
  144.9 0.5 collective-permute-start.3
  145.4 0.1 collective-permute-start.2
  145.5 1.5 collective-permute-done.4
  147.0 2.0 %collective-permute-done.3 = f32[64,64]{1,0:T(8,128)S(1)} collective-permute-done((f32[64,64]{1,0:T(8,128)}, f32[64,64]{1,0:T(8,128)S(1)}, u32[]{:S(2)}, u32[]{:S(2)}) %collective-permute-start.3) | collective-permute-done | bytes 16416 | tf_op jit(solution)/shard_map/ppermute | solution.py:316
  149.0 0.5 collective-permute-done.2
  149.5 0.8 add_add_fusion.1
  150.3 3.7 %collective-permute-start.7 = (f32[64,64]{1,0:T(8,128)S(1)}, f32[64,64]{1,0:T(8,128)S(1)}, u32[]{:S(2)}, u32[]{:S(2)}) collective-permute-start(f32[64,64]{1,0:T(8,128)S(1)} %add_add_fusion.1), channel_id=1, source_target_pairs={{0,24},{1,25},{2,26},{3,27},{4,28},{5,29},{6,30},{7,31},{8,16},{9,... | collective-permute-start | bytes 49160 | tf_op jit(solution)/shard_map/ppermute | solution.py:316
  154.0 0.0 collective-permute-start.6
  154.0 0.8 collective-permute-start.5
  154.8 1.4 collective-permute-done.7
  156.2 2.6 %collective-permute-done.6 = f32[64,64]{1,0:T(8,128)S(1)} collective-permute-done((f32[64,64]{1,0:T(8,128)S(1)}, f32[64,64]{1,0:T(8,128)S(1)}, u32[]{:S(2)}, u32[]{:S(2)}) %collective-permute-start.6) | collective-permute-done | bytes 16416 | tf_op jit(solution)/shard_map/ppermute | solution.py:316
  158.8 0.0 collective-permute-done.5
  158.8 0.0 copy-done.2
  158.8 0.6 add_add_fusion
  (2 shorter events, 0.0 us)
Async XLA Ops:
  98.5 5.2 %collective-permute-start.1 = (f32[736,512]{1,0:T(8,128)}, f32[736,512]{1,0:T(8,128)S(1)}, u32[]{:S(2)}, u32[]{:S(2)}) collective-permute-start(f32[736,512]{1,0:T(8,128)} %get-tuple-element.8.pack_mine), channel_id=1, source_target_pairs={{0,1},{1,0},{2,3},{3,2},{4,5},{5,4},{6,7},{7,6},{8,9},{9,8},{10,11... | collective-permute-start | bytes 4521992 | tf_op jit(solution)/shard_map/ppermute | solution.py:316
  99.0 4.7 %collective-permute-start = (f32[512,512]{1,0:T(8,128)}, f32[512,512]{1,0:T(8,128)S(1)}, u32[]{:S(2)}, u32[]{:S(2)}) collective-permute-start(f32[512,512]{1,0:T(8,128)} %get-tuple-element.7.pivot_mine), channel_id=1, source_target_pairs={{0,1},{1,0},{2,3},{3,2},{4,5},{5,4},{6,7},{7,6},{8,9},{9,8},{10,11... | collective-permute-start | bytes 3145736 | tf_op jit(solution)/shard_map/ppermute | solution.py:316
  103.7 1.0 copy-start.1
  103.7 1.4 copy-start
  105.1 53.6 %copy-start.2 = (f32[64,64]{1,0:T(8,128)S(1)}, f32[64,64]{1,0:T(8,128)}, u32[]{:S(2)}) copy-start(f32[64,64]{1,0:T(8,128)} %param.7) | copy-start | bytes 49156
  141.1 5.9 %collective-permute-start.4 = (f32[64,64]{1,0:T(8,128)}, f32[64,64]{1,0:T(8,128)S(1)}, u32[]{:S(2)}, u32[]{:S(2)}) collective-permute-start(f32[64,64]{1,0:T(8,128)} %get-tuple-element.11), channel_id=1, source_target_pairs={{0,6},{1,7},{2,4},{3,5},{4,2},{5,3},{6,0},{7,1},{8,14},{9,15},{10,... | collective-permute-start | bytes 49160 | tf_op jit(solution)/shard_map/ppermute | solution.py:316
  144.9 4.1 %collective-permute-start.3 = (f32[64,64]{1,0:T(8,128)}, f32[64,64]{1,0:T(8,128)S(1)}, u32[]{:S(2)}, u32[]{:S(2)}) collective-permute-start(f32[64,64]{1,0:T(8,128)} %get-tuple-element.11), channel_id=1, source_target_pairs={{0,4},{1,5},{2,6},{3,7},{4,0},{5,1},{6,2},{7,3},{8,12},{9,13},{10,... | collective-permute-start | bytes 49160 | tf_op jit(solution)/shard_map/ppermute | solution.py:316
  145.4 4.1 %collective-permute-start.2 = (f32[64,64]{1,0:T(8,128)}, f32[64,64]{1,0:T(8,128)S(1)}, u32[]{:S(2)}, u32[]{:S(2)}) collective-permute-start(f32[64,64]{1,0:T(8,128)} %get-tuple-element.11), channel_id=1, source_target_pairs={{0,2},{1,3},{2,0},{3,1},{4,6},{5,7},{6,4},{7,5},{8,10},{9,11},{10,... | collective-permute-start | bytes 49160 | tf_op jit(solution)/shard_map/ppermute | solution.py:316
  150.3 5.9 %collective-permute-start.7 = (f32[64,64]{1,0:T(8,128)S(1)}, f32[64,64]{1,0:T(8,128)S(1)}, u32[]{:S(2)}, u32[]{:S(2)}) collective-permute-start(f32[64,64]{1,0:T(8,128)S(1)} %add_add_fusion.1), channel_id=1, source_target_pairs={{0,24},{1,25},{2,26},{3,27},{4,28},{5,29},{6,30},{7,31},{8,16},{9,... | collective-permute-start | bytes 49160 | tf_op jit(solution)/shard_map/ppermute | solution.py:316
  154.0 4.8 %collective-permute-start.6 = (f32[64,64]{1,0:T(8,128)S(1)}, f32[64,64]{1,0:T(8,128)S(1)}, u32[]{:S(2)}, u32[]{:S(2)}) collective-permute-start(f32[64,64]{1,0:T(8,128)S(1)} %add_add_fusion.1), channel_id=1, source_target_pairs={{0,16},{1,17},{2,18},{3,19},{4,20},{5,21},{6,22},{7,23},{8,24},{9,... | collective-permute-start | bytes 49160 | tf_op jit(solution)/shard_map/ppermute | solution.py:316
  154.0 4.8 %collective-permute-start.5 = (f32[64,64]{1,0:T(8,128)S(1)}, f32[64,64]{1,0:T(8,128)S(1)}, u32[]{:S(2)}, u32[]{:S(2)}) collective-permute-start(f32[64,64]{1,0:T(8,128)S(1)} %add_add_fusion.1), channel_id=1, source_target_pairs={{0,8},{1,9},{2,10},{3,11},{4,12},{5,13},{6,14},{7,15},{8,0},{9,1},... | collective-permute-start | bytes 49160 | tf_op jit(solution)/shard_map/ppermute | solution.py:316

commit v3 on v2

--- a/solution.py
+++ b/solution.py
@@ -47,18 +47,30 @@
     return jnp.where(panel, 0.0, value) - total(terms)
 
 
-def late_update(rows):
-    top = [row_of(rows[15], k) for k in range(SUB)]
-    return rows[:1] + [cleared(value, LANES - SUB, top) for value in rows[1:15]] + rows[15:]
-
-
-def panel_step(state, late):
-    rows, columns = list(state[:16]), list(state[16:])
+def late_update(work, step, top):
+    value = work[...]
+    high, low = split(
+        jnp.concatenate([jnp.where(step % 2 == k, top, jnp.zeros_like(top)) for k in (0, 1)], axis=0)
+    )
+    right = tuple(
+        jnp.concatenate(
+            [jnp.where(step // 2 == k, part, jnp.zeros_like(part)) for k in range(8)], axis=0
+        )
+        for part in (high, low)
+    )
+    lane = lax.broadcasted_iota(jnp.int32, (LANES, LANES), 1)
+    panel = (lane >= SUB * step) & (lane < SUB * (step + 1))
+    work[...] = jnp.where(panel, 0.0, value) - dot3(split(value), right)
+    work[pl.ds(pl.multiple_of(SUB * step, SUB), SUB), :] = top
+
+
+def panel_step(work, step, state, late):
+    row, columns, last = state[0], list(state[1:9]), state[9]
     sub = lax.broadcasted_iota(jnp.int32, (SUB, LANES), 0)
     lane = lax.broadcasted_iota(jnp.int32, (SUB, LANES), 1)
     if late:
-        rows = late_update(rows)
-    top = jnp.where(lane < SUB, jnp.where(lane == sub, 1.0, 0.0).astype(F32), rows[0])
+        late_update(work, step - 1, last)
+    top = jnp.where(lane < SUB, jnp.where(lane == sub, 1.0, 0.0).astype(F32), row)
     for pivot in range(SUB):
         inverse = pltpu.reciprocal(row_of(columns[pivot], pivot))
         here = sub == pivot
@@ -70,26 +82,33 @@
 
         columns[pivot + 1 :] = [eliminated(value) for value in columns[pivot + 1 :]]
         top = eliminated(top)
-    following = cleared(rows[1], 0, [row_of(top, k) for k in range(SUB)])
+    following = work[pl.ds(pl.multiple_of((step + 1) % 16 * SUB, SUB), SUB), :]
+    following = pltpu.roll(following, (LANES - SUB * step) % LANES, 1)
+    following = cleared(following, 0, [row_of(top, k) for k in range(SUB)])
     columns = [column_of(following, SUB + k) for k in range(SUB)]
-    rows = [pltpu.roll(value, LANES - SUB, 1) for value in [following] + rows[2:] + [top]]
-    return tuple(rows + columns)
-
-
-def invert_128(blocks):
+    row = pltpu.roll(following, LANES - SUB, 1)
+    return (row, *columns, pltpu.roll(top, SUB * step, 1))
+
+
+def invert_128(blocks, works):
     states = []
-    for block in blocks:
-        rows = [block[SUB * k : SUB * (k + 1), :] for k in range(16)]
-        columns = [column_of(rows[0], k) for k in range(SUB)]
-        states.append(panel_step(tuple(rows + columns), False))
-    states = lax.fori_loop(
-        1, 16, lambda _, carry: tuple(panel_step(s, True) for s in carry), tuple(states)
-    )
-    return [jnp.concatenate(late_update(list(state[:16])), axis=0) for state in states]
-
-
-def invert_256(blocks):
-    firsts = invert_128([block[0] for block in blocks])
+    for block, work in zip(blocks, works):
+        work[...] = block
+        row = block[:SUB, :]
+        columns = [column_of(row, k) for k in range(SUB)]
+        states.append(panel_step(work, 0, (row, *columns, row), False))
+
+    def step(index, carry):
+        return tuple(panel_step(work, index, state, True) for work, state in zip(works, carry))
+
+    states = lax.fori_loop(1, 16, step, tuple(states))
+    for work, state in zip(works, states):
+        late_update(work, 15, state[9])
+    return [work[...] for work in works]
+
+
+def invert_256(blocks, works):
+    firsts = invert_128([block[0] for block in blocks], works)
     seconds, sides = [], []
     for first, (_, right, below, last) in zip(firsts, blocks):
         first, right, below = split(first), split(right), split(below)
@@ -97,7 +116,7 @@
         seconds.append(last - dot3(low, right))
         sides.append((low, split(dot3(first, right))))
     results = []
-    for first, second, (low, high) in zip(firsts, invert_128(seconds), sides):
+    for first, second, (low, high) in zip(firsts, invert_128(seconds, works), sides):
         corner = split(second)
         below = dot3(corner, low)
         top = jnp.concatenate([first + dot3(high, split(below)), -dot3(high, corner)], axis=1)
@@ -136,9 +155,10 @@
     return jnp.concatenate(scales, axis=1)
 
 
-def eliminate(systems):
+def eliminate(systems, works):
     scales = [equilibrate(system[0]) for system in systems]
-    upper = [split(x) for x in invert_256([quarters(s[0][:HALF, :HALF]) for s in systems])]
+    upper = [quarters(system[0][:HALF, :HALF]) for system in systems]
+    upper = [split(value) for value in invert_256(upper, works)]
     lower = []
     for (pivot, g, gh, gl, zh, zl), inverse, scale in zip(systems, upper, scales):
         right = split(pivot[:HALF, HALF:])
@@ -152,7 +172,7 @@
             zh[rows, :HALF], zl[rows, :HALF] = solved
             part = split(g[rows, HALF:] * scale[:, HALF:] - dot3(solved, right))
             gh[rows, HALF:], gl[rows, HALF:] = part
-    lower = [split(x) for x in invert_256([quarters(value) for value in lower])]
+    lower = [split(x) for x in invert_256([quarters(value) for value in lower], works)]
     for (pivot, g, gh, gl, zh, zl), inverse in zip(systems, lower):
         for start, size in chunks(g.shape[0]):
             rows = pl.ds(start, size)
@@ -177,7 +197,7 @@
 
 def front_kernel(
     side, diag, lower, arrow, pivot_out, pack_out, outer_out,
-    dv, lv, av, ga, gah, gal, zah, zal, gb, gbh, gbl, zbh, zbl, pivot, sems,
+    dv, lv, av, ga, gah, gal, zah, zal, gb, gbh, gbl, zbh, zbl, pivot, work, sems,
 ):
     width, tip = diag.shape[1], arrow.shape[1]
     two = 2 * width
@@ -204,7 +224,7 @@
     first = (dv.at[1], ga, gah, gal, zah, zal)
     third = (dv.at[3], gb, gbh, gbl, zbh, zbl)
     outer_out[...] = dv[3]
-    eliminate([first, third])
+    eliminate([first, third], [work.at[0], work.at[1]])
 
     def pick(left, right):
         return jnp.where(is_left, left, right)
@@ -238,7 +258,7 @@
     tip_tip = -update(first, *tt) - drop(update(third, *tt))
 
     second = (pivot, ga, gah, gal, zah, zal)
-    eliminate([second])
+    eliminate([second], [work.at[0]])
     for start, size in chunks(width):
         rows = pl.ds(start, size)
         pivot_out[rows, :] = pivot_out[rows, :] - update(second, width + start, size, width, width)
@@ -255,7 +275,7 @@
 
 def merge_kernel(
     side, pivot_mine, pivot_other, pack_mine, pack_other, outer_mine, merged, tip_out,
-    g, gh, gl, zh, zl, pivot,
+    g, gh, gl, zh, zl, pivot, work,
 ):
     width = pivot.shape[0]
     tip = tip_out.shape[0]
@@ -273,7 +293,7 @@
     at = pl.ds(width, tip)
     g[two:, :] = pack_mine[at, :] + pack_other[at, :]
     system = (pivot, g, gh, gl, zh, zl)
-    eliminate([system])
+    eliminate([system], [work])
     at = pl.ds(base, tip)
     tip_tip = pack_mine[at, :tip] + pack_other[at, :tip] - update(system, two, tip, two, tip)
     tip_out[...] = tip_tip
@@ -360,7 +380,8 @@
         ]
         + system
         + system
-        + [pltpu.VMEM((width, width), F32), pltpu.SemaphoreType.DMA((3 * count,))],
+        + [pltpu.VMEM((width, width), F32), pltpu.VMEM((2, LANES, LANES), F32)]
+        + [pltpu.SemaphoreType.DMA((3 * count,))],
         compiler_params=params,
         name="front",
     )(side, diag_blocks, lower_blocks, arrow_blocks)
@@ -374,7 +395,7 @@
         ],
         in_specs=[smem] + [pl.BlockSpec(memory_space=pltpu.VMEM)] * 5,
         out_specs=[pl.BlockSpec(memory_space=pltpu.VMEM)] * 2,
-        scratch_shapes=system + [pltpu.VMEM((width, width), F32)],
+        scratch_shapes=system + [pltpu.VMEM((width, width), F32), pltpu.VMEM((LANES, LANES), F32)],
         compiler_params=params,
         name="merge",
     )(side, pivot, pivot_other, pack, pack_other, outer)

time: 160 us -> 154 us (0.963)
  Pallas kernels: 134 us -> 128 us
    pallas_call x1, Pallas kernels: 97.9 us -> 90.2 us  [local(): pl.pallas_call(front_kernel, out_shape=[jax.ShapeDtypeStruct((width, widt...]
    pallas_call x1, Pallas kernels: 35.9 us -> 38 us  [local(): pl.pallas_call(merge_kernel, out_shape=[jax.ShapeDtypeStruct((half, front...]
where the time goes in v3:
time: 154 us
  Pallas kernels  128 us (83%)
  waiting for transfers between devices  12.7 us (8%)
  starting transfers between devices  9.44 us (6%)
    pallas_call x1, Pallas kernels, local(): pl.pallas_call(front_kernel, out_shape=[jax.ShapeDtypeStruct((width, widt...  90.2 us
    pallas_call x1, Pallas kernels, local(): pl.pallas_call(merge_kernel, out_shape=[jax.ShapeDtypeStruct((half, front...  38 us
    ppermute x8, waiting for transfers between devices, swapped(): return lax.ppermute(value, axis, [(k, k ^ mask) for k in range(count)])  12.7 us
    ppermute x8, starting transfers between devices, swapped(): return lax.ppermute(value, axis, [(k, k ^ mask) for k in range(count)])  9.44 us
  transfers between devices with their start and end apart: 8, of which 6 were waited for; matrix products, arithmetic and copies ran while one was open for 0% of the time, Pallas kernels for 0%

profile of v3, /device:TPU:0, one launch (start us, length us, event | category | flops | bytes accessed | tf_op | source)
XLA Modules:
  0.0 153.8 jit_solution(12143256570817870980)
XLA Ops:
  0.6 90.2 %front.1 = (f32[512,512]{1,0:T(8,128)}, f32[736,512]{1,0:T(8,128)}, f32[512,512]{1,0:T(8,128)}) custom-call(s32[1]{0:T(128)} %bitcast.side, f32[4,512,512]{2,1,0:T(8,128)} %diag.1, f32[4,512,512]{2,1,0:T(8,128)} %lower.1, f32[4,64,512]{2,1,0:T(8,128)} %arrow.1), custom_call_target="tpu_custom_call" | custom-call | tf_op jit(solution)/shard_map/front/pallas_call | solution.py:367
  90.9 0.5 collective-permute-start.1
  91.4 0.1 collective-permute-start
  91.5 4.6 %collective-permute-done.pivot_other = f32[512,512]{1,0:T(8,128)S(1)} collective-permute-done((f32[512,512]{1,0:T(8,128)}, f32[512,512]{1,0:T(8,128)S(1)}, u32[]{:S(2)}, u32[]{:S(2)}) %collective-permute-start) | collective-permute-done | bytes 1048608 | tf_op jit(solution)/shard_map/ppermute | solution.py:336
  96.0 0.0 copy-start.1
  96.1 0.0 collective-permute-done.1.pack_other
  96.1 1.0 copy-done.1
  97.1 0.4 copy-done
  97.5 38.0 %merge.1 = (f32[544,1088]{1,0:T(8,128)}, f32[64,64]{1,0:T(8,128)}) custom-call(s32[1]{0:T(128)} %bitcast.side, f32[512,512]{1,0:T(8,128)} %get-tuple-element.7.pivot_mine, f32[512,512]{1,0:T(8,128)} %copy-done.1, f32[736,512]{1,0:T(8,128)} %get-tuple-element.8.pack_mine, f32[736,512]{1,0:T(8,128)} %copy-done, f32[512,512]{1,0:T(8,128)} %get-tuple-element.9.outer_mine), custom_call_target="tpu_custom_call" | custom-call | tf_op jit(solution)/shard_map/merge/pallas_call | solution.py:390
  135.5 3.8 %collective-permute-start.4 = (f32[64,64]{1,0:T(8,128)}, f32[64,64]{1,0:T(8,128)S(1)}, u32[]{:S(2)}, u32[]{:S(2)}) collective-permute-start(f32[64,64]{1,0:T(8,128)} %get-tuple-element.11), channel_id=1, source_target_pairs={{0,6},{1,7},{2,4},{3,5},{4,2},{5,3},{6,0},{7,1},{8,14},{9,15},{10,... | collective-permute-start | bytes 49160 | tf_op jit(solution)/shard_map/ppermute | solution.py:336
  139.3 0.5 collective-permute-start.3
  139.8 0.1 collective-permute-start.2
  139.9 1.5 collective-permute-done.4
  141.4 2.0 %collective-permute-done.3 = f32[64,64]{1,0:T(8,128)S(1)} collective-permute-done((f32[64,64]{1,0:T(8,128)}, f32[64,64]{1,0:T(8,128)S(1)}, u32[]{:S(2)}, u32[]{:S(2)}) %collective-permute-start.3) | collective-permute-done | bytes 16416 | tf_op jit(solution)/shard_map/ppermute | solution.py:336
  143.4 0.5 collective-permute-done.2
  143.9 0.8 add_add_fusion.1
  144.7 3.7 %collective-permute-start.7 = (f32[64,64]{1,0:T(8,128)S(1)}, f32[64,64]{1,0:T(8,128)S(1)}, u32[]{:S(2)}, u32[]{:S(2)}) collective-permute-start(f32[64,64]{1,0:T(8,128)S(1)} %add_add_fusion.1), channel_id=1, source_target_pairs={{0,24},{1,25},{2,26},{3,27},{4,28},{5,29},{6,30},{7,31},{8,16},{9,... | collective-permute-start | bytes 49160 | tf_op jit(solution)/shard_map/ppermute | solution.py:336
  148.4 0.0 collective-permute-start.6
  148.4 0.8 collective-permute-start.5
  149.2 1.4 collective-permute-done.7
  150.6 2.6 %collective-permute-done.6 = f32[64,64]{1,0:T(8,128)S(1)} collective-permute-done((f32[64,64]{1,0:T(8,128)S(1)}, f32[64,64]{1,0:T(8,128)S(1)}, u32[]{:S(2)}, u32[]{:S(2)}) %collective-permute-start.6) | collective-permute-done | bytes 16416 | tf_op jit(solution)/shard_map/ppermute | solution.py:336
  153.2 0.0 collective-permute-done.5
  153.2 0.0 copy-done.2
  153.2 0.6 add_add_fusion
  (2 shorter events, 0.0 us)
Async XLA Ops:
  90.9 5.2 %collective-permute-start.1 = (f32[736,512]{1,0:T(8,128)}, f32[736,512]{1,0:T(8,128)S(1)}, u32[]{:S(2)}, u32[]{:S(2)}) collective-permute-start(f32[736,512]{1,0:T(8,128)} %get-tuple-element.8.pack_mine), channel_id=1, source_target_pairs={{0,1},{1,0},{2,3},{3,2},{4,5},{5,4},{6,7},{7,6},{8,9},{9,8},{10,11... | collective-permute-start | bytes 4521992 | tf_op jit(solution)/shard_map/ppermute | solution.py:336
  91.4 4.7 %collective-permute-start = (f32[512,512]{1,0:T(8,128)}, f32[512,512]{1,0:T(8,128)S(1)}, u32[]{:S(2)}, u32[]{:S(2)}) collective-permute-start(f32[512,512]{1,0:T(8,128)} %get-tuple-element.7.pivot_mine), channel_id=1, source_target_pairs={{0,1},{1,0},{2,3},{3,2},{4,5},{5,4},{6,7},{7,6},{8,9},{9,8},{10,11... | collective-permute-start | bytes 3145736 | tf_op jit(solution)/shard_map/ppermute | solution.py:336
  96.0 1.0 copy-start.1
  96.1 1.4 copy-start
  97.5 55.7 %copy-start.2 = (f32[64,64]{1,0:T(8,128)S(1)}, f32[64,64]{1,0:T(8,128)}, u32[]{:S(2)}) copy-start(f32[64,64]{1,0:T(8,128)} %param.7) | copy-start | bytes 49156
  135.5 5.9 %collective-permute-start.4 = (f32[64,64]{1,0:T(8,128)}, f32[64,64]{1,0:T(8,128)S(1)}, u32[]{:S(2)}, u32[]{:S(2)}) collective-permute-start(f32[64,64]{1,0:T(8,128)} %get-tuple-element.11), channel_id=1, source_target_pairs={{0,6},{1,7},{2,4},{3,5},{4,2},{5,3},{6,0},{7,1},{8,14},{9,15},{10,... | collective-permute-start | bytes 49160 | tf_op jit(solution)/shard_map/ppermute | solution.py:336
  139.3 4.1 %collective-permute-start.3 = (f32[64,64]{1,0:T(8,128)}, f32[64,64]{1,0:T(8,128)S(1)}, u32[]{:S(2)}, u32[]{:S(2)}) collective-permute-start(f32[64,64]{1,0:T(8,128)} %get-tuple-element.11), channel_id=1, source_target_pairs={{0,4},{1,5},{2,6},{3,7},{4,0},{5,1},{6,2},{7,3},{8,12},{9,13},{10,... | collective-permute-start | bytes 49160 | tf_op jit(solution)/shard_map/ppermute | solution.py:336
  139.8 4.1 %collective-permute-start.2 = (f32[64,64]{1,0:T(8,128)}, f32[64,64]{1,0:T(8,128)S(1)}, u32[]{:S(2)}, u32[]{:S(2)}) collective-permute-start(f32[64,64]{1,0:T(8,128)} %get-tuple-element.11), channel_id=1, source_target_pairs={{0,2},{1,3},{2,0},{3,1},{4,6},{5,7},{6,4},{7,5},{8,10},{9,11},{10,... | collective-permute-start | bytes 49160 | tf_op jit(solution)/shard_map/ppermute | solution.py:336
  144.7 5.9 %collective-permute-start.7 = (f32[64,64]{1,0:T(8,128)S(1)}, f32[64,64]{1,0:T(8,128)S(1)}, u32[]{:S(2)}, u32[]{:S(2)}) collective-permute-start(f32[64,64]{1,0:T(8,128)S(1)} %add_add_fusion.1), channel_id=1, source_target_pairs={{0,24},{1,25},{2,26},{3,27},{4,28},{5,29},{6,30},{7,31},{8,16},{9,... | collective-permute-start | bytes 49160 | tf_op jit(solution)/shard_map/ppermute | solution.py:336
  148.4 4.8 %collective-permute-start.6 = (f32[64,64]{1,0:T(8,128)S(1)}, f32[64,64]{1,0:T(8,128)S(1)}, u32[]{:S(2)}, u32[]{:S(2)}) collective-permute-start(f32[64,64]{1,0:T(8,128)S(1)} %add_add_fusion.1), channel_id=1, source_target_pairs={{0,16},{1,17},{2,18},{3,19},{4,20},{5,21},{6,22},{7,23},{8,24},{9,... | collective-permute-start | bytes 49160 | tf_op jit(solution)/shard_map/ppermute | solution.py:336
  148.4 4.8 %collective-permute-start.5 = (f32[64,64]{1,0:T(8,128)S(1)}, f32[64,64]{1,0:T(8,128)S(1)}, u32[]{:S(2)}, u32[]{:S(2)}) collective-permute-start(f32[64,64]{1,0:T(8,128)S(1)} %add_add_fusion.1), channel_id=1, source_target_pairs={{0,8},{1,9},{2,10},{3,11},{4,12},{5,13},{6,14},{7,15},{8,0},{9,1},... | collective-permute-start | bytes 49160 | tf_op jit(solution)/shard_map/ppermute | solution.py:336

commit v4 on v3

--- a/solution.py
+++ b/solution.py
@@ -64,26 +64,38 @@
     work[pl.ds(pl.multiple_of(SUB * step, SUB), SUB), :] = top
 
 
+def eliminated(value, pivot, first, second, corner, inverse):
+    sub = lax.broadcasted_iota(jnp.int32, (SUB, LANES), 0)
+    a, b, d = corner
+    upper, lower = row_of(value, pivot), row_of(value, pivot + 1)
+    upper, lower = d * upper - b * lower, a * lower - b * upper
+    product = first * upper + second * lower
+    rest = value - product * inverse
+    return jnp.where(
+        sub == pivot, upper * inverse, jnp.where(sub == pivot + 1, lower * inverse, rest)
+    )
+
+
 def panel_step(work, step, state, late):
     row, columns, last = state[0], list(state[1:9]), state[9]
     sub = lax.broadcasted_iota(jnp.int32, (SUB, LANES), 0)
     lane = lax.broadcasted_iota(jnp.int32, (SUB, LANES), 1)
+    following = work[pl.ds(pl.multiple_of((step + 1) % 16 * SUB, SUB), SUB), :]
     if late:
         late_update(work, step - 1, last)
+        before = pltpu.roll(last, (LANES + SUB - SUB * step) % LANES, 1)
+        following = pltpu.roll(following, (LANES + SUB - SUB * step) % LANES, 1)
+        following = cleared(following, 0, [row_of(before, k) for k in range(SUB)])
+        following = pltpu.roll(following, LANES - SUB, 1)
     top = jnp.where(lane < SUB, jnp.where(lane == sub, 1.0, 0.0).astype(F32), row)
-    for pivot in range(SUB):
-        inverse = pltpu.reciprocal(row_of(columns[pivot], pivot))
-        here = sub == pivot
-
-        def eliminated(value):
-            row = row_of(value, pivot)
-            product = columns[pivot] * row
-            return jnp.where(here, row * inverse, value - product * inverse)
-
-        columns[pivot + 1 :] = [eliminated(value) for value in columns[pivot + 1 :]]
-        top = eliminated(top)
-    following = work[pl.ds(pl.multiple_of((step + 1) % 16 * SUB, SUB), SUB), :]
-    following = pltpu.roll(following, (LANES - SUB * step) % LANES, 1)
+    for pivot in range(0, SUB, 2):
+        a = row_of(columns[pivot], pivot)
+        b = row_of(columns[pivot + 1], pivot)
+        d = row_of(columns[pivot + 1], pivot + 1)
+        inverse = pltpu.reciprocal(a * d - b * b)
+        pair = (columns[pivot], columns[pivot + 1], (a, b, d), inverse)
+        columns[pivot + 2 :] = [eliminated(value, pivot, *pair) for value in columns[pivot + 2 :]]
+        top = eliminated(top, pivot, *pair)
     following = cleared(following, 0, [row_of(top, k) for k in range(SUB)])
     columns = [column_of(following, SUB + k) for k in range(SUB)]
     row = pltpu.roll(following, LANES - SUB, 1)
@@ -101,7 +113,7 @@
     def step(index, carry):
         return tuple(panel_step(work, index, state, True) for work, state in zip(works, carry))
 
-    states = lax.fori_loop(1, 16, step, tuple(states))
+    states = lax.fori_loop(1, 16, step, tuple(states), unroll=3)
     for work, state in zip(works, states):
         late_update(work, 15, state[9])
     return [work[...] for work in works]
@@ -264,43 +276,80 @@
         pivot_out[rows, :] = pivot_out[rows, :] - update(second, width + start, size, width, width)
         pack_out[rows, :] = -update(second, start, size, width, width)
         outer_out[rows, :] = outer_out[rows, :] - update(second, start, size, 0, width)
-    pack_out[width : width + tip, :] = tip_pivot - update(second, two, tip, width, width)
-    pack_out[width + tip : width + 2 * tip, :] = tip_outer - update(second, two, tip, 0, width)
-    base = width + 2 * tip
-    pack_out[base : base + tip, :] = jnp.zeros((tip, width), F32)
-    pack_out[base : base + tip, :tip] = tip_tip - update(second, *tt)
-    spill = pack_out.shape[0] - base - tip
-    pack_out[base + tip :, :] = outer_out[:spill, :]
+    pivot_out[width : width + tip, :] = tip_pivot - update(second, two, tip, width, width)
+    pivot_out[width + tip :, :] = jnp.zeros((tip, width), F32)
+    pivot_out[width + tip :, :tip] = tip_tip - update(second, *tt)
+    pack_out[width : width + tip, :] = tip_outer - update(second, two, tip, 0, width)
+    spill = pack_out.shape[0] - width - tip
+    pack_out[width + tip :, :] = outer_out[:spill, :]
+
+
+def invert_512(pivot, work):
+    scale = equilibrate(pivot)
+    (first,) = invert_256([quarters(pivot[:HALF, :HALF])], [work])
+    right = split(pivot[:HALF, HALF:])
+    below = split(pivot[HALF:, :HALF])
+    upper = split(first)
+    low = split(dot3(below, upper))
+    high = split(dot3(upper, right))
+    (second,) = invert_256([quarters(pivot[HALF:, HALF:] - dot3(low, right))], [work])
+    corner = split(second)
+    below = dot3(corner, low)
+    pivot[:HALF, :HALF] = first + dot3(high, split(below))
+    pivot[:HALF, HALF:] = -dot3(high, corner)
+    pivot[HALF:, :HALF] = -below
+    pivot[HALF:, HALF:] = second
+    for start in range(0, pivot.shape[0], LANES):
+        rows = pl.ds(start, LANES)
+        down = jnp.broadcast_to(scale[:, start : start + LANES], (LANES, LANES)).T
+        for lanes in range(0, pivot.shape[0], LANES):
+            across = scale[:, lanes : lanes + LANES]
+            lanes = pl.ds(lanes, LANES)
+            pivot[rows, lanes] = pivot[rows, lanes] * down * across
+
+
+def factor_kernel(mine, other, inverse, tip_out, work):
+    width, tip = inverse.shape[0], tip_out.shape[0]
+    inverse[...] = mine[:width, :] + other[:width, :]
+    invert_512(inverse, work)
+    at = pl.ds(width, tip)
+    coupling = split(mine[at, :] + other[at, :])
+    solved = split(dot3(coupling, split(inverse[...])))
+    at = pl.ds(width + tip, tip)
+    tip_out[...] = mine[at, :tip] + other[at, :tip] - dot3(solved, coupling, NT)
 
 
 def merge_kernel(
-    side, pivot_mine, pivot_other, pack_mine, pack_other, outer_mine, merged, tip_out,
-    g, gh, gl, zh, zl, pivot, work,
+    side, inverse, tip_tip, pivot_mine, pivot_other, pack_mine, pack_other, outer_mine, merged,
+    gh, gl, zh, zl,
 ):
-    width = pivot.shape[0]
-    tip = tip_out.shape[0]
+    width, tip = inverse.shape[0], tip_tip.shape[0]
     two = 2 * width
-    base = width + 2 * tip
     half = merged.shape[0]
     spill = half - width
     is_left = side[0] == 0
-    pivot[...] = pivot_mine[...] + pivot_other[...]
     for start, size in chunks(width):
         rows = pl.ds(start, size)
-        mine, other = pack_mine[rows, :], pack_other[rows, :]
-        g[rows, :] = jnp.where(is_left, mine, other)
-        g[pl.ds(width + start, size), :] = jnp.where(is_left, other, mine)
+        mine, other = split(pack_mine[rows, :]), split(pack_other[rows, :])
+        gh[rows, :] = jnp.where(is_left, mine[0], other[0])
+        gl[rows, :] = jnp.where(is_left, mine[1], other[1])
+        rows = pl.ds(width + start, size)
+        gh[rows, :] = jnp.where(is_left, other[0], mine[0])
+        gl[rows, :] = jnp.where(is_left, other[1], mine[1])
     at = pl.ds(width, tip)
-    g[two:, :] = pack_mine[at, :] + pack_other[at, :]
-    system = (pivot, g, gh, gl, zh, zl)
-    eliminate([system], [work])
-    at = pl.ds(base, tip)
-    tip_tip = pack_mine[at, :tip] + pack_other[at, :tip] - update(system, two, tip, two, tip)
-    tip_out[...] = tip_tip
-    outer_tip = pl.ds(width + tip, tip)
+    gh[two:, :], gl[two:, :] = split(pivot_mine[at, :] + pivot_other[at, :])
+    solver = split(inverse[...])
+    system = (None, None, gh, gl, zh, zl)
+    outer_tip = pl.ds(width, tip)
+
+    def solve(start, size):
+        rows = pl.ds(start, size)
+        zh[rows, :], zl[rows, :] = split(dot3((gh[rows, :], gl[rows, :]), solver))
 
     @pl.when(is_left)
     def _():
+        for start, size in chunks(half):
+            solve(start, size)
         for start, size in chunks(width):
             rows = pl.ds(start, size)
             merged[rows, :width] = outer_mine[rows, :] - update(system, start, size, 0, width)
@@ -308,13 +357,15 @@
             mine = pack_mine[outer_tip, start : start + size].T
             merged[rows, two:] = mine - update(system, start, size, two, tip)
         merged[width:, :width] = -update(system, width, spill, 0, width)
-        other = pack_other[base + tip :, :]
+        other = pack_other[width + tip :, :]
         merged[width:, width:two] = other - update(system, width, spill, width, width)
         other = pack_other[outer_tip, :LANES].T[:spill, :]
         merged[width:, two:] = other - update(system, width, spill, two, tip)
 
     @pl.when(jnp.logical_not(is_left))
     def _():
+        for start, size in chunks(width + tip):
+            solve(width + start, size)
         for start, size in chunks(width):
             skip = spill if start == 0 else 0
             rows = pl.ds(start + skip - spill, size - skip)
@@ -328,7 +379,7 @@
         rows = pl.ds(half - tip, tip)
         merged[rows, :width] = pack_other[outer_tip, :] - update(system, two, tip, 0, width)
         merged[rows, width:two] = pack_mine[outer_tip, :] - update(system, two, tip, width, width)
-        merged[rows, two:] = tip_tip
+        merged[rows, two:] = tip_tip[...]
 
 
 def swapped(value, axis, mask):
@@ -349,30 +400,27 @@
     return value
 
 
-def whole(*shape):
-    return pl.BlockSpec(shape, lambda: (0,) * len(shape), memory_space=pltpu.VMEM)
-
-
 def local(diag_blocks, lower_blocks, arrow_blocks, tip_block):
     count, width = diag_blocks.shape[:2]
     tip = arrow_blocks.shape[1]
     front = 2 * width + tip
     half = front // 2
     spill = half - width
-    packed = width + 3 * tip + spill
     side = (lax.axis_index("tm") % 2).astype(jnp.int32).reshape(1)
     smem = pl.BlockSpec(memory_space=pltpu.SMEM)
-    system = [pltpu.VMEM((front, width), F32)] + [pltpu.VMEM((front, width), BF16)] * 4
+    vmem = pl.BlockSpec(memory_space=pltpu.VMEM)
+    parts = [pltpu.VMEM((front, width), BF16)] * 4
+    system = [pltpu.VMEM((front, width), F32)] + parts
     params = pltpu.CompilerParams(vmem_limit_bytes=56 * 2**20)
     pivot, pack, outer = pl.pallas_call(
         front_kernel,
         out_shape=[
-            jax.ShapeDtypeStruct((width, width), F32),
-            jax.ShapeDtypeStruct((packed, width), F32),
+            jax.ShapeDtypeStruct((width + 2 * tip, width), F32),
+            jax.ShapeDtypeStruct((width + tip + spill, width), F32),
             jax.ShapeDtypeStruct((width, width), F32),
         ],
         in_specs=[smem] + [pl.BlockSpec(memory_space=pl.ANY)] * 3,
-        out_specs=[pl.BlockSpec(memory_space=pltpu.VMEM)] * 3,
+        out_specs=[vmem] * 3,
         scratch_shapes=[
             pltpu.VMEM((count, width, width), F32),
             pltpu.VMEM((count, width, width), F32),
@@ -387,18 +435,29 @@
     )(side, diag_blocks, lower_blocks, arrow_blocks)
     pivot_other = swapped(pivot, "tm", 1)
     pack_other = swapped(pack, "tm", 1)
-    merged, tip_tip = pl.pallas_call(
-        merge_kernel,
+    inverse, tip_tip = pl.pallas_call(
+        factor_kernel,
         out_shape=[
-            jax.ShapeDtypeStruct((half, front), F32),
+            jax.ShapeDtypeStruct((width, width), F32),
             jax.ShapeDtypeStruct((tip, tip), F32),
         ],
-        in_specs=[smem] + [pl.BlockSpec(memory_space=pltpu.VMEM)] * 5,
-        out_specs=[pl.BlockSpec(memory_space=pltpu.VMEM)] * 2,
-        scratch_shapes=system + [pltpu.VMEM((width, width), F32), pltpu.VMEM((LANES, LANES), F32)],
-        compiler_params=params,
+        in_specs=[vmem] * 2,
+        out_specs=[vmem] * 2,
+        scratch_shapes=[pltpu.VMEM((LANES, LANES), F32)],
+        compiler_params=pltpu.CompilerParams(vmem_limit_bytes=24 * 2**20),
+        cost_estimate=pl.CostEstimate(flops=10**10, bytes_accessed=10**7, transcendentals=0),
+        name="factor",
+    )(pivot, pivot_other)
+    merged = pl.pallas_call(
+        merge_kernel,
+        out_shape=jax.ShapeDtypeStruct((half, front), F32),
+        in_specs=[smem] + [vmem] * 7,
+        out_specs=vmem,
+        scratch_shapes=parts,
+        compiler_params=pltpu.CompilerParams(vmem_limit_bytes=40 * 2**20),
+        cost_estimate=pl.CostEstimate(flops=5 * 10**9, bytes_accessed=10**7, transcendentals=0),
         name="merge",
-    )(side, pivot, pivot_other, pack, pack_other, outer)
+    )(side, inverse, tip_tip, pivot, pivot_other, pack, pack_other, outer)
     return merged, tip_block + sum_over_pairs(tip_tip, "tm")
 
 

time: 154 us -> 123 us (0.80)
  Pallas kernels: 128 us -> 104 us
  waiting for transfers between devices: 12.7 us -> 6.57 us
    pallas_call x2 -> x3, Pallas kernels: 128 us -> 104 us  [the longest x1 74.3 us: local(): pl.pallas_call(front_kernel, out_shape=[jax.ShapeDtypeStruct((width + 2 *...]
    ppermute x8, waiting for transfers between devices: 12.7 us -> 6.57 us  [swapped(): return lax.ppermute(value, axis, [(k, k ^ mask) for k in range(count)])]
  transfers between devices with their start and end apart: 8 -> 8, of which waited for: 6 -> 4; matrix products, arithmetic and copies ran while one was open for 0% -> 0% of each run, Pallas kernels for 0% -> 24%
where the time goes in v4:
time: 123 us
  Pallas kernels  104 us (85%)
  starting transfers between devices  9.58 us (8%)
  waiting for transfers between devices  6.57 us (5%)
  local copies, waits for them, and re-layouts  1.33 us (1%)
    pallas_call x1, Pallas kernels, local(): pl.pallas_call(front_kernel, out_shape=[jax.ShapeDtypeStruct((width + 2 *...  74.3 us
    pallas_call x1, Pallas kernels, local(): pl.pallas_call(factor_kernel, out_shape=[jax.ShapeDtypeStruct((width, wid...  23.3 us
    ppermute x8, starting transfers between devices, swapped(): return lax.ppermute(value, axis, [(k, k ^ mask) for k in range(count)])  9.58 us
    ppermute x8, waiting for transfers between devices, swapped(): return lax.ppermute(value, axis, [(k, k ^ mask) for k in range(count)])  6.57 us
    pallas_call x1, Pallas kernels, local(): pl.pallas_call(merge_kernel, out_shape=jax.ShapeDtypeStruct((half, front)...  6.33 us
  transfers between devices with their start and end apart: 8, of which 4 were waited for; matrix products, arithmetic and copies ran while one was open for 0% of the time, Pallas kernels for 24%

profile of v4, /device:TPU:0, one launch (start us, length us, event | category | flops | bytes accessed | tf_op | source)
XLA Modules:
  0.0 122.8 jit_solution(5948763654612290255)
XLA Ops:
  0.6 74.3 %front.1 = (f32[640,512]{1,0:T(8,128)}, f32[608,512]{1,0:T(8,128)}, f32[512,512]{1,0:T(8,128)}) custom-call(s32[1]{0:T(128)} %bitcast.side, f32[4,512,512]{2,1,0:T(8,128)} %diag.1, f32[4,512,512]{2,1,0:T(8,128)} %lower.1, f32[4,64,512]{2,1,0:T(8,128)} %arrow.1), custom_call_target="tpu_custom_call" | custom-call | tf_op jit(solution)/shard_map/front/pallas_call | solution.py:415
  74.9 0.5 collective-permute-start
  75.5 0.1 collective-permute-start.1
  75.6 2.8 %collective-permute-done.other.pivot_other = f32[640,512]{1,0:T(8,128)S(1)} collective-permute-done((f32[640,512]{1,0:T(8,128)}, f32[640,512]{1,0:T(8,128)S(1)}, u32[]{:S(2)}, u32[]{:S(2)}) %collective-permute-start) | collective-permute-done | bytes 1310752 | tf_op jit(solution)/shard_map/ppermute | solution.py:387
  78.3 1.3 %copy-done = f32[640,512]{1,0:T(8,128)S(1)} copy-done((f32[640,512]{1,0:T(8,128)S(1)}, f32[640,512]{1,0:T(8,128)}, u32[]{:S(2)}) %copy-start) | copy-done | bytes 1310744
  79.7 23.3 %factor.1 = (f32[512,512]{1,0:T(8,128)S(1)}, f32[64,64]{1,0:T(8,128)S(1)}) custom-call(f32[640,512]{1,0:T(8,128)S(1)} %copy-done, f32[640,512]{1,0:T(8,128)S(1)} %collective-permute-done.other.pivot_other), custom_call_target="tpu_custom_call" | custom-call | flops 10000000000 | bytes 10000000 | tf_op jit(solution)/shard_map/factor/pallas_call | solution.py:438
  103.0 3.9 %collective-permute-start.4 = (f32[64,64]{1,0:T(8,128)S(1)}, f32[64,64]{1,0:T(8,128)S(1)}, u32[]{:S(2)}, u32[]{:S(2)}) collective-permute-start(f32[64,64]{1,0:T(8,128)S(1)} %get-tuple-element.9.tip_tip), channel_id=1, source_target_pairs={{0,6},{1,7},{2,4},{3,5},{4,2},{5,3},{6,0},{7,1},{8,14},{9,15},{10,... | collective-permute-start | bytes 49160 | tf_op jit(solution)/shard_map/ppermute | solution.py:387
  106.9 0.5 collective-permute-start.3
  107.4 0.2 collective-permute-start.2
  107.5 1.3 %collective-permute-done.4 = f32[64,64]{1,0:T(8,128)S(1)} collective-permute-done((f32[64,64]{1,0:T(8,128)S(1)}, f32[64,64]{1,0:T(8,128)S(1)}, u32[]{:S(2)}, u32[]{:S(2)}) %collective-permute-start.4) | collective-permute-done | bytes 16416 | tf_op jit(solution)/shard_map/ppermute | solution.py:387
  108.8 2.0 %collective-permute-done.3 = f32[64,64]{1,0:T(8,128)S(1)} collective-permute-done((f32[64,64]{1,0:T(8,128)S(1)}, f32[64,64]{1,0:T(8,128)S(1)}, u32[]{:S(2)}, u32[]{:S(2)}) %collective-permute-start.3) | collective-permute-done | bytes 16416 | tf_op jit(solution)/shard_map/ppermute | solution.py:387
  110.8 0.5 collective-permute-done.2
  111.3 3.7 %collective-permute-start.7 = (f32[64,64]{1,0:T(8,128)S(1)}, f32[64,64]{1,0:T(8,128)S(1)}, u32[]{:S(2)}, u32[]{:S(2)}) collective-permute-start(f32[64,64]{1,0:T(8,128)S(1)} %add_add_fusion.1), channel_id=1, source_target_pairs={{0,24},{1,25},{2,26},{3,27},{4,28},{5,29},{6,30},{7,31},{8,16},{9,... | collective-permute-start | bytes 49160 | tf_op jit(solution)/shard_map/ppermute | solution.py:387
  115.0 0.0 collective-permute-start.6
  115.0 0.8 collective-permute-start.5
  115.8 0.0 collective-permute-done.1.pack_other
  115.8 0.0 copy-done.1
  115.8 0.0 copy-done.2
  115.8 0.0 copy-start.4
  115.8 6.3 %merge.1 = f32[544,1088]{1,0:T(8,128)} custom-call(s32[1]{0:T(128)} %bitcast.side, f32[512,512]{1,0:T(8,128)S(1)} %get-tuple-element.8.inverse, f32[64,64]{1,0:T(8,128)S(1)} %get-tuple-element.9.tip_tip, f32[640,512]{1,0:T(8,128)S(1)} %copy-done.1, f32[640,512]{1,0:T(8,128)S(1)} %collective-permute-done.other.pivot_other, f32[608,512]{1,0:T(8,128)S(1)} %copy-done.2, ...), custom_call_target="tpu_custom_call" | custom-call | flops 5000000000 | bytes 10000000 | tf_op jit(solution)/shard_map/merge/pallas_call | solution.py:451
  122.1 0.0 collective-permute-done.7
  122.1 0.0 collective-permute-done.6
  122.1 0.0 collective-permute-done.5
  122.2 0.6 add_add_fusion
  (7 shorter events, 0.0 us)
Async XLA Ops:
  74.9 3.4 %collective-permute-start = (f32[640,512]{1,0:T(8,128)}, f32[640,512]{1,0:T(8,128)S(1)}, u32[]{:S(2)}, u32[]{:S(2)}) collective-permute-start(f32[640,512]{1,0:T(8,128)} %get-tuple-element.7.mine.pivot_mine), channel_id=1, source_target_pairs={{0,1},{1,0},{2,3},{3,2},{4,5},{5,4},{6,7},{7,6},{8,9},{9,8},{10,11... | collective-permute-start | bytes 3932168 | tf_op jit(solution)/shard_map/ppermute | solution.py:387
  75.5 40.3 %collective-permute-start.1 = (f32[608,512]{1,0:T(8,128)}, f32[608,512]{1,0:T(8,128)S(1)}, u32[]{:S(2)}, u32[]{:S(2)}) collective-permute-start(f32[608,512]{1,0:T(8,128)} %get-tuple-element.10.pack_mine), channel_id=1, source_target_pairs={{0,1},{1,0},{2,3},{3,2},{4,5},{5,4},{6,7},{7,6},{8,9},{9,8},{10,11... | collective-permute-start | bytes 3735560 | tf_op jit(solution)/shard_map/ppermute | solution.py:387
  78.3 1.3 %copy-start = (f32[640,512]{1,0:T(8,128)S(1)}, f32[640,512]{1,0:T(8,128)}, u32[]{:S(2)}) copy-start(f32[640,512]{1,0:T(8,128)} %get-tuple-element.7.mine.pivot_mine) | copy-start | bytes 3932164
  79.7 36.1 %copy-start.1 = (f32[640,512]{1,0:T(8,128)S(1)}, f32[640,512]{1,0:T(8,128)}, u32[]{:S(2)}) copy-start(f32[640,512]{1,0:T(8,128)} %get-tuple-element.7.mine.pivot_mine) | copy-start | bytes 3932164
  79.7 36.1 %copy-start.2 = (f32[608,512]{1,0:T(8,128)S(1)}, f32[608,512]{1,0:T(8,128)}, u32[]{:S(2)}) copy-start(f32[608,512]{1,0:T(8,128)} %get-tuple-element.10.pack_mine) | copy-start | bytes 3735556
  79.7 36.1 %copy-start.3 = (f32[512,512]{1,0:T(8,128)S(1)}, f32[512,512]{1,0:T(8,128)}, u32[]{:S(2)}) copy-start(f32[512,512]{1,0:T(8,128)} %get-tuple-element.11.outer_mine) | copy-start | bytes 3145732
  103.0 5.8 %collective-permute-start.4 = (f32[64,64]{1,0:T(8,128)S(1)}, f32[64,64]{1,0:T(8,128)S(1)}, u32[]{:S(2)}, u32[]{:S(2)}) collective-permute-start(f32[64,64]{1,0:T(8,128)S(1)} %get-tuple-element.9.tip_tip), channel_id=1, source_target_pairs={{0,6},{1,7},{2,4},{3,5},{4,2},{5,3},{6,0},{7,1},{8,14},{9,15},{10,... | collective-permute-start | bytes 49160 | tf_op jit(solution)/shard_map/ppermute | solution.py:387
  106.9 3.9 %collective-permute-start.3 = (f32[64,64]{1,0:T(8,128)S(1)}, f32[64,64]{1,0:T(8,128)S(1)}, u32[]{:S(2)}, u32[]{:S(2)}) collective-permute-start(f32[64,64]{1,0:T(8,128)S(1)} %get-tuple-element.9.tip_tip), channel_id=1, source_target_pairs={{0,4},{1,5},{2,6},{3,7},{4,0},{5,1},{6,2},{7,3},{8,12},{9,13},{10,... | collective-permute-start | bytes 49160 | tf_op jit(solution)/shard_map/ppermute | solution.py:387
  107.4 3.9 %collective-permute-start.2 = (f32[64,64]{1,0:T(8,128)S(1)}, f32[64,64]{1,0:T(8,128)S(1)}, u32[]{:S(2)}, u32[]{:S(2)}) collective-permute-start(f32[64,64]{1,0:T(8,128)S(1)} %get-tuple-element.9.tip_tip), channel_id=1, source_target_pairs={{0,2},{1,3},{2,0},{3,1},{4,6},{5,7},{6,4},{7,5},{8,10},{9,11},{10,... | collective-permute-start | bytes 49160 | tf_op jit(solution)/shard_map/ppermute | solution.py:387
  111.3 10.8 %collective-permute-start.7 = (f32[64,64]{1,0:T(8,128)S(1)}, f32[64,64]{1,0:T(8,128)S(1)}, u32[]{:S(2)}, u32[]{:S(2)}) collective-permute-start(f32[64,64]{1,0:T(8,128)S(1)} %add_add_fusion.1), channel_id=1, source_target_pairs={{0,24},{1,25},{2,26},{3,27},{4,28},{5,29},{6,30},{7,31},{8,16},{9,... | collective-permute-start | bytes 49160 | tf_op jit(solution)/shard_map/ppermute | solution.py:387
  115.0 7.2 %collective-permute-start.6 = (f32[64,64]{1,0:T(8,128)S(1)}, f32[64,64]{1,0:T(8,128)S(1)}, u32[]{:S(2)}, u32[]{:S(2)}) collective-permute-start(f32[64,64]{1,0:T(8,128)S(1)} %add_add_fusion.1), channel_id=1, source_target_pairs={{0,16},{1,17},{2,18},{3,19},{4,20},{5,21},{6,22},{7,23},{8,24},{9,... | collective-permute-start | bytes 49160 | tf_op jit(solution)/shard_map/ppermute | solution.py:387
  115.0 7.2 %collective-permute-start.5 = (f32[64,64]{1,0:T(8,128)S(1)}, f32[64,64]{1,0:T(8,128)S(1)}, u32[]{:S(2)}, u32[]{:S(2)}) collective-permute-start(f32[64,64]{1,0:T(8,128)S(1)} %add_add_fusion.1), channel_id=1, source_target_pairs={{0,8},{1,9},{2,10},{3,11},{4,12},{5,13},{6,14},{7,15},{8,0},{9,1},... | collective-permute-start | bytes 49160 | tf_op jit(solution)/shard_map/ppermute | solution.py:387
  115.8 6.4 %copy-start.4 = (f32[64,64]{1,0:T(8,128)S(1)}, f32[64,64]{1,0:T(8,128)}, u32[]{:S(2)}) copy-start(f32[64,64]{1,0:T(8,128)} %param.7) | copy-start | bytes 49156

commit v5 on v4

--- a/solution.py
+++ b/solution.py
@@ -10,6 +10,7 @@
 F32 = jnp.float32
 BF16 = jnp.bfloat16
 SUB = 8
+PAIR = 16
 LANES = 128
 HALF = 256
 NN = (((1,), (0,)), ((), ()))
@@ -49,19 +50,16 @@
 
 def late_update(work, step, top):
     value = work[...]
-    high, low = split(
-        jnp.concatenate([jnp.where(step % 2 == k, top, jnp.zeros_like(top)) for k in (0, 1)], axis=0)
-    )
     right = tuple(
         jnp.concatenate(
-            [jnp.where(step // 2 == k, part, jnp.zeros_like(part)) for k in range(8)], axis=0
+            [jnp.where(step == k, part, jnp.zeros_like(part)) for k in range(8)], axis=0
         )
-        for part in (high, low)
+        for part in split(top)
     )
     lane = lax.broadcasted_iota(jnp.int32, (LANES, LANES), 1)
-    panel = (lane >= SUB * step) & (lane < SUB * (step + 1))
+    panel = (lane >= PAIR * step) & (lane < PAIR * (step + 1))
     work[...] = jnp.where(panel, 0.0, value) - dot3(split(value), right)
-    work[pl.ds(pl.multiple_of(SUB * step, SUB), SUB), :] = top
+    work[pl.ds(pl.multiple_of(PAIR * step, PAIR), PAIR), :] = top
 
 
 def eliminated(value, pivot, first, second, corner, inverse):
@@ -76,17 +74,22 @@
     )
 
 
-def panel_step(work, step, state, late):
-    row, columns, last = state[0], list(state[1:9]), state[9]
+def turned(value, count):
+    return pltpu.roll(value, (LANES - count) % LANES, 1)
+
+
+def rows_of(value):
+    return [row_of(value, k) for k in range(SUB)]
+
+
+def columns_of(value, start):
+    return [column_of(value, start + k) for k in range(SUB)]
+
+
+def panel(row, columns):
+    columns = list(columns)
     sub = lax.broadcasted_iota(jnp.int32, (SUB, LANES), 0)
     lane = lax.broadcasted_iota(jnp.int32, (SUB, LANES), 1)
-    following = work[pl.ds(pl.multiple_of((step + 1) % 16 * SUB, SUB), SUB), :]
-    if late:
-        late_update(work, step - 1, last)
-        before = pltpu.roll(last, (LANES + SUB - SUB * step) % LANES, 1)
-        following = pltpu.roll(following, (LANES + SUB - SUB * step) % LANES, 1)
-        following = cleared(following, 0, [row_of(before, k) for k in range(SUB)])
-        following = pltpu.roll(following, LANES - SUB, 1)
     top = jnp.where(lane < SUB, jnp.where(lane == sub, 1.0, 0.0).astype(F32), row)
     for pivot in range(0, SUB, 2):
         a = row_of(columns[pivot], pivot)
@@ -96,26 +99,44 @@
         pair = (columns[pivot], columns[pivot + 1], (a, b, d), inverse)
         columns[pivot + 2 :] = [eliminated(value, pivot, *pair) for value in columns[pivot + 2 :]]
         top = eliminated(top, pivot, *pair)
-    following = cleared(following, 0, [row_of(top, k) for k in range(SUB)])
-    columns = [column_of(following, SUB + k) for k in range(SUB)]
-    row = pltpu.roll(following, LANES - SUB, 1)
-    return (row, *columns, pltpu.roll(top, SUB * step, 1))
+    return top
+
+
+def pair_step(work, step, state, late):
+    first, second, columns, last = state[0], state[1], state[2:10], state[10]
+    if late:
+        late_update(work, step - 1, last)
+    following = work[pl.ds(pl.multiple_of((step + 1) % 8 * PAIR, PAIR), PAIR), :]
+    following = [turned(following[k : k + SUB, :], PAIR * step) for k in (0, SUB)]
+    top = panel(first, columns)
+    rows = rows_of(top)
+    second = cleared(second, 0, rows)
+    columns = columns_of(second, SUB)
+    following = [turned(cleared(value, 0, rows), SUB) for value in following]
+    bottom = panel(turned(second, SUB), columns)
+    rows = rows_of(bottom)
+    following = [cleared(value, 0, rows) for value in following]
+    columns = columns_of(following[0], SUB)
+    top = cleared(turned(top, SUB), 0, rows)
+    last = jnp.concatenate([top, bottom], axis=0)
+    last = pltpu.roll(last, (PAIR * step + SUB) % LANES, 1)
+    return (*(turned(value, SUB) for value in following), *columns, last)
 
 
 def invert_128(blocks, works):
     states = []
     for block, work in zip(blocks, works):
         work[...] = block
-        row = block[:SUB, :]
-        columns = [column_of(row, k) for k in range(SUB)]
-        states.append(panel_step(work, 0, (row, *columns, row), False))
+        rows = [block[:SUB, :], block[SUB:PAIR, :]]
+        state = (*rows, *columns_of(rows[0], 0), block[:PAIR, :])
+        states.append(pair_step(work, 0, state, False))
 
     def step(index, carry):
-        return tuple(panel_step(work, index, state, True) for work, state in zip(works, carry))
-
-    states = lax.fori_loop(1, 16, step, tuple(states), unroll=3)
+        return tuple(pair_step(work, index, state, True) for work, state in zip(works, carry))
+
+    states = lax.fori_loop(1, 8, step, tuple(states))
     for work, state in zip(works, states):
-        late_update(work, 15, state[9])
+        late_update(work, 7, state[10])
     return [work[...] for work in works]
 
 
@@ -209,7 +230,7 @@
 
 def front_kernel(
     side, diag, lower, arrow, pivot_out, pack_out, outer_out,
-    dv, lv, av, ga, gah, gal, zah, zal, gb, gbh, gbl, zbh, zbl, pivot, work, sems,
+    dv, lv, av, ga, gah, gal, zah, zal, gb, gbh, gbl, zbh, zbl, pivot, work, work_b, sems,
 ):
     width, tip = diag.shape[1], arrow.shape[1]
     two = 2 * width
@@ -236,7 +257,7 @@
     first = (dv.at[1], ga, gah, gal, zah, zal)
     third = (dv.at[3], gb, gbh, gbl, zbh, zbl)
     outer_out[...] = dv[3]
-    eliminate([first, third], [work.at[0], work.at[1]])
+    eliminate([first, third], [work, work_b])
 
     def pick(left, right):
         return jnp.where(is_left, left, right)
@@ -270,7 +291,7 @@
     tip_tip = -update(first, *tt) - drop(update(third, *tt))
 
     second = (pivot, ga, gah, gal, zah, zal)
-    eliminate([second], [work.at[0]])
+    eliminate([second], [work])
     for start, size in chunks(width):
         rows = pl.ds(start, size)
         pivot_out[rows, :] = pivot_out[rows, :] - update(second, width + start, size, width, width)
@@ -428,7 +449,8 @@
         ]
         + system
         + system
-        + [pltpu.VMEM((width, width), F32), pltpu.VMEM((2, LANES, LANES), F32)]
+        + [pltpu.VMEM((width, width), F32)]
+        + [pltpu.VMEM((LANES, LANES), F32)] * 2
         + [pltpu.SemaphoreType.DMA((3 * count,))],
         compiler_params=params,
         name="front",

time: 123 us -> 115 us (0.935)
  Pallas kernels: 104 us -> 96 us
    pallas_call x1, Pallas kernels: 74.3 us -> 67.7 us  [local(): pl.pallas_call(front_kernel, out_shape=[jax.ShapeDtypeStruct((width + 2 *...]
    pallas_call x1, Pallas kernels: 23.3 us -> 22 us  [local(): pl.pallas_call(factor_kernel, out_shape=[jax.ShapeDtypeStruct((width, wid...]
  transfers between devices with their start and end apart: 8 -> 8, of which waited for: 4 -> 4; matrix products, arithmetic and copies ran while one was open for 0% -> 0% of each run, Pallas kernels for 24% -> 25%
where the time goes in v5:
time: 115 us
  Pallas kernels  96 us (83%)
  starting transfers between devices  9.58 us (8%)
  waiting for transfers between devices  6.58 us (6%)
  local copies, waits for them, and re-layouts  1.33 us (1%)
    pallas_call x1, Pallas kernels, local(): pl.pallas_call(front_kernel, out_shape=[jax.ShapeDtypeStruct((width + 2 *...  67.7 us
    pallas_call x1, Pallas kernels, local(): pl.pallas_call(factor_kernel, out_shape=[jax.ShapeDtypeStruct((width, wid...  22 us
    ppermute x8, starting transfers between devices, swapped(): return lax.ppermute(value, axis, [(k, k ^ mask) for k in range(count)])  9.58 us
    ppermute x8, waiting for transfers between devices, swapped(): return lax.ppermute(value, axis, [(k, k ^ mask) for k in range(count)])  6.58 us
    pallas_call x1, Pallas kernels, local(): pl.pallas_call(merge_kernel, out_shape=jax.ShapeDtypeStruct((half, front)...  6.33 us
  transfers between devices with their start and end apart: 8, of which 4 were waited for; matrix products, arithmetic and copies ran while one was open for 0% of the time, Pallas kernels for 25%

profile of v5, /device:TPU:0, one launch (start us, length us, event | category | flops | bytes accessed | tf_op | source)
XLA Modules:
  0.0 114.8 jit_solution(3453589401050505596)
XLA Ops:
  0.6 67.7 %front.1 = (f32[640,512]{1,0:T(8,128)}, f32[608,512]{1,0:T(8,128)}, f32[512,512]{1,0:T(8,128)}) custom-call(s32[1]{0:T(128)} %bitcast.side, f32[4,512,512]{2,1,0:T(8,128)} %diag.1, f32[4,512,512]{2,1,0:T(8,128)} %lower.1, f32[4,64,512]{2,1,0:T(8,128)} %arrow.1), custom_call_target="tpu_custom_call" | custom-call | tf_op jit(solution)/shard_map/front/pallas_call | solution.py:436
  68.3 0.5 collective-permute-start
  68.8 0.1 collective-permute-start.1
  68.9 2.8 %collective-permute-done.other.pivot_other = f32[640,512]{1,0:T(8,128)S(1)} collective-permute-done((f32[640,512]{1,0:T(8,128)}, f32[640,512]{1,0:T(8,128)S(1)}, u32[]{:S(2)}, u32[]{:S(2)}) %collective-permute-start) | collective-permute-done | bytes 1310752 | tf_op jit(solution)/shard_map/ppermute | solution.py:408
  71.7 1.3 %copy-done = f32[640,512]{1,0:T(8,128)S(1)} copy-done((f32[640,512]{1,0:T(8,128)S(1)}, f32[640,512]{1,0:T(8,128)}, u32[]{:S(2)}) %copy-start) | copy-done | bytes 1310744
  73.0 22.0 %factor.1 = (f32[512,512]{1,0:T(8,128)S(1)}, f32[64,64]{1,0:T(8,128)S(1)}) custom-call(f32[640,512]{1,0:T(8,128)S(1)} %copy-done, f32[640,512]{1,0:T(8,128)S(1)} %collective-permute-done.other.pivot_other), custom_call_target="tpu_custom_call" | custom-call | flops 10000000000 | bytes 10000000 | tf_op jit(solution)/shard_map/factor/pallas_call | solution.py:460
  95.0 3.9 %collective-permute-start.4 = (f32[64,64]{1,0:T(8,128)S(1)}, f32[64,64]{1,0:T(8,128)S(1)}, u32[]{:S(2)}, u32[]{:S(2)}) collective-permute-start(f32[64,64]{1,0:T(8,128)S(1)} %get-tuple-element.9.tip_tip), channel_id=1, source_target_pairs={{0,6},{1,7},{2,4},{3,5},{4,2},{5,3},{6,0},{7,1},{8,14},{9,15},{10,... | collective-permute-start | bytes 49160 | tf_op jit(solution)/shard_map/ppermute | solution.py:408
  98.9 0.5 collective-permute-start.3
  99.4 0.1 collective-permute-start.2
  99.6 1.3 %collective-permute-done.4 = f32[64,64]{1,0:T(8,128)S(1)} collective-permute-done((f32[64,64]{1,0:T(8,128)S(1)}, f32[64,64]{1,0:T(8,128)S(1)}, u32[]{:S(2)}, u32[]{:S(2)}) %collective-permute-start.4) | collective-permute-done | bytes 16416 | tf_op jit(solution)/shard_map/ppermute | solution.py:408
  100.8 2.0 %collective-permute-done.3 = f32[64,64]{1,0:T(8,128)S(1)} collective-permute-done((f32[64,64]{1,0:T(8,128)S(1)}, f32[64,64]{1,0:T(8,128)S(1)}, u32[]{:S(2)}, u32[]{:S(2)}) %collective-permute-start.3) | collective-permute-done | bytes 16416 | tf_op jit(solution)/shard_map/ppermute | solution.py:408
  102.8 0.5 collective-permute-done.2
  103.4 3.7 %collective-permute-start.7 = (f32[64,64]{1,0:T(8,128)S(1)}, f32[64,64]{1,0:T(8,128)S(1)}, u32[]{:S(2)}, u32[]{:S(2)}) collective-permute-start(f32[64,64]{1,0:T(8,128)S(1)} %add_add_fusion.1), channel_id=1, source_target_pairs={{0,24},{1,25},{2,26},{3,27},{4,28},{5,29},{6,30},{7,31},{8,16},{9,... | collective-permute-start | bytes 49160 | tf_op jit(solution)/shard_map/ppermute | solution.py:408
  107.0 0.0 collective-permute-start.6
  107.0 0.8 collective-permute-start.5
  107.8 0.0 collective-permute-done.1.pack_other
  107.8 0.0 copy-done.1
  107.8 0.0 copy-done.2
  107.8 0.0 copy-start.4
  107.9 6.3 %merge.1 = f32[544,1088]{1,0:T(8,128)} custom-call(s32[1]{0:T(128)} %bitcast.side, f32[512,512]{1,0:T(8,128)S(1)} %get-tuple-element.8.inverse, f32[64,64]{1,0:T(8,128)S(1)} %get-tuple-element.9.tip_tip, f32[640,512]{1,0:T(8,128)S(1)} %copy-done.1, f32[640,512]{1,0:T(8,128)S(1)} %collective-permute-done.other.pivot_other, f32[608,512]{1,0:T(8,128)S(1)} %copy-done.2, ...), custom_call_target="tpu_custom_call" | custom-call | flops 5000000000 | bytes 10000000 | tf_op jit(solution)/shard_map/merge/pallas_call | solution.py:473
  114.2 0.0 collective-permute-done.7
  114.2 0.0 collective-permute-done.6
  114.2 0.0 collective-permute-done.5
  114.2 0.6 add_add_fusion
  (7 shorter events, 0.0 us)
Async XLA Ops:
  68.3 3.4 %collective-permute-start = (f32[640,512]{1,0:T(8,128)}, f32[640,512]{1,0:T(8,128)S(1)}, u32[]{:S(2)}, u32[]{:S(2)}) collective-permute-start(f32[640,512]{1,0:T(8,128)} %get-tuple-element.7.mine.pivot_mine), channel_id=1, source_target_pairs={{0,1},{1,0},{2,3},{3,2},{4,5},{5,4},{6,7},{7,6},{8,9},{9,8},{10,11... | collective-permute-start | bytes 3932168 | tf_op jit(solution)/shard_map/ppermute | solution.py:408
  68.8 39.0 %collective-permute-start.1 = (f32[608,512]{1,0:T(8,128)}, f32[608,512]{1,0:T(8,128)S(1)}, u32[]{:S(2)}, u32[]{:S(2)}) collective-permute-start(f32[608,512]{1,0:T(8,128)} %get-tuple-element.10.pack_mine), channel_id=1, source_target_pairs={{0,1},{1,0},{2,3},{3,2},{4,5},{5,4},{6,7},{7,6},{8,9},{9,8},{10,11... | collective-permute-start | bytes 3735560 | tf_op jit(solution)/shard_map/ppermute | solution.py:408
  71.7 1.3 %copy-start = (f32[640,512]{1,0:T(8,128)S(1)}, f32[640,512]{1,0:T(8,128)}, u32[]{:S(2)}) copy-start(f32[640,512]{1,0:T(8,128)} %get-tuple-element.7.mine.pivot_mine) | copy-start | bytes 3932164
  73.0 34.8 %copy-start.1 = (f32[640,512]{1,0:T(8,128)S(1)}, f32[640,512]{1,0:T(8,128)}, u32[]{:S(2)}) copy-start(f32[640,512]{1,0:T(8,128)} %get-tuple-element.7.mine.pivot_mine) | copy-start | bytes 3932164
  73.0 34.8 %copy-start.2 = (f32[608,512]{1,0:T(8,128)S(1)}, f32[608,512]{1,0:T(8,128)}, u32[]{:S(2)}) copy-start(f32[608,512]{1,0:T(8,128)} %get-tuple-element.10.pack_mine) | copy-start | bytes 3735556
  73.0 34.8 %copy-start.3 = (f32[512,512]{1,0:T(8,128)S(1)}, f32[512,512]{1,0:T(8,128)}, u32[]{:S(2)}) copy-start(f32[512,512]{1,0:T(8,128)} %get-tuple-element.11.outer_mine) | copy-start | bytes 3145732
  95.0 5.8 %collective-permute-start.4 = (f32[64,64]{1,0:T(8,128)S(1)}, f32[64,64]{1,0:T(8,128)S(1)}, u32[]{:S(2)}, u32[]{:S(2)}) collective-permute-start(f32[64,64]{1,0:T(8,128)S(1)} %get-tuple-element.9.tip_tip), channel_id=1, source_target_pairs={{0,6},{1,7},{2,4},{3,5},{4,2},{5,3},{6,0},{7,1},{8,14},{9,15},{10,... | collective-permute-start | bytes 49160 | tf_op jit(solution)/shard_map/ppermute | solution.py:408
  98.9 3.9 %collective-permute-start.3 = (f32[64,64]{1,0:T(8,128)S(1)}, f32[64,64]{1,0:T(8,128)S(1)}, u32[]{:S(2)}, u32[]{:S(2)}) collective-permute-start(f32[64,64]{1,0:T(8,128)S(1)} %get-tuple-element.9.tip_tip), channel_id=1, source_target_pairs={{0,4},{1,5},{2,6},{3,7},{4,0},{5,1},{6,2},{7,3},{8,12},{9,13},{10,... | collective-permute-start | bytes 49160 | tf_op jit(solution)/shard_map/ppermute | solution.py:408
  99.4 3.9 %collective-permute-start.2 = (f32[64,64]{1,0:T(8,128)S(1)}, f32[64,64]{1,0:T(8,128)S(1)}, u32[]{:S(2)}, u32[]{:S(2)}) collective-permute-start(f32[64,64]{1,0:T(8,128)S(1)} %get-tuple-element.9.tip_tip), channel_id=1, source_target_pairs={{0,2},{1,3},{2,0},{3,1},{4,6},{5,7},{6,4},{7,5},{8,10},{9,11},{10,... | collective-permute-start | bytes 49160 | tf_op jit(solution)/shard_map/ppermute | solution.py:408
  103.4 10.8 %collective-permute-start.7 = (f32[64,64]{1,0:T(8,128)S(1)}, f32[64,64]{1,0:T(8,128)S(1)}, u32[]{:S(2)}, u32[]{:S(2)}) collective-permute-start(f32[64,64]{1,0:T(8,128)S(1)} %add_add_fusion.1), channel_id=1, source_target_pairs={{0,24},{1,25},{2,26},{3,27},{4,28},{5,29},{6,30},{7,31},{8,16},{9,... | collective-permute-start | bytes 49160 | tf_op jit(solution)/shard_map/ppermute | solution.py:408
  107.0 7.2 %collective-permute-start.6 = (f32[64,64]{1,0:T(8,128)S(1)}, f32[64,64]{1,0:T(8,128)S(1)}, u32[]{:S(2)}, u32[]{:S(2)}) collective-permute-start(f32[64,64]{1,0:T(8,128)S(1)} %add_add_fusion.1), channel_id=1, source_target_pairs={{0,16},{1,17},{2,18},{3,19},{4,20},{5,21},{6,22},{7,23},{8,24},{9,... | collective-permute-start | bytes 49160 | tf_op jit(solution)/shard_map/ppermute | solution.py:408
  107.0 7.2 %collective-permute-start.5 = (f32[64,64]{1,0:T(8,128)S(1)}, f32[64,64]{1,0:T(8,128)S(1)}, u32[]{:S(2)}, u32[]{:S(2)}) collective-permute-start(f32[64,64]{1,0:T(8,128)S(1)} %add_add_fusion.1), channel_id=1, source_target_pairs={{0,8},{1,9},{2,10},{3,11},{4,12},{5,13},{6,14},{7,15},{8,0},{9,1},... | collective-permute-start | bytes 49160 | tf_op jit(solution)/shard_map/ppermute | solution.py:408
  107.8 6.4 %copy-start.4 = (f32[64,64]{1,0:T(8,128)S(1)}, f32[64,64]{1,0:T(8,128)}, u32[]{:S(2)}) copy-start(f32[64,64]{1,0:T(8,128)} %param.7) | copy-start | bytes 49156

commit v6 on v5

--- a/solution.py
+++ b/solution.py
@@ -43,8 +43,8 @@
 
 def cleared(value, start, top):
     lane = lax.broadcasted_iota(jnp.int32, (SUB, LANES), 1)
-    panel = (lane >= start) & (lane < start + SUB)
-    terms = [column_of(value, start + k) * top[k] for k in range(SUB)]
+    panel = (lane >= start) & (lane < start + len(top))
+    terms = [column_of(value, start + k) * row for k, row in enumerate(top)]
     return jnp.where(panel, 0.0, value) - total(terms)
 
 
@@ -86,11 +86,12 @@
     return [column_of(value, start + k) for k in range(SUB)]
 
 
-def panel(row, columns):
+def panel(row, columns, start):
     columns = list(columns)
     sub = lax.broadcasted_iota(jnp.int32, (SUB, LANES), 0)
-    lane = lax.broadcasted_iota(jnp.int32, (SUB, LANES), 1)
-    top = jnp.where(lane < SUB, jnp.where(lane == sub, 1.0, 0.0).astype(F32), row)
+    lane = lax.broadcasted_iota(jnp.int32, (SUB, LANES), 1) - start
+    inside = (lane >= 0) & (lane < SUB)
+    top = jnp.where(inside, jnp.where(lane == sub, 1.0, 0.0).astype(F32), row)
     for pivot in range(0, SUB, 2):
         a = row_of(columns[pivot], pivot)
         b = row_of(columns[pivot + 1], pivot)
@@ -103,24 +104,24 @@
 
 
 def pair_step(work, step, state, late):
-    first, second, columns, last = state[0], state[1], state[2:10], state[10]
+    first, second, columns, last = state[0], state[1], state[2:10], list(state[10:])
+    following = work[pl.ds(pl.multiple_of((step + 1) % 8 * PAIR, PAIR), PAIR), :]
+    following = [following[:SUB, :], following[SUB:, :]]
     if late:
-        late_update(work, step - 1, last)
-    following = work[pl.ds(pl.multiple_of((step + 1) % 8 * PAIR, PAIR), PAIR), :]
-    following = [turned(following[k : k + SUB, :], PAIR * step) for k in (0, SUB)]
-    top = panel(first, columns)
+        late_update(work, step - 1, pltpu.roll(jnp.concatenate(last, axis=0), PAIR * (step - 1), 1))
+        rows = rows_of(last[0]) + rows_of(last[1])
+        following = [turned(value, PAIR * (step - 1)) for value in following]
+        following = [turned(cleared(value, 0, rows), PAIR) for value in following]
+    top = panel(first, columns, 0)
     rows = rows_of(top)
     second = cleared(second, 0, rows)
-    columns = columns_of(second, SUB)
-    following = [turned(cleared(value, 0, rows), SUB) for value in following]
-    bottom = panel(turned(second, SUB), columns)
+    following = [cleared(value, 0, rows) for value in following]
+    bottom = panel(second, columns_of(second, SUB), SUB)
     rows = rows_of(bottom)
-    following = [cleared(value, 0, rows) for value in following]
-    columns = columns_of(following[0], SUB)
-    top = cleared(turned(top, SUB), 0, rows)
-    last = jnp.concatenate([top, bottom], axis=0)
-    last = pltpu.roll(last, (PAIR * step + SUB) % LANES, 1)
-    return (*(turned(value, SUB) for value in following), *columns, last)
+    following = [cleared(value, SUB, rows) for value in following]
+    top = cleared(top, SUB, rows)
+    columns = columns_of(following[0], PAIR)
+    return (*(turned(value, PAIR) for value in following), *columns, top, bottom)
 
 
 def invert_128(blocks, works):
@@ -128,7 +129,7 @@
     for block, work in zip(blocks, works):
         work[...] = block
         rows = [block[:SUB, :], block[SUB:PAIR, :]]
-        state = (*rows, *columns_of(rows[0], 0), block[:PAIR, :])
+        state = (*rows, *columns_of(rows[0], 0), *rows)
         states.append(pair_step(work, 0, state, False))
 
     def step(index, carry):
@@ -136,7 +137,7 @@
 
     states = lax.fori_loop(1, 8, step, tuple(states))
     for work, state in zip(works, states):
-        late_update(work, 7, state[10])
+        late_update(work, 7, pltpu.roll(jnp.concatenate(state[10:], axis=0), 7 * PAIR, 1))
     return [work[...] for work in works]
 
 

time: 115 us -> 112 us (0.974)
  Pallas kernels: 96 us -> 93.5 us
    pallas_call x1, Pallas kernels: 22 us -> 20.6 us  [local(): pl.pallas_call(factor_kernel, out_shape=[jax.ShapeDtypeStruct((width, wid...]
    pallas_call x1, Pallas kernels: 67.7 us -> 66.3 us  [local(): pl.pallas_call(front_kernel, out_shape=[jax.ShapeDtypeStruct((width + 2 *...]
  transfers between devices with their start and end apart: 8 -> 8, of which waited for: 4 -> 4; matrix products, arithmetic and copies ran while one was open for 0% -> 0% of each run, Pallas kernels for 25% -> 24%
where the time goes in v6:
time: 112 us
  Pallas kernels  93.5 us (83%)
  starting transfers between devices  9.58 us (9%)
  waiting for transfers between devices  6.57 us (6%)
  local copies, waits for them, and re-layouts  1.33 us (1%)
    pallas_call x1, Pallas kernels, local(): pl.pallas_call(front_kernel, out_shape=[jax.ShapeDtypeStruct((width + 2 *...  66.3 us
    pallas_call x1, Pallas kernels, local(): pl.pallas_call(factor_kernel, out_shape=[jax.ShapeDtypeStruct((width, wid...  20.6 us
    ppermute x8, starting transfers between devices, swapped(): return lax.ppermute(value, axis, [(k, k ^ mask) for k in range(count)])  9.58 us
    ppermute x8, waiting for transfers between devices, swapped(): return lax.ppermute(value, axis, [(k, k ^ mask) for k in range(count)])  6.57 us
    pallas_call x1, Pallas kernels, local(): pl.pallas_call(merge_kernel, out_shape=jax.ShapeDtypeStruct((half, front)...  6.57 us
  transfers between devices with their start and end apart: 8, of which 4 were waited for; matrix products, arithmetic and copies ran while one was open for 0% of the time, Pallas kernels for 24%

profile of v6, /device:TPU:0, one launch (start us, length us, event | category | flops | bytes accessed | tf_op | source)
XLA Modules:
  0.0 112.3 jit_solution(10056501430010457140)
XLA Ops:
  0.6 66.3 %front.1 = (f32[640,512]{1,0:T(8,128)}, f32[608,512]{1,0:T(8,128)}, f32[512,512]{1,0:T(8,128)}) custom-call(s32[1]{0:T(128)} %bitcast.side, f32[4,512,512]{2,1,0:T(8,128)} %diag.1, f32[4,512,512]{2,1,0:T(8,128)} %lower.1, f32[4,64,512]{2,1,0:T(8,128)} %arrow.1), custom_call_target="tpu_custom_call" | custom-call | tf_op jit(solution)/shard_map/front/pallas_call | solution.py:437
  66.9 0.5 collective-permute-start
  67.5 0.1 collective-permute-start.1
  67.5 2.8 %collective-permute-done.other.pivot_other = f32[640,512]{1,0:T(8,128)S(1)} collective-permute-done((f32[640,512]{1,0:T(8,128)}, f32[640,512]{1,0:T(8,128)S(1)}, u32[]{:S(2)}, u32[]{:S(2)}) %collective-permute-start) | collective-permute-done | bytes 1310752 | tf_op jit(solution)/shard_map/ppermute | solution.py:409
  70.3 1.3 %copy-done = f32[640,512]{1,0:T(8,128)S(1)} copy-done((f32[640,512]{1,0:T(8,128)S(1)}, f32[640,512]{1,0:T(8,128)}, u32[]{:S(2)}) %copy-start) | copy-done | bytes 1310744
  71.7 20.6 %factor.1 = (f32[512,512]{1,0:T(8,128)S(1)}, f32[64,64]{1,0:T(8,128)S(1)}) custom-call(f32[640,512]{1,0:T(8,128)S(1)} %copy-done, f32[640,512]{1,0:T(8,128)S(1)} %collective-permute-done.other.pivot_other), custom_call_target="tpu_custom_call" | custom-call | flops 10000000000 | bytes 10000000 | tf_op jit(solution)/shard_map/factor/pallas_call | solution.py:461
  92.3 3.9 %collective-permute-start.4 = (f32[64,64]{1,0:T(8,128)S(1)}, f32[64,64]{1,0:T(8,128)S(1)}, u32[]{:S(2)}, u32[]{:S(2)}) collective-permute-start(f32[64,64]{1,0:T(8,128)S(1)} %get-tuple-element.9.tip_tip), channel_id=1, source_target_pairs={{0,6},{1,7},{2,4},{3,5},{4,2},{5,3},{6,0},{7,1},{8,14},{9,15},{10,... | collective-permute-start | bytes 49160 | tf_op jit(solution)/shard_map/ppermute | solution.py:409
  96.2 0.5 collective-permute-start.3
  96.7 0.1 collective-permute-start.2
  96.8 1.3 %collective-permute-done.4 = f32[64,64]{1,0:T(8,128)S(1)} collective-permute-done((f32[64,64]{1,0:T(8,128)S(1)}, f32[64,64]{1,0:T(8,128)S(1)}, u32[]{:S(2)}, u32[]{:S(2)}) %collective-permute-start.4) | collective-permute-done | bytes 16416 | tf_op jit(solution)/shard_map/ppermute | solution.py:409
  98.1 2.0 %collective-permute-done.3 = f32[64,64]{1,0:T(8,128)S(1)} collective-permute-done((f32[64,64]{1,0:T(8,128)S(1)}, f32[64,64]{1,0:T(8,128)S(1)}, u32[]{:S(2)}, u32[]{:S(2)}) %collective-permute-start.3) | collective-permute-done | bytes 16416 | tf_op jit(solution)/shard_map/ppermute | solution.py:409
  100.1 0.5 collective-permute-done.2
  100.6 3.7 %collective-permute-start.7 = (f32[64,64]{1,0:T(8,128)S(1)}, f32[64,64]{1,0:T(8,128)S(1)}, u32[]{:S(2)}, u32[]{:S(2)}) collective-permute-start(f32[64,64]{1,0:T(8,128)S(1)} %add_add_fusion.1), channel_id=1, source_target_pairs={{0,24},{1,25},{2,26},{3,27},{4,28},{5,29},{6,30},{7,31},{8,16},{9,... | collective-permute-start | bytes 49160 | tf_op jit(solution)/shard_map/ppermute | solution.py:409
  104.3 0.0 collective-permute-start.6
  104.3 0.8 collective-permute-start.5
  105.1 0.0 collective-permute-done.1.pack_other
  105.1 0.0 copy-done.1
  105.1 0.0 copy-done.2
  105.1 0.0 copy-start.4
  105.1 6.6 %merge.1 = f32[544,1088]{1,0:T(8,128)} custom-call(s32[1]{0:T(128)} %bitcast.side, f32[512,512]{1,0:T(8,128)S(1)} %get-tuple-element.8.inverse, f32[64,64]{1,0:T(8,128)S(1)} %get-tuple-element.9.tip_tip, f32[640,512]{1,0:T(8,128)S(1)} %copy-done.1, f32[640,512]{1,0:T(8,128)S(1)} %collective-permute-done.other.pivot_other, f32[608,512]{1,0:T(8,128)S(1)} %copy-done.2, ...), custom_call_target="tpu_custom_call" | custom-call | flops 5000000000 | bytes 10000000 | tf_op jit(solution)/shard_map/merge/pallas_call | solution.py:474
  111.7 0.0 collective-permute-done.7
  111.7 0.0 collective-permute-done.6
  111.7 0.0 collective-permute-done.5
  111.7 0.6 add_add_fusion
  (7 shorter events, 0.0 us)
Async XLA Ops:
  66.9 3.4 %collective-permute-start = (f32[640,512]{1,0:T(8,128)}, f32[640,512]{1,0:T(8,128)S(1)}, u32[]{:S(2)}, u32[]{:S(2)}) collective-permute-start(f32[640,512]{1,0:T(8,128)} %get-tuple-element.7.mine.pivot_mine), channel_id=1, source_target_pairs={{0,1},{1,0},{2,3},{3,2},{4,5},{5,4},{6,7},{7,6},{8,9},{9,8},{10,11... | collective-permute-start | bytes 3932168 | tf_op jit(solution)/shard_map/ppermute | solution.py:409
  67.5 37.6 %collective-permute-start.1 = (f32[608,512]{1,0:T(8,128)}, f32[608,512]{1,0:T(8,128)S(1)}, u32[]{:S(2)}, u32[]{:S(2)}) collective-permute-start(f32[608,512]{1,0:T(8,128)} %get-tuple-element.10.pack_mine), channel_id=1, source_target_pairs={{0,1},{1,0},{2,3},{3,2},{4,5},{5,4},{6,7},{7,6},{8,9},{9,8},{10,11... | collective-permute-start | bytes 3735560 | tf_op jit(solution)/shard_map/ppermute | solution.py:409
  70.3 1.3 %copy-start = (f32[640,512]{1,0:T(8,128)S(1)}, f32[640,512]{1,0:T(8,128)}, u32[]{:S(2)}) copy-start(f32[640,512]{1,0:T(8,128)} %get-tuple-element.7.mine.pivot_mine) | copy-start | bytes 3932164
  71.6 33.4 %copy-start.1 = (f32[640,512]{1,0:T(8,128)S(1)}, f32[640,512]{1,0:T(8,128)}, u32[]{:S(2)}) copy-start(f32[640,512]{1,0:T(8,128)} %get-tuple-element.7.mine.pivot_mine) | copy-start | bytes 3932164
  71.6 33.4 %copy-start.2 = (f32[608,512]{1,0:T(8,128)S(1)}, f32[608,512]{1,0:T(8,128)}, u32[]{:S(2)}) copy-start(f32[608,512]{1,0:T(8,128)} %get-tuple-element.10.pack_mine) | copy-start | bytes 3735556
  71.6 33.4 %copy-start.3 = (f32[512,512]{1,0:T(8,128)S(1)}, f32[512,512]{1,0:T(8,128)}, u32[]{:S(2)}) copy-start(f32[512,512]{1,0:T(8,128)} %get-tuple-element.11.outer_mine) | copy-start | bytes 3145732
  92.3 5.8 %collective-permute-start.4 = (f32[64,64]{1,0:T(8,128)S(1)}, f32[64,64]{1,0:T(8,128)S(1)}, u32[]{:S(2)}, u32[]{:S(2)}) collective-permute-start(f32[64,64]{1,0:T(8,128)S(1)} %get-tuple-element.9.tip_tip), channel_id=1, source_target_pairs={{0,6},{1,7},{2,4},{3,5},{4,2},{5,3},{6,0},{7,1},{8,14},{9,15},{10,... | collective-permute-start | bytes 49160 | tf_op jit(solution)/shard_map/ppermute | solution.py:409
  96.2 3.9 %collective-permute-start.3 = (f32[64,64]{1,0:T(8,128)S(1)}, f32[64,64]{1,0:T(8,128)S(1)}, u32[]{:S(2)}, u32[]{:S(2)}) collective-permute-start(f32[64,64]{1,0:T(8,128)S(1)} %get-tuple-element.9.tip_tip), channel_id=1, source_target_pairs={{0,4},{1,5},{2,6},{3,7},{4,0},{5,1},{6,2},{7,3},{8,12},{9,13},{10,... | collective-permute-start | bytes 49160 | tf_op jit(solution)/shard_map/ppermute | solution.py:409
  96.7 3.9 %collective-permute-start.2 = (f32[64,64]{1,0:T(8,128)S(1)}, f32[64,64]{1,0:T(8,128)S(1)}, u32[]{:S(2)}, u32[]{:S(2)}) collective-permute-start(f32[64,64]{1,0:T(8,128)S(1)} %get-tuple-element.9.tip_tip), channel_id=1, source_target_pairs={{0,2},{1,3},{2,0},{3,1},{4,6},{5,7},{6,4},{7,5},{8,10},{9,11},{10,... | collective-permute-start | bytes 49160 | tf_op jit(solution)/shard_map/ppermute | solution.py:409
  100.6 11.1 %collective-permute-start.7 = (f32[64,64]{1,0:T(8,128)S(1)}, f32[64,64]{1,0:T(8,128)S(1)}, u32[]{:S(2)}, u32[]{:S(2)}) collective-permute-start(f32[64,64]{1,0:T(8,128)S(1)} %add_add_fusion.1), channel_id=1, source_target_pairs={{0,24},{1,25},{2,26},{3,27},{4,28},{5,29},{6,30},{7,31},{8,16},{9,... | collective-permute-start | bytes 49160 | tf_op jit(solution)/shard_map/ppermute | solution.py:409
  104.3 7.4 %collective-permute-start.6 = (f32[64,64]{1,0:T(8,128)S(1)}, f32[64,64]{1,0:T(8,128)S(1)}, u32[]{:S(2)}, u32[]{:S(2)}) collective-permute-start(f32[64,64]{1,0:T(8,128)S(1)} %add_add_fusion.1), channel_id=1, source_target_pairs={{0,16},{1,17},{2,18},{3,19},{4,20},{5,21},{6,22},{7,23},{8,24},{9,... | collective-permute-start | bytes 49160 | tf_op jit(solution)/shard_map/ppermute | solution.py:409
  104.3 7.4 %collective-permute-start.5 = (f32[64,64]{1,0:T(8,128)S(1)}, f32[64,64]{1,0:T(8,128)S(1)}, u32[]{:S(2)}, u32[]{:S(2)}) collective-permute-start(f32[64,64]{1,0:T(8,128)S(1)} %add_add_fusion.1), channel_id=1, source_target_pairs={{0,8},{1,9},{2,10},{3,11},{4,12},{5,13},{6,14},{7,15},{8,0},{9,1},... | collective-permute-start | bytes 49160 | tf_op jit(solution)/shard_map/ppermute | solution.py:409
  105.1 6.6 %copy-start.4 = (f32[64,64]{1,0:T(8,128)S(1)}, f32[64,64]{1,0:T(8,128)}, u32[]{:S(2)}) copy-start(f32[64,64]{1,0:T(8,128)} %param.7) | copy-start | bytes 49156

commit v7 on v6

--- a/solution.py
+++ b/solution.py
@@ -62,18 +62,6 @@
     work[pl.ds(pl.multiple_of(PAIR * step, PAIR), PAIR), :] = top
 
 
-def eliminated(value, pivot, first, second, corner, inverse):
-    sub = lax.broadcasted_iota(jnp.int32, (SUB, LANES), 0)
-    a, b, d = corner
-    upper, lower = row_of(value, pivot), row_of(value, pivot + 1)
-    upper, lower = d * upper - b * lower, a * lower - b * upper
-    product = first * upper + second * lower
-    rest = value - product * inverse
-    return jnp.where(
-        sub == pivot, upper * inverse, jnp.where(sub == pivot + 1, lower * inverse, rest)
-    )
-
-
 def turned(value, count):
     return pltpu.roll(value, (LANES - count) % LANES, 1)
 
@@ -87,20 +75,46 @@
 
 
 def panel(row, columns, start):
-    columns = list(columns)
     sub = lax.broadcasted_iota(jnp.int32, (SUB, LANES), 0)
     lane = lax.broadcasted_iota(jnp.int32, (SUB, LANES), 1) - start
     inside = (lane >= 0) & (lane < SUB)
-    top = jnp.where(inside, jnp.where(lane == sub, 1.0, 0.0).astype(F32), row)
-    for pivot in range(0, SUB, 2):
-        a = row_of(columns[pivot], pivot)
-        b = row_of(columns[pivot + 1], pivot)
-        d = row_of(columns[pivot + 1], pivot + 1)
+    rows = rows_of(jnp.where(inside, jnp.where(lane == sub, 1.0, 0.0).astype(F32), row))
+    entry = {(i, k): row_of(columns[k], i) for k in range(SUB) for i in range(k, SUB)}
+    factors = {}
+    for k in range(0, SUB, 2):
+        a, b, d = entry[k, k], entry[k + 1, k], entry[k + 1, k + 1]
         inverse = pltpu.reciprocal(a * d - b * b)
-        pair = (columns[pivot], columns[pivot + 1], (a, b, d), inverse)
-        columns[pivot + 2 :] = [eliminated(value, pivot, *pair) for value in columns[pivot + 2 :]]
-        top = eliminated(top, pivot, *pair)
-    return top
+        below = range(k + 2, SUB)
+        raw = {
+            i: (d * entry[i, k] - b * entry[i, k + 1], a * entry[i, k + 1] - b * entry[i, k])
+            for i in below
+        }
+        for i in below:
+            factors[i, k], factors[i, k + 1] = raw[i][0] * inverse, raw[i][1] * inverse
+        for j in below:
+            for i in range(j, SUB):
+                left = raw[i] if i < k + 4 else (factors[i, k], factors[i, k + 1])
+                product = left[0] * entry[j, k] + left[1] * entry[j, k + 1]
+                entry[i, j] = entry[i, j] - (product * inverse if i < k + 4 else product)
+        for i in below:
+            rows[i] = rows[i] - (factors[i, k] * rows[k] + factors[i, k + 1] * rows[k + 1])
+        rows[k], rows[k + 1] = (
+            (d * rows[k] - b * rows[k + 1]) * inverse,
+            (a * rows[k + 1] - b * rows[k]) * inverse,
+        )
+    for k in range(SUB - 2, 0, -2):
+        for i in range(k):
+            rows[i] = rows[i] - (factors[k, i] * rows[k] + factors[k + 1, i] * rows[k + 1])
+    return rows
+
+
+def joined(rows):
+    sub = lax.broadcasted_iota(jnp.int32, (SUB, LANES), 0)
+    for half in (1, 2, 4):
+        rows = [
+            jnp.where(sub & half == 0, rows[k], rows[k + 1]) for k in range(0, len(rows), 2)
+        ]
+    return rows[0]
 
 
 def pair_step(work, step, state, late):
@@ -112,12 +126,12 @@
         rows = rows_of(last[0]) + rows_of(last[1])
         following = [turned(value, PAIR * (step - 1)) for value in following]
         following = [turned(cleared(value, 0, rows), PAIR) for value in following]
-    top = panel(first, columns, 0)
-    rows = rows_of(top)
+    rows = panel(first, columns, 0)
+    top = joined(rows)
     second = cleared(second, 0, rows)
     following = [cleared(value, 0, rows) for value in following]
-    bottom = panel(second, columns_of(second, SUB), SUB)
-    rows = rows_of(bottom)
+    rows = panel(second, columns_of(second, SUB), SUB)
+    bottom = joined(rows)
     following = [cleared(value, SUB, rows) for value in following]
     top = cleared(top, SUB, rows)
     columns = columns_of(following[0], PAIR)

time: 112 us -> 113 us (level)
  no operation moved by 1% of the time
where the time goes in v7:
time: 113 us
  Pallas kernels  94.5 us (84%)
  starting transfers between devices  9.57 us (8%)
  waiting for transfers between devices  6.58 us (6%)
  local copies, waits for them, and re-layouts  1.33 us (1%)
    pallas_call x1, Pallas kernels, local(): pl.pallas_call(front_kernel, out_shape=[jax.ShapeDtypeStruct((width + 2 *...  66.9 us
    pallas_call x1, Pallas kernels, local(): pl.pallas_call(factor_kernel, out_shape=[jax.ShapeDtypeStruct((width, wid...  21 us
    ppermute x8, starting transfers between devices, swapped(): return lax.ppermute(value, axis, [(k, k ^ mask) for k in range(count)])  9.57 us
    ppermute x8, waiting for transfers between devices, swapped(): return lax.ppermute(value, axis, [(k, k ^ mask) for k in range(count)])  6.58 us
    pallas_call x1, Pallas kernels, local(): pl.pallas_call(merge_kernel, out_shape=jax.ShapeDtypeStruct((half, front)...  6.57 us
  transfers between devices with their start and end apart: 8, of which 4 were waited for; matrix products, arithmetic and copies ran while one was open for 0% of the time, Pallas kernels for 24%

profile of v7, /device:TPU:0, one launch (start us, length us, event | category | flops | bytes accessed | tf_op | source)
XLA Modules:
  0.0 113.3 jit_solution(6157232558690976642)
XLA Ops:
  0.6 66.9 %front.1 = (f32[640,512]{1,0:T(8,128)}, f32[608,512]{1,0:T(8,128)}, f32[512,512]{1,0:T(8,128)}) custom-call(s32[1]{0:T(128)} %bitcast.side, f32[4,512,512]{2,1,0:T(8,128)} %diag.1, f32[4,512,512]{2,1,0:T(8,128)} %lower.1, f32[4,64,512]{2,1,0:T(8,128)} %arrow.1), custom_call_target="tpu_custom_call" | custom-call | tf_op jit(solution)/shard_map/front/pallas_call | solution.py:451
  67.5 0.5 collective-permute-start
  68.0 0.1 collective-permute-start.1
  68.1 2.8 %collective-permute-done.other.pivot_other = f32[640,512]{1,0:T(8,128)S(1)} collective-permute-done((f32[640,512]{1,0:T(8,128)}, f32[640,512]{1,0:T(8,128)S(1)}, u32[]{:S(2)}, u32[]{:S(2)}) %collective-permute-start) | collective-permute-done | bytes 1310752 | tf_op jit(solution)/shard_map/ppermute | solution.py:423
  70.9 1.3 %copy-done = f32[640,512]{1,0:T(8,128)S(1)} copy-done((f32[640,512]{1,0:T(8,128)S(1)}, f32[640,512]{1,0:T(8,128)}, u32[]{:S(2)}) %copy-start) | copy-done | bytes 1310744
  72.2 21.0 %factor.1 = (f32[512,512]{1,0:T(8,128)S(1)}, f32[64,64]{1,0:T(8,128)S(1)}) custom-call(f32[640,512]{1,0:T(8,128)S(1)} %copy-done, f32[640,512]{1,0:T(8,128)S(1)} %collective-permute-done.other.pivot_other), custom_call_target="tpu_custom_call" | custom-call | flops 10000000000 | bytes 10000000 | tf_op jit(solution)/shard_map/factor/pallas_call | solution.py:475
  93.3 3.9 %collective-permute-start.4 = (f32[64,64]{1,0:T(8,128)S(1)}, f32[64,64]{1,0:T(8,128)S(1)}, u32[]{:S(2)}, u32[]{:S(2)}) collective-permute-start(f32[64,64]{1,0:T(8,128)S(1)} %get-tuple-element.9.tip_tip), channel_id=1, source_target_pairs={{0,6},{1,7},{2,4},{3,5},{4,2},{5,3},{6,0},{7,1},{8,14},{9,15},{10,... | collective-permute-start | bytes 49160 | tf_op jit(solution)/shard_map/ppermute | solution.py:423
  97.2 0.5 collective-permute-start.3
  97.7 0.1 collective-permute-start.2
  97.8 1.3 %collective-permute-done.4 = f32[64,64]{1,0:T(8,128)S(1)} collective-permute-done((f32[64,64]{1,0:T(8,128)S(1)}, f32[64,64]{1,0:T(8,128)S(1)}, u32[]{:S(2)}, u32[]{:S(2)}) %collective-permute-start.4) | collective-permute-done | bytes 16416 | tf_op jit(solution)/shard_map/ppermute | solution.py:423
  99.0 2.0 %collective-permute-done.3 = f32[64,64]{1,0:T(8,128)S(1)} collective-permute-done((f32[64,64]{1,0:T(8,128)S(1)}, f32[64,64]{1,0:T(8,128)S(1)}, u32[]{:S(2)}, u32[]{:S(2)}) %collective-permute-start.3) | collective-permute-done | bytes 16416 | tf_op jit(solution)/shard_map/ppermute | solution.py:423
  101.1 0.5 collective-permute-done.2
  101.6 3.7 %collective-permute-start.7 = (f32[64,64]{1,0:T(8,128)S(1)}, f32[64,64]{1,0:T(8,128)S(1)}, u32[]{:S(2)}, u32[]{:S(2)}) collective-permute-start(f32[64,64]{1,0:T(8,128)S(1)} %add_add_fusion.1), channel_id=1, source_target_pairs={{0,24},{1,25},{2,26},{3,27},{4,28},{5,29},{6,30},{7,31},{8,16},{9,... | collective-permute-start | bytes 49160 | tf_op jit(solution)/shard_map/ppermute | solution.py:423
  105.3 0.0 collective-permute-start.6
  105.3 0.8 collective-permute-start.5
  106.0 0.0 collective-permute-done.1.pack_other
  106.0 0.0 copy-done.1
  106.1 0.0 copy-done.2
  106.1 0.0 copy-start.4
  106.1 6.6 %merge.1 = f32[544,1088]{1,0:T(8,128)} custom-call(s32[1]{0:T(128)} %bitcast.side, f32[512,512]{1,0:T(8,128)S(1)} %get-tuple-element.8.inverse, f32[64,64]{1,0:T(8,128)S(1)} %get-tuple-element.9.tip_tip, f32[640,512]{1,0:T(8,128)S(1)} %copy-done.1, f32[640,512]{1,0:T(8,128)S(1)} %collective-permute-done.other.pivot_other, f32[608,512]{1,0:T(8,128)S(1)} %copy-done.2, ...), custom_call_target="tpu_custom_call" | custom-call | flops 5000000000 | bytes 10000000 | tf_op jit(solution)/shard_map/merge/pallas_call | solution.py:488
  112.6 0.0 collective-permute-done.7
  112.6 0.0 collective-permute-done.6
  112.7 0.0 collective-permute-done.5
  112.7 0.6 add_add_fusion
  (7 shorter events, 0.0 us)
Async XLA Ops:
  67.5 3.4 %collective-permute-start = (f32[640,512]{1,0:T(8,128)}, f32[640,512]{1,0:T(8,128)S(1)}, u32[]{:S(2)}, u32[]{:S(2)}) collective-permute-start(f32[640,512]{1,0:T(8,128)} %get-tuple-element.7.mine.pivot_mine), channel_id=1, source_target_pairs={{0,1},{1,0},{2,3},{3,2},{4,5},{5,4},{6,7},{7,6},{8,9},{9,8},{10,11... | collective-permute-start | bytes 3932168 | tf_op jit(solution)/shard_map/ppermute | solution.py:423
  68.0 38.0 %collective-permute-start.1 = (f32[608,512]{1,0:T(8,128)}, f32[608,512]{1,0:T(8,128)S(1)}, u32[]{:S(2)}, u32[]{:S(2)}) collective-permute-start(f32[608,512]{1,0:T(8,128)} %get-tuple-element.10.pack_mine), channel_id=1, source_target_pairs={{0,1},{1,0},{2,3},{3,2},{4,5},{5,4},{6,7},{7,6},{8,9},{9,8},{10,11... | collective-permute-start | bytes 3735560 | tf_op jit(solution)/shard_map/ppermute | solution.py:423
  70.9 1.3 %copy-start = (f32[640,512]{1,0:T(8,128)S(1)}, f32[640,512]{1,0:T(8,128)}, u32[]{:S(2)}) copy-start(f32[640,512]{1,0:T(8,128)} %get-tuple-element.7.mine.pivot_mine) | copy-start | bytes 3932164
  72.2 33.8 %copy-start.1 = (f32[640,512]{1,0:T(8,128)S(1)}, f32[640,512]{1,0:T(8,128)}, u32[]{:S(2)}) copy-start(f32[640,512]{1,0:T(8,128)} %get-tuple-element.7.mine.pivot_mine) | copy-start | bytes 3932164
  72.2 33.8 %copy-start.2 = (f32[608,512]{1,0:T(8,128)S(1)}, f32[608,512]{1,0:T(8,128)}, u32[]{:S(2)}) copy-start(f32[608,512]{1,0:T(8,128)} %get-tuple-element.10.pack_mine) | copy-start | bytes 3735556
  72.2 33.8 %copy-start.3 = (f32[512,512]{1,0:T(8,128)S(1)}, f32[512,512]{1,0:T(8,128)}, u32[]{:S(2)}) copy-start(f32[512,512]{1,0:T(8,128)} %get-tuple-element.11.outer_mine) | copy-start | bytes 3145732
  93.3 5.8 %collective-permute-start.4 = (f32[64,64]{1,0:T(8,128)S(1)}, f32[64,64]{1,0:T(8,128)S(1)}, u32[]{:S(2)}, u32[]{:S(2)}) collective-permute-start(f32[64,64]{1,0:T(8,128)S(1)} %get-tuple-element.9.tip_tip), channel_id=1, source_target_pairs={{0,6},{1,7},{2,4},{3,5},{4,2},{5,3},{6,0},{7,1},{8,14},{9,15},{10,... | collective-permute-start | bytes 49160 | tf_op jit(solution)/shard_map/ppermute | solution.py:423
  97.2 3.9 %collective-permute-start.3 = (f32[64,64]{1,0:T(8,128)S(1)}, f32[64,64]{1,0:T(8,128)S(1)}, u32[]{:S(2)}, u32[]{:S(2)}) collective-permute-start(f32[64,64]{1,0:T(8,128)S(1)} %get-tuple-element.9.tip_tip), channel_id=1, source_target_pairs={{0,4},{1,5},{2,6},{3,7},{4,0},{5,1},{6,2},{7,3},{8,12},{9,13},{10,... | collective-permute-start | bytes 49160 | tf_op jit(solution)/shard_map/ppermute | solution.py:423
  97.7 3.9 %collective-permute-start.2 = (f32[64,64]{1,0:T(8,128)S(1)}, f32[64,64]{1,0:T(8,128)S(1)}, u32[]{:S(2)}, u32[]{:S(2)}) collective-permute-start(f32[64,64]{1,0:T(8,128)S(1)} %get-tuple-element.9.tip_tip), channel_id=1, source_target_pairs={{0,2},{1,3},{2,0},{3,1},{4,6},{5,7},{6,4},{7,5},{8,10},{9,11},{10,... | collective-permute-start | bytes 49160 | tf_op jit(solution)/shard_map/ppermute | solution.py:423
  101.6 11.1 %collective-permute-start.7 = (f32[64,64]{1,0:T(8,128)S(1)}, f32[64,64]{1,0:T(8,128)S(1)}, u32[]{:S(2)}, u32[]{:S(2)}) collective-permute-start(f32[64,64]{1,0:T(8,128)S(1)} %add_add_fusion.1), channel_id=1, source_target_pairs={{0,24},{1,25},{2,26},{3,27},{4,28},{5,29},{6,30},{7,31},{8,16},{9,... | collective-permute-start | bytes 49160 | tf_op jit(solution)/shard_map/ppermute | solution.py:423
  105.3 7.4 %collective-permute-start.6 = (f32[64,64]{1,0:T(8,128)S(1)}, f32[64,64]{1,0:T(8,128)S(1)}, u32[]{:S(2)}, u32[]{:S(2)}) collective-permute-start(f32[64,64]{1,0:T(8,128)S(1)} %add_add_fusion.1), channel_id=1, source_target_pairs={{0,16},{1,17},{2,18},{3,19},{4,20},{5,21},{6,22},{7,23},{8,24},{9,... | collective-permute-start | bytes 49160 | tf_op jit(solution)/shard_map/ppermute | solution.py:423
  105.3 7.4 %collective-permute-start.5 = (f32[64,64]{1,0:T(8,128)S(1)}, f32[64,64]{1,0:T(8,128)S(1)}, u32[]{:S(2)}, u32[]{:S(2)}) collective-permute-start(f32[64,64]{1,0:T(8,128)S(1)} %add_add_fusion.1), channel_id=1, source_target_pairs={{0,8},{1,9},{2,10},{3,11},{4,12},{5,13},{6,14},{7,15},{8,0},{9,1},... | collective-permute-start | bytes 49160 | tf_op jit(solution)/shard_map/ppermute | solution.py:423
  106.1 6.6 %copy-start.4 = (f32[64,64]{1,0:T(8,128)S(1)}, f32[64,64]{1,0:T(8,128)}, u32[]{:S(2)}) copy-start(f32[64,64]{1,0:T(8,128)} %param.7) | copy-start | bytes 49156

commit v8 on v6

--- a/solution.py
+++ b/solution.py
@@ -13,6 +13,8 @@
 PAIR = 16
 LANES = 128
 HALF = 256
+CHUNK = 576
+SLICE = 80
 NN = (((1,), (0,)), ((), ()))
 NT = (((1,), (1,)), ((), ()))
 
@@ -24,7 +26,9 @@
 
 def dot3(left, right, dims=NN):
     one = functools.partial(lax.dot_general, dimension_numbers=dims, preferred_element_type=F32)
-    return one(left[0], right[0]) + (one(left[0], right[1]) + one(left[1], right[0]))
+    count = left[0].shape[0]
+    both = one(jnp.concatenate(left, axis=0), right[0])
+    return both[:count] + (both[count:] + one(left[0], right[1]))
 
 
 def row_of(value, index):
@@ -124,7 +128,8 @@
     return (*(turned(value, PAIR) for value in following), *columns, top, bottom)
 
 
-def invert_128(blocks, works):
+def invert_128(blocks, works, beside, slot):
+    beside(slot)
     states = []
     for block, work in zip(blocks, works):
         work[...] = block
@@ -133,6 +138,7 @@
         states.append(pair_step(work, 0, state, False))
 
     def step(index, carry):
+        beside(slot + index)
         return tuple(pair_step(work, index, state, True) for work, state in zip(works, carry))
 
     states = lax.fori_loop(1, 8, step, tuple(states))
@@ -141,8 +147,8 @@
     return [work[...] for work in works]
 
 
-def invert_256(blocks, works):
-    firsts = invert_128([block[0] for block in blocks], works)
+def invert_256(blocks, works, beside=lambda slot: None):
+    firsts = invert_128([block[0] for block in blocks], works, beside, 0)
     seconds, sides = [], []
     for first, (_, right, below, last) in zip(firsts, blocks):
         first, right, below = split(first), split(right), split(below)
@@ -150,7 +156,7 @@
         seconds.append(last - dot3(low, right))
         sides.append((low, split(dot3(first, right))))
     results = []
-    for first, second, (low, high) in zip(firsts, invert_128(seconds, works), sides):
+    for first, second, (low, high) in zip(firsts, invert_128(seconds, works, beside, 8), sides):
         corner = split(second)
         below = dot3(corner, low)
         top = jnp.concatenate([first + dot3(high, split(below)), -dot3(high, corner)], axis=1)
@@ -169,7 +175,8 @@
 
 
 def chunks(count):
-    return [(start, min(HALF, count - start)) for start in range(0, count, HALF)]
+    parts = -(-count // CHUNK)
+    return [(k * count // parts, count // parts) for k in range(parts)]
 
 
 def equilibrate(pivot):
@@ -191,23 +198,29 @@
 
 def eliminate(systems, works):
     scales = [equilibrate(system[0]) for system in systems]
-    upper = [quarters(system[0][:HALF, :HALF]) for system in systems]
-    upper = [split(value) for value in invert_256(upper, works)]
+    upper = invert_256([quarters(system[0][:HALF, :HALF]) for system in systems], works)
     lower = []
-    for (pivot, g, gh, gl, zh, zl), inverse, scale in zip(systems, upper, scales):
-        right = split(pivot[:HALF, HALF:])
+    for system, inverse, scale in zip(systems, upper, scales):
+        pivot, parts, row = system[0], system[6], system[7]
+        inverse, right = split(inverse), split(pivot[:HALF, HALF:])
+        parts[0], parts[1], parts[2], parts[3] = (*inverse, *right)
+        row[...] = scale
         low = split(dot3(split(pivot[HALF:, :HALF]), inverse))
         lower.append(pivot[HALF:, HALF:] - dot3(low, right))
-        for start, size in chunks(g.shape[0]):
-            rows = pl.ds(start, size)
-            part = split(g[rows, :HALF] * scale[:, :HALF])
+
+    def forward(slot):
+        for _, g, gh, gl, zh, zl, parts, row in systems:
+            start = jnp.minimum(slot * (SLICE // PAIR), (g.shape[0] - SLICE) // PAIR) * PAIR
+            rows = pl.ds(pl.multiple_of(start, PAIR), SLICE)
+            part = split(g[rows, :HALF] * row[:, :HALF])
             gh[rows, :HALF], gl[rows, :HALF] = part
-            solved = split(dot3(part, inverse))
+            solved = split(dot3(part, (parts[0], parts[1])))
             zh[rows, :HALF], zl[rows, :HALF] = solved
-            part = split(g[rows, HALF:] * scale[:, HALF:] - dot3(solved, right))
+            part = split(g[rows, HALF:] * row[:, HALF:] - dot3(solved, (parts[2], parts[3])))
             gh[rows, HALF:], gl[rows, HALF:] = part
-    lower = [split(x) for x in invert_256([quarters(value) for value in lower], works)]
-    for (pivot, g, gh, gl, zh, zl), inverse in zip(systems, lower):
+
+    lower = [split(x) for x in invert_256([quarters(x) for x in lower], works, forward)]
+    for (_, g, gh, gl, zh, zl, *_), inverse in zip(systems, lower):
         for start, size in chunks(g.shape[0]):
             rows = pl.ds(start, size)
             solved = split(dot3((gh[rows, HALF:], gl[rows, HALF:]), inverse))
@@ -215,7 +228,7 @@
 
 
 def update(system, row, rows, column, columns):
-    _, _, gh, gl, zh, zl = system
+    gh, gl, zh, zl = system[2:6]
     row, column = pl.ds(row, rows), pl.ds(column, columns)
     return dot3((zh[row, :], zl[row, :]), (gh[column, :], gl[column, :]), NT)
 
@@ -231,7 +244,7 @@
 
 def front_kernel(
     side, diag, lower, arrow, pivot_out, pack_out, outer_out,
-    dv, lv, av, ga, gah, gal, zah, zal, gb, gbh, gbl, zbh, zbl, pivot, work, work_b, sems,
+    dv, lv, av, ga, gah, gal, zah, zal, pa, ra, gb, gbh, gbl, zbh, zbl, pb, rb, pivot, work, work_b, sems,
 ):
     width, tip = diag.shape[1], arrow.shape[1]
     two = 2 * width
@@ -255,8 +268,8 @@
     gb[:width, :] = lv[3]
     transpose_into(gb, width, lv.at[2])
     gb[two:, :] = av[3]
-    first = (dv.at[1], ga, gah, gal, zah, zal)
-    third = (dv.at[3], gb, gbh, gbl, zbh, zbl)
+    first = (dv.at[1], ga, gah, gal, zah, zal, pa, ra)
+    third = (dv.at[3], gb, gbh, gbl, zbh, zbl, pb, rb)
     outer_out[...] = dv[3]
     eliminate([first, third], [work, work_b])
 
@@ -291,7 +304,7 @@
     tt = (two, tip, two, tip)
     tip_tip = -update(first, *tt) - drop(update(third, *tt))
 
-    second = (pivot, ga, gah, gal, zah, zal)
+    second = (pivot, ga, gah, gal, zah, zal, pa, ra)
     eliminate([second], [work])
     for start, size in chunks(width):
         rows = pl.ds(start, size)
@@ -433,6 +446,7 @@
     vmem = pl.BlockSpec(memory_space=pltpu.VMEM)
     parts = [pltpu.VMEM((front, width), BF16)] * 4
     system = [pltpu.VMEM((front, width), F32)] + parts
+    system += [pltpu.VMEM((4, HALF, HALF), BF16), pltpu.VMEM((1, width), F32)]
     params = pltpu.CompilerParams(vmem_limit_bytes=56 * 2**20)
     pivot, pack, outer = pl.pallas_call(
         front_kernel,

time: 112 us -> 108 us (0.964)
  Pallas kernels: 93.5 us -> 89.2 us
    pallas_call x1, Pallas kernels: 66.3 us -> 62.7 us  [local(): pl.pallas_call(front_kernel, out_shape=[jax.ShapeDtypeStruct((width + 2 *...]
where the time goes in v8:
time: 108 us
  Pallas kernels  89.2 us (83%)
  starting transfers between devices  9.57 us (9%)
  waiting for transfers between devices  6.58 us (6%)
  local copies, waits for them, and re-layouts  1.33 us (1%)
    pallas_call x1, Pallas kernels, local(): pl.pallas_call(front_kernel, out_shape=[jax.ShapeDtypeStruct((width + 2 *...  62.7 us
    pallas_call x1, Pallas kernels, local(): pl.pallas_call(factor_kernel, out_shape=[jax.ShapeDtypeStruct((width, wid...  20.4 us
    ppermute x8, starting transfers between devices, swapped(): return lax.ppermute(value, axis, [(k, k ^ mask) for k in range(count)])  9.57 us
    ppermute x8, waiting for transfers between devices, swapped(): return lax.ppermute(value, axis, [(k, k ^ mask) for k in range(count)])  6.58 us
    pallas_call x1, Pallas kernels, local(): pl.pallas_call(merge_kernel, out_shape=jax.ShapeDtypeStruct((half, front)...  6.01 us
  transfers between devices with their start and end apart: 8, of which 4 were waited for; matrix products, arithmetic and copies ran while one was open for 0% of the time, Pallas kernels for 24%

profile of v8, /device:TPU:0, one launch (start us, length us, event | category | flops | bytes accessed | tf_op | source)
XLA Modules:
  0.0 108.0 jit_solution(15034673699991195167)
XLA Ops:
  0.6 62.7 %front.1 = (f32[640,512]{1,0:T(8,128)}, f32[608,512]{1,0:T(8,128)}, f32[512,512]{1,0:T(8,128)}) custom-call(s32[1]{0:T(128)} %bitcast.side, f32[4,512,512]{2,1,0:T(8,128)} %diag.1, f32[4,512,512]{2,1,0:T(8,128)} %lower.1, f32[4,64,512]{2,1,0:T(8,128)} %arrow.1), custom_call_target="tpu_custom_call" | custom-call | tf_op jit(solution)/shard_map/front/pallas_call | solution.py:451
  63.4 0.5 collective-permute-start
  63.9 0.1 collective-permute-start.1
  64.0 2.8 %collective-permute-done.other.pivot_other = f32[640,512]{1,0:T(8,128)S(1)} collective-permute-done((f32[640,512]{1,0:T(8,128)}, f32[640,512]{1,0:T(8,128)S(1)}, u32[]{:S(2)}, u32[]{:S(2)}) %collective-permute-start) | collective-permute-done | bytes 1310752 | tf_op jit(solution)/shard_map/ppermute | solution.py:422
  66.8 1.3 %copy-done = f32[640,512]{1,0:T(8,128)S(1)} copy-done((f32[640,512]{1,0:T(8,128)S(1)}, f32[640,512]{1,0:T(8,128)}, u32[]{:S(2)}) %copy-start) | copy-done | bytes 1310744
  68.1 20.4 %factor.1 = (f32[512,512]{1,0:T(8,128)S(1)}, f32[64,64]{1,0:T(8,128)S(1)}) custom-call(f32[640,512]{1,0:T(8,128)S(1)} %copy-done, f32[640,512]{1,0:T(8,128)S(1)} %collective-permute-done.other.pivot_other), custom_call_target="tpu_custom_call" | custom-call | flops 10000000000 | bytes 10000000 | tf_op jit(solution)/shard_map/factor/pallas_call | solution.py:475
  88.5 3.9 %collective-permute-start.4 = (f32[64,64]{1,0:T(8,128)S(1)}, f32[64,64]{1,0:T(8,128)S(1)}, u32[]{:S(2)}, u32[]{:S(2)}) collective-permute-start(f32[64,64]{1,0:T(8,128)S(1)} %get-tuple-element.9.tip_tip), channel_id=1, source_target_pairs={{0,6},{1,7},{2,4},{3,5},{4,2},{5,3},{6,0},{7,1},{8,14},{9,15},{10,... | collective-permute-start | bytes 49160 | tf_op jit(solution)/shard_map/ppermute | solution.py:422
  92.4 0.5 collective-permute-start.3
  92.9 0.1 collective-permute-start.2
  93.1 1.3 %collective-permute-done.4 = f32[64,64]{1,0:T(8,128)S(1)} collective-permute-done((f32[64,64]{1,0:T(8,128)S(1)}, f32[64,64]{1,0:T(8,128)S(1)}, u32[]{:S(2)}, u32[]{:S(2)}) %collective-permute-start.4) | collective-permute-done | bytes 16416 | tf_op jit(solution)/shard_map/ppermute | solution.py:422
  94.3 2.0 %collective-permute-done.3 = f32[64,64]{1,0:T(8,128)S(1)} collective-permute-done((f32[64,64]{1,0:T(8,128)S(1)}, f32[64,64]{1,0:T(8,128)S(1)}, u32[]{:S(2)}, u32[]{:S(2)}) %collective-permute-start.3) | collective-permute-done | bytes 16416 | tf_op jit(solution)/shard_map/ppermute | solution.py:422
  96.3 0.5 collective-permute-done.2
  96.9 3.7 %collective-permute-start.7 = (f32[64,64]{1,0:T(8,128)S(1)}, f32[64,64]{1,0:T(8,128)S(1)}, u32[]{:S(2)}, u32[]{:S(2)}) collective-permute-start(f32[64,64]{1,0:T(8,128)S(1)} %add_add_fusion.1), channel_id=1, source_target_pairs={{0,24},{1,25},{2,26},{3,27},{4,28},{5,29},{6,30},{7,31},{8,16},{9,... | collective-permute-start | bytes 49160 | tf_op jit(solution)/shard_map/ppermute | solution.py:422
  100.5 0.0 collective-permute-start.6
  100.5 0.8 collective-permute-start.5
  101.3 0.0 collective-permute-done.1.pack_other
  101.3 0.0 copy-done.1
  101.3 0.0 copy-done.2
  101.3 0.0 copy-start.4
  101.3 6.0 %merge.1 = f32[544,1088]{1,0:T(8,128)} custom-call(s32[1]{0:T(128)} %bitcast.side, f32[512,512]{1,0:T(8,128)S(1)} %get-tuple-element.8.inverse, f32[64,64]{1,0:T(8,128)S(1)} %get-tuple-element.9.tip_tip, f32[640,512]{1,0:T(8,128)S(1)} %copy-done.1, f32[640,512]{1,0:T(8,128)S(1)} %collective-permute-done.other.pivot_other, f32[608,512]{1,0:T(8,128)S(1)} %copy-done.2, ...), custom_call_target="tpu_custom_call" | custom-call | flops 5000000000 | bytes 10000000 | tf_op jit(solution)/shard_map/merge/pallas_call | solution.py:488
  107.4 0.0 collective-permute-done.7
  107.4 0.0 collective-permute-done.6
  107.4 0.0 collective-permute-done.5
  107.4 0.6 add_add_fusion
  (7 shorter events, 0.0 us)
Async XLA Ops:
  63.4 3.4 %collective-permute-start = (f32[640,512]{1,0:T(8,128)}, f32[640,512]{1,0:T(8,128)S(1)}, u32[]{:S(2)}, u32[]{:S(2)}) collective-permute-start(f32[640,512]{1,0:T(8,128)} %get-tuple-element.7.mine.pivot_mine), channel_id=1, source_target_pairs={{0,1},{1,0},{2,3},{3,2},{4,5},{5,4},{6,7},{7,6},{8,9},{9,8},{10,11... | collective-permute-start | bytes 3932168 | tf_op jit(solution)/shard_map/ppermute | solution.py:422
  63.9 37.4 %collective-permute-start.1 = (f32[608,512]{1,0:T(8,128)}, f32[608,512]{1,0:T(8,128)S(1)}, u32[]{:S(2)}, u32[]{:S(2)}) collective-permute-start(f32[608,512]{1,0:T(8,128)} %get-tuple-element.10.pack_mine), channel_id=1, source_target_pairs={{0,1},{1,0},{2,3},{3,2},{4,5},{5,4},{6,7},{7,6},{8,9},{9,8},{10,11... | collective-permute-start | bytes 3735560 | tf_op jit(solution)/shard_map/ppermute | solution.py:422
  66.8 1.3 %copy-start = (f32[640,512]{1,0:T(8,128)S(1)}, f32[640,512]{1,0:T(8,128)}, u32[]{:S(2)}) copy-start(f32[640,512]{1,0:T(8,128)} %get-tuple-element.7.mine.pivot_mine) | copy-start | bytes 3932164
  68.1 33.2 %copy-start.1 = (f32[640,512]{1,0:T(8,128)S(1)}, f32[640,512]{1,0:T(8,128)}, u32[]{:S(2)}) copy-start(f32[640,512]{1,0:T(8,128)} %get-tuple-element.7.mine.pivot_mine) | copy-start | bytes 3932164
  68.1 33.2 %copy-start.2 = (f32[608,512]{1,0:T(8,128)S(1)}, f32[608,512]{1,0:T(8,128)}, u32[]{:S(2)}) copy-start(f32[608,512]{1,0:T(8,128)} %get-tuple-element.10.pack_mine) | copy-start | bytes 3735556
  68.1 33.2 %copy-start.3 = (f32[512,512]{1,0:T(8,128)S(1)}, f32[512,512]{1,0:T(8,128)}, u32[]{:S(2)}) copy-start(f32[512,512]{1,0:T(8,128)} %get-tuple-element.11.outer_mine) | copy-start | bytes 3145732
  88.5 5.8 %collective-permute-start.4 = (f32[64,64]{1,0:T(8,128)S(1)}, f32[64,64]{1,0:T(8,128)S(1)}, u32[]{:S(2)}, u32[]{:S(2)}) collective-permute-start(f32[64,64]{1,0:T(8,128)S(1)} %get-tuple-element.9.tip_tip), channel_id=1, source_target_pairs={{0,6},{1,7},{2,4},{3,5},{4,2},{5,3},{6,0},{7,1},{8,14},{9,15},{10,... | collective-permute-start | bytes 49160 | tf_op jit(solution)/shard_map/ppermute | solution.py:422
  92.4 3.9 %collective-permute-start.3 = (f32[64,64]{1,0:T(8,128)S(1)}, f32[64,64]{1,0:T(8,128)S(1)}, u32[]{:S(2)}, u32[]{:S(2)}) collective-permute-start(f32[64,64]{1,0:T(8,128)S(1)} %get-tuple-element.9.tip_tip), channel_id=1, source_target_pairs={{0,4},{1,5},{2,6},{3,7},{4,0},{5,1},{6,2},{7,3},{8,12},{9,13},{10,... | collective-permute-start | bytes 49160 | tf_op jit(solution)/shard_map/ppermute | solution.py:422
  92.9 3.9 %collective-permute-start.2 = (f32[64,64]{1,0:T(8,128)S(1)}, f32[64,64]{1,0:T(8,128)S(1)}, u32[]{:S(2)}, u32[]{:S(2)}) collective-permute-start(f32[64,64]{1,0:T(8,128)S(1)} %get-tuple-element.9.tip_tip), channel_id=1, source_target_pairs={{0,2},{1,3},{2,0},{3,1},{4,6},{5,7},{6,4},{7,5},{8,10},{9,11},{10,... | collective-permute-start | bytes 49160 | tf_op jit(solution)/shard_map/ppermute | solution.py:422
  96.9 10.5 %collective-permute-start.7 = (f32[64,64]{1,0:T(8,128)S(1)}, f32[64,64]{1,0:T(8,128)S(1)}, u32[]{:S(2)}, u32[]{:S(2)}) collective-permute-start(f32[64,64]{1,0:T(8,128)S(1)} %add_add_fusion.1), channel_id=1, source_target_pairs={{0,24},{1,25},{2,26},{3,27},{4,28},{5,29},{6,30},{7,31},{8,16},{9,... | collective-permute-start | bytes 49160 | tf_op jit(solution)/shard_map/ppermute | solution.py:422
  100.5 6.8 %collective-permute-start.6 = (f32[64,64]{1,0:T(8,128)S(1)}, f32[64,64]{1,0:T(8,128)S(1)}, u32[]{:S(2)}, u32[]{:S(2)}) collective-permute-start(f32[64,64]{1,0:T(8,128)S(1)} %add_add_fusion.1), channel_id=1, source_target_pairs={{0,16},{1,17},{2,18},{3,19},{4,20},{5,21},{6,22},{7,23},{8,24},{9,... | collective-permute-start | bytes 49160 | tf_op jit(solution)/shard_map/ppermute | solution.py:422
  100.5 6.8 %collective-permute-start.5 = (f32[64,64]{1,0:T(8,128)S(1)}, f32[64,64]{1,0:T(8,128)S(1)}, u32[]{:S(2)}, u32[]{:S(2)}) collective-permute-start(f32[64,64]{1,0:T(8,128)S(1)} %add_add_fusion.1), channel_id=1, source_target_pairs={{0,8},{1,9},{2,10},{3,11},{4,12},{5,13},{6,14},{7,15},{8,0},{9,1},... | collective-permute-start | bytes 49160 | tf_op jit(solution)/shard_map/ppermute | solution.py:422
  101.3 6.0 %copy-start.4 = (f32[64,64]{1,0:T(8,128)S(1)}, f32[64,64]{1,0:T(8,128)}, u32[]{:S(2)}) copy-start(f32[64,64]{1,0:T(8,128)} %param.7) | copy-start | bytes 49156

commit v9 on v8

--- a/solution.py
+++ b/solution.py
@@ -128,7 +128,7 @@
     return (*(turned(value, PAIR) for value in following), *columns, top, bottom)
 
 
-def invert_128(blocks, works, beside, slot):
+def invert_128(blocks, works, beside, slot, unroll):
     beside(slot)
     states = []
     for block, work in zip(blocks, works):
@@ -141,14 +141,14 @@
         beside(slot + index)
         return tuple(pair_step(work, index, state, True) for work, state in zip(works, carry))
 
-    states = lax.fori_loop(1, 8, step, tuple(states))
+    states = lax.fori_loop(1, 8, step, tuple(states), unroll=unroll)
     for work, state in zip(works, states):
         late_update(work, 7, pltpu.roll(jnp.concatenate(state[10:], axis=0), 7 * PAIR, 1))
     return [work[...] for work in works]
 
 
-def invert_256(blocks, works, beside=lambda slot: None):
-    firsts = invert_128([block[0] for block in blocks], works, beside, 0)
+def invert_256(blocks, works, beside=lambda slot: None, unroll=1):
+    firsts = invert_128([block[0] for block in blocks], works, beside, 0, unroll)
     seconds, sides = [], []
     for first, (_, right, below, last) in zip(firsts, blocks):
         first, right, below = split(first), split(right), split(below)
@@ -156,7 +156,7 @@
         seconds.append(last - dot3(low, right))
         sides.append((low, split(dot3(first, right))))
     results = []
-    for first, second, (low, high) in zip(firsts, invert_128(seconds, works, beside, 8), sides):
+    for first, second, (low, high) in zip(firsts, invert_128(seconds, works, beside, 8, unroll), sides):
         corner = split(second)
         below = dot3(corner, low)
         top = jnp.concatenate([first + dot3(high, split(below)), -dot3(high, corner)], axis=1)
@@ -196,9 +196,10 @@
     return jnp.concatenate(scales, axis=1)
 
 
-def eliminate(systems, works):
+def eliminate(systems, works, beside, prepare):
     scales = [equilibrate(system[0]) for system in systems]
-    upper = invert_256([quarters(system[0][:HALF, :HALF]) for system in systems], works)
+    upper = invert_256([quarters(system[0][:HALF, :HALF]) for system in systems], works, beside)
+    prepare()
     lower = []
     for system, inverse, scale in zip(systems, upper, scales):
         pivot, parts, row = system[0], system[6], system[7]
@@ -244,7 +245,7 @@
 
 def front_kernel(
     side, diag, lower, arrow, pivot_out, pack_out, outer_out,
-    dv, lv, av, ga, gah, gal, zah, zal, pa, ra, gb, gbh, gbl, zbh, zbl, pb, rb, pivot, work, work_b, sems,
+    dv, lv, av, ga, gb, gh, gl, zh, zl, pa, pb, ra, rb, pivot, terms, work, work_b, sems,
 ):
     width, tip = diag.shape[1], arrow.shape[1]
     two = 2 * width
@@ -258,20 +259,27 @@
     ]
     for copy in copies:
         copy.start()
-    for copy in copies:
+    is_left = side[0] == 0
+    first = (dv.at[1], ga, gh.at[0], gl.at[0], zh.at[0], zl.at[0], pa, ra)
+    third = (dv.at[3], gb, gh.at[1], gl.at[1], zh.at[1], zl.at[1], pb, rb)
+    for copy in copies[:2]:
         copy.wait()
-    is_left = side[0] == 0
-
-    transpose_into(ga, 0, lv.at[0])
-    ga[width:two, :] = lv[1]
-    ga[two:, :] = av[1]
-    gb[:width, :] = lv[3]
-    transpose_into(gb, width, lv.at[2])
-    gb[two:, :] = av[3]
-    first = (dv.at[1], ga, gah, gal, zah, zal, pa, ra)
-    third = (dv.at[3], gb, gbh, gbl, zbh, zbl, pb, rb)
     outer_out[...] = dv[3]
-    eliminate([first, third], [work, work_b])
+
+    def nothing(slot):
+        pass
+
+    def couplings():
+        for copy in copies[2:]:
+            copy.wait()
+        transpose_into(ga, 0, lv.at[0])
+        ga[width:two, :] = lv[1]
+        ga[two:, :] = av[1]
+        gb[:width, :] = lv[3]
+        transpose_into(gb, width, lv.at[2])
+        gb[two:, :] = av[3]
+
+    eliminate([first, third], [work, work_b], nothing, couplings)
 
     def pick(left, right):
         return jnp.where(is_left, left, right)
@@ -279,55 +287,61 @@
     def drop(value):
         return jnp.where(is_left, value, jnp.zeros_like(value))
 
-    for start, size in chunks(width):
-        rows = pl.ds(start, size)
-        shared = pl.ds(width + start, size)
-        e = (width + start, size, width, width)
-        pivot[rows, :] = dv[2, rows, :] - update(first, *e) - drop(update(third, *e))
-        fe = (start, size, width, width)
-        near = -update(first, *fe)
-        far = -update(third, *fe)
-        ga[rows, :] = pick(near, lv[2, rows, :])
-        ga[shared, :] = pick(far, near)
-        ff = (start, size, 0, width)
-        near = dv[0, rows, :] - update(first, *ff)
-        far = -update(third, *ff)
-        pivot_out[rows, :] = pick(far, near)
-        outer_out[rows, :] = pick(near, outer_out[rows, :])
-    te = (two, tip, width, width)
-    ga[two:, :] = av[2] - update(first, *te) - drop(update(third, *te))
-    tf = (two, tip, 0, width)
-    near = av[0] - update(first, *tf)
-    far = -update(third, *tf)
-    tip_pivot = pick(far, near)
-    tip_outer = pick(near, av[3])
+    e = (width, width, width, width)
+    pivot[...] = dv[2] - update(first, *e) - drop(update(third, *e))
+
+    def rest(slot):
+        chain, piece, half = slot // 8, slot // 2 % 4, slot % 2
+        lanes = pl.ds(pl.multiple_of(half * HALF, HALF), HALF)
+        across = pl.ds(pl.multiple_of(piece * HALF, HALF), HALF)
+        column = pl.ds(pl.multiple_of((width + piece * HALF) % two, HALF), HALF)
+        right = (gh[chain, column, lanes], gl[chain, column, lanes])
+        for row, size, target in ((0, width, 0), (two, tip, width)):
+            rows, down = pl.ds(row, size), pl.ds(target, size)
+            term = dot3((zh[chain, rows, lanes], zl[chain, rows, lanes]), right, NT)
+            held = terms[chain, down, across]
+            terms[chain, down, across] = jnp.where(half == 0, 0.0, held) + term
+
     tt = (two, tip, two, tip)
-    tip_tip = -update(first, *tt) - drop(update(third, *tt))
-
-    second = (pivot, ga, gah, gal, zah, zal, pa, ra)
-    eliminate([second], [work])
-    for start, size in chunks(width):
-        rows = pl.ds(start, size)
-        pivot_out[rows, :] = pivot_out[rows, :] - update(second, width + start, size, width, width)
-        pack_out[rows, :] = -update(second, start, size, width, width)
-        outer_out[rows, :] = outer_out[rows, :] - update(second, start, size, 0, width)
-    pivot_out[width : width + tip, :] = tip_pivot - update(second, two, tip, width, width)
-    pivot_out[width + tip :, :] = jnp.zeros((tip, width), F32)
-    pivot_out[width + tip :, :tip] = tip_tip - update(second, *tt)
-    pack_out[width : width + tip, :] = tip_outer - update(second, two, tip, 0, width)
+
+    def fronts():
+        near, far = -terms[0, :width, :width], -terms[1, :width, :width]
+        ga[:width, :] = pick(near, lv[2])
+        ga[width:two, :] = pick(far, near)
+        ga[two:, :] = av[2] - terms[0, width:, :width] - drop(terms[1, width:, :width])
+        near, far = dv[0] - terms[0, :width, width:], -terms[1, :width, width:]
+        pivot_out[:width, :] = pick(far, near)
+        outer_out[...] = pick(near, outer_out[...])
+        near, far = av[0] - terms[0, width:, width:], -terms[1, width:, width:]
+        pivot_out[width : width + tip, :] = pick(far, near)
+        pack_out[width : width + tip, :] = pick(near, av[3])
+        pivot_out[width + tip :, :] = jnp.zeros((tip, width), F32)
+        pivot_out[width + tip :, :tip] = -update(first, *tt) - drop(update(third, *tt))
+
+    second = (pivot, ga, gh.at[0], gl.at[0], zh.at[0], zl.at[0], pa, ra)
+    eliminate([second], [work], rest, fronts)
+    pivot_out[:width, :] = pivot_out[:width, :] - update(second, width, width, width, width)
+    pack_out[:width, :] = -update(second, 0, width, width, width)
+    outer_out[...] = outer_out[...] - update(second, 0, width, 0, width)
+    at = pl.ds(width, tip)
+    pivot_out[at, :] = pivot_out[at, :] - update(second, two, tip, width, width)
+    pack_out[at, :] = pack_out[at, :] - update(second, two, tip, 0, width)
+    at = pl.ds(width + tip, tip)
+    pivot_out[at, :tip] = pivot_out[at, :tip] - update(second, *tt)
     spill = pack_out.shape[0] - width - tip
     pack_out[width + tip :, :] = outer_out[:spill, :]
 
 
 def invert_512(pivot, work):
     scale = equilibrate(pivot)
-    (first,) = invert_256([quarters(pivot[:HALF, :HALF])], [work])
+    (first,) = invert_256([quarters(pivot[:HALF, :HALF])], [work], unroll=7)
     right = split(pivot[:HALF, HALF:])
     below = split(pivot[HALF:, :HALF])
     upper = split(first)
     low = split(dot3(below, upper))
     high = split(dot3(upper, right))
-    (second,) = invert_256([quarters(pivot[HALF:, HALF:] - dot3(low, right))], [work])
+    last = pivot[HALF:, HALF:] - dot3(low, right)
+    (second,) = invert_256([quarters(last)], [work], unroll=7)
     corner = split(second)
     below = dot3(corner, low)
     pivot[:HALF, :HALF] = first + dot3(high, split(below))
@@ -445,8 +459,6 @@
     smem = pl.BlockSpec(memory_space=pltpu.SMEM)
     vmem = pl.BlockSpec(memory_space=pltpu.VMEM)
     parts = [pltpu.VMEM((front, width), BF16)] * 4
-    system = [pltpu.VMEM((front, width), F32)] + parts
-    system += [pltpu.VMEM((4, HALF, HALF), BF16), pltpu.VMEM((1, width), F32)]
     params = pltpu.CompilerParams(vmem_limit_bytes=56 * 2**20)
     pivot, pack, outer = pl.pallas_call(
         front_kernel,
@@ -462,9 +474,11 @@
             pltpu.VMEM((count, width, width), F32),
             pltpu.VMEM((count, tip, width), F32),
         ]
-        + system
-        + system
-        + [pltpu.VMEM((width, width), F32)]
+        + [pltpu.VMEM((front, width), F32)] * 2
+        + [pltpu.VMEM((2, front, width), BF16)] * 4
+        + [pltpu.VMEM((4, HALF, HALF), BF16)] * 2
+        + [pltpu.VMEM((1, width), F32)] * 2
+        + [pltpu.VMEM((width, width), F32), pltpu.VMEM((2, width + tip, 2 * width), F32)]
         + [pltpu.VMEM((LANES, LANES), F32)] * 2
         + [pltpu.SemaphoreType.DMA((3 * count,))],
         compiler_params=params,

time: 108 us -> 103 us (0.954)
  Pallas kernels: 89.2 us -> 84 us
    pallas_call x1, Pallas kernels: 62.7 us -> 58.3 us  [local(): pl.pallas_call(front_kernel, out_shape=[jax.ShapeDtypeStruct((width + 2 *...]
  transfers between devices with their start and end apart: 8 -> 8, of which waited for: 4 -> 4; matrix products, arithmetic and copies ran while one was open for 0% -> 0% of each run, Pallas kernels for 24% -> 25%
where the time goes in v9:
time: 103 us
  Pallas kernels  84 us (82%)
  starting transfers between devices  9.56 us (9%)
  waiting for transfers between devices  6.58 us (6%)
  local copies, waits for them, and re-layouts  1.33 us (1%)
    pallas_call x1, Pallas kernels, local(): pl.pallas_call(front_kernel, out_shape=[jax.ShapeDtypeStruct((width + 2 *...  58.3 us
    pallas_call x1, Pallas kernels, local(): pl.pallas_call(factor_kernel, out_shape=[jax.ShapeDtypeStruct((width, wid...  19.8 us
    ppermute x8, starting transfers between devices, swapped(): return lax.ppermute(value, axis, [(k, k ^ mask) for k in range(count)])  9.56 us
    ppermute x8, waiting for transfers between devices, swapped(): return lax.ppermute(value, axis, [(k, k ^ mask) for k in range(count)])  6.58 us
    pallas_call x1, Pallas kernels, local(): pl.pallas_call(merge_kernel, out_shape=jax.ShapeDtypeStruct((half, front)...  5.9 us
  transfers between devices with their start and end apart: 8, of which 4 were waited for; matrix products, arithmetic and copies ran while one was open for 0% of the time, Pallas kernels for 25%

profile of v9, /device:TPU:0, one launch (start us, length us, event | category | flops | bytes accessed | tf_op | source)
XLA Modules:
  0.0 102.8 jit_solution(12456108198063271798)
XLA Ops:
  0.6 58.3 %front.1 = (f32[640,512]{1,0:T(8,128)}, f32[608,512]{1,0:T(8,128)}, f32[512,512]{1,0:T(8,128)}) custom-call(s32[1]{0:T(128)} %bitcast.side, f32[4,512,512]{2,1,0:T(8,128)} %diag.1, f32[4,512,512]{2,1,0:T(8,128)} %lower.1, f32[4,64,512]{2,1,0:T(8,128)} %arrow.1), custom_call_target="tpu_custom_call" | custom-call | tf_op jit(solution)/shard_map/front/pallas_call | solution.py:463
  58.9 0.5 collective-permute-start
  59.4 0.1 collective-permute-start.1
  59.5 2.8 %collective-permute-done.other.pivot_other = f32[640,512]{1,0:T(8,128)S(1)} collective-permute-done((f32[640,512]{1,0:T(8,128)}, f32[640,512]{1,0:T(8,128)S(1)}, u32[]{:S(2)}, u32[]{:S(2)}) %collective-permute-start) | collective-permute-done | bytes 1310752 | tf_op jit(solution)/shard_map/ppermute | solution.py:436
  62.3 1.3 %copy-done = f32[640,512]{1,0:T(8,128)S(1)} copy-done((f32[640,512]{1,0:T(8,128)S(1)}, f32[640,512]{1,0:T(8,128)}, u32[]{:S(2)}) %copy-start) | copy-done | bytes 1310744
  63.6 19.8 %factor.1 = (f32[512,512]{1,0:T(8,128)S(1)}, f32[64,64]{1,0:T(8,128)S(1)}) custom-call(f32[640,512]{1,0:T(8,128)S(1)} %copy-done, f32[640,512]{1,0:T(8,128)S(1)} %collective-permute-done.other.pivot_other), custom_call_target="tpu_custom_call" | custom-call | flops 10000000000 | bytes 10000000 | tf_op jit(solution)/shard_map/factor/pallas_call | solution.py:489
  83.5 3.9 %collective-permute-start.4 = (f32[64,64]{1,0:T(8,128)S(1)}, f32[64,64]{1,0:T(8,128)S(1)}, u32[]{:S(2)}, u32[]{:S(2)}) collective-permute-start(f32[64,64]{1,0:T(8,128)S(1)} %get-tuple-element.9.tip_tip), channel_id=1, source_target_pairs={{0,6},{1,7},{2,4},{3,5},{4,2},{5,3},{6,0},{7,1},{8,14},{9,15},{10,... | collective-permute-start | bytes 49160 | tf_op jit(solution)/shard_map/ppermute | solution.py:436
  87.3 0.5 collective-permute-start.3
  87.9 0.1 collective-permute-start.2
  88.0 1.3 %collective-permute-done.4 = f32[64,64]{1,0:T(8,128)S(1)} collective-permute-done((f32[64,64]{1,0:T(8,128)S(1)}, f32[64,64]{1,0:T(8,128)S(1)}, u32[]{:S(2)}, u32[]{:S(2)}) %collective-permute-start.4) | collective-permute-done | bytes 16416 | tf_op jit(solution)/shard_map/ppermute | solution.py:436
  89.2 2.0 %collective-permute-done.3 = f32[64,64]{1,0:T(8,128)S(1)} collective-permute-done((f32[64,64]{1,0:T(8,128)S(1)}, f32[64,64]{1,0:T(8,128)S(1)}, u32[]{:S(2)}, u32[]{:S(2)}) %collective-permute-start.3) | collective-permute-done | bytes 16416 | tf_op jit(solution)/shard_map/ppermute | solution.py:436
  91.3 0.5 collective-permute-done.2
  91.8 3.7 %collective-permute-start.7 = (f32[64,64]{1,0:T(8,128)S(1)}, f32[64,64]{1,0:T(8,128)S(1)}, u32[]{:S(2)}, u32[]{:S(2)}) collective-permute-start(f32[64,64]{1,0:T(8,128)S(1)} %add_add_fusion.1), channel_id=1, source_target_pairs={{0,24},{1,25},{2,26},{3,27},{4,28},{5,29},{6,30},{7,31},{8,16},{9,... | collective-permute-start | bytes 49160 | tf_op jit(solution)/shard_map/ppermute | solution.py:436
  95.4 0.0 collective-permute-start.6
  95.4 0.8 collective-permute-start.5
  96.2 0.0 collective-permute-done.1.pack_other
  96.2 0.0 copy-done.1
  96.2 0.0 copy-done.3
  96.3 0.0 copy-start.4
  96.3 5.9 %merge.1 = f32[544,1088]{1,0:T(8,128)} custom-call(s32[1]{0:T(128)} %bitcast.side, f32[512,512]{1,0:T(8,128)S(1)} %get-tuple-element.8.inverse, f32[64,64]{1,0:T(8,128)S(1)} %get-tuple-element.9.tip_tip, f32[640,512]{1,0:T(8,128)S(1)} %copy-done.1, f32[640,512]{1,0:T(8,128)S(1)} %collective-permute-done.other.pivot_other, f32[608,512]{1,0:T(8,128)S(1)} %copy-done.2, ...), custom_call_target="tpu_custom_call" | custom-call | flops 5000000000 | bytes 10000000 | tf_op jit(solution)/shard_map/merge/pallas_call | solution.py:502
  102.2 0.0 collective-permute-done.7
  102.2 0.0 collective-permute-done.6
  102.2 0.0 collective-permute-done.5
  102.2 0.6 add_add_fusion
  (7 shorter events, 0.0 us)
Async XLA Ops:
  58.9 3.4 %collective-permute-start = (f32[640,512]{1,0:T(8,128)}, f32[640,512]{1,0:T(8,128)S(1)}, u32[]{:S(2)}, u32[]{:S(2)}) collective-permute-start(f32[640,512]{1,0:T(8,128)} %get-tuple-element.7.mine.pivot_mine), channel_id=1, source_target_pairs={{0,1},{1,0},{2,3},{3,2},{4,5},{5,4},{6,7},{7,6},{8,9},{9,8},{10,11... | collective-permute-start | bytes 3932168 | tf_op jit(solution)/shard_map/ppermute | solution.py:436
  59.4 36.8 %collective-permute-start.1 = (f32[608,512]{1,0:T(8,128)}, f32[608,512]{1,0:T(8,128)S(1)}, u32[]{:S(2)}, u32[]{:S(2)}) collective-permute-start(f32[608,512]{1,0:T(8,128)} %get-tuple-element.10.pack_mine), channel_id=1, source_target_pairs={{0,1},{1,0},{2,3},{3,2},{4,5},{5,4},{6,7},{7,6},{8,9},{9,8},{10,11... | collective-permute-start | bytes 3735560 | tf_op jit(solution)/shard_map/ppermute | solution.py:436
  62.3 1.3 %copy-start = (f32[640,512]{1,0:T(8,128)S(1)}, f32[640,512]{1,0:T(8,128)}, u32[]{:S(2)}) copy-start(f32[640,512]{1,0:T(8,128)} %get-tuple-element.7.mine.pivot_mine) | copy-start | bytes 3932164
  63.6 32.6 %copy-start.1 = (f32[640,512]{1,0:T(8,128)S(1)}, f32[640,512]{1,0:T(8,128)}, u32[]{:S(2)}) copy-start(f32[640,512]{1,0:T(8,128)} %get-tuple-element.7.mine.pivot_mine) | copy-start | bytes 3932164
  63.6 32.6 %copy-start.2 = (f32[608,512]{1,0:T(8,128)S(1)}, f32[608,512]{1,0:T(8,128)}, u32[]{:S(2)}) copy-start(f32[608,512]{1,0:T(8,128)} %get-tuple-element.10.pack_mine) | copy-start | bytes 3735556
  63.6 32.6 %copy-start.3 = (f32[512,512]{1,0:T(8,128)S(1)}, f32[512,512]{1,0:T(8,128)}, u32[]{:S(2)}) copy-start(f32[512,512]{1,0:T(8,128)} %get-tuple-element.11.outer_mine) | copy-start | bytes 3145732
  83.5 5.8 %collective-permute-start.4 = (f32[64,64]{1,0:T(8,128)S(1)}, f32[64,64]{1,0:T(8,128)S(1)}, u32[]{:S(2)}, u32[]{:S(2)}) collective-permute-start(f32[64,64]{1,0:T(8,128)S(1)} %get-tuple-element.9.tip_tip), channel_id=1, source_target_pairs={{0,6},{1,7},{2,4},{3,5},{4,2},{5,3},{6,0},{7,1},{8,14},{9,15},{10,... | collective-permute-start | bytes 49160 | tf_op jit(solution)/shard_map/ppermute | solution.py:436
  87.3 3.9 %collective-permute-start.3 = (f32[64,64]{1,0:T(8,128)S(1)}, f32[64,64]{1,0:T(8,128)S(1)}, u32[]{:S(2)}, u32[]{:S(2)}) collective-permute-start(f32[64,64]{1,0:T(8,128)S(1)} %get-tuple-element.9.tip_tip), channel_id=1, source_target_pairs={{0,4},{1,5},{2,6},{3,7},{4,0},{5,1},{6,2},{7,3},{8,12},{9,13},{10,... | collective-permute-start | bytes 49160 | tf_op jit(solution)/shard_map/ppermute | solution.py:436
  87.9 3.9 %collective-permute-start.2 = (f32[64,64]{1,0:T(8,128)S(1)}, f32[64,64]{1,0:T(8,128)S(1)}, u32[]{:S(2)}, u32[]{:S(2)}) collective-permute-start(f32[64,64]{1,0:T(8,128)S(1)} %get-tuple-element.9.tip_tip), channel_id=1, source_target_pairs={{0,2},{1,3},{2,0},{3,1},{4,6},{5,7},{6,4},{7,5},{8,10},{9,11},{10,... | collective-permute-start | bytes 49160 | tf_op jit(solution)/shard_map/ppermute | solution.py:436
  91.8 10.4 %collective-permute-start.7 = (f32[64,64]{1,0:T(8,128)S(1)}, f32[64,64]{1,0:T(8,128)S(1)}, u32[]{:S(2)}, u32[]{:S(2)}) collective-permute-start(f32[64,64]{1,0:T(8,128)S(1)} %add_add_fusion.1), channel_id=1, source_target_pairs={{0,24},{1,25},{2,26},{3,27},{4,28},{5,29},{6,30},{7,31},{8,16},{9,... | collective-permute-start | bytes 49160 | tf_op jit(solution)/shard_map/ppermute | solution.py:436
  95.4 6.7 %collective-permute-start.6 = (f32[64,64]{1,0:T(8,128)S(1)}, f32[64,64]{1,0:T(8,128)S(1)}, u32[]{:S(2)}, u32[]{:S(2)}) collective-permute-start(f32[64,64]{1,0:T(8,128)S(1)} %add_add_fusion.1), channel_id=1, source_target_pairs={{0,16},{1,17},{2,18},{3,19},{4,20},{5,21},{6,22},{7,23},{8,24},{9,... | collective-permute-start | bytes 49160 | tf_op jit(solution)/shard_map/ppermute | solution.py:436
  95.4 6.7 %collective-permute-start.5 = (f32[64,64]{1,0:T(8,128)S(1)}, f32[64,64]{1,0:T(8,128)S(1)}, u32[]{:S(2)}, u32[]{:S(2)}) collective-permute-start(f32[64,64]{1,0:T(8,128)S(1)} %add_add_fusion.1), channel_id=1, source_target_pairs={{0,8},{1,9},{2,10},{3,11},{4,12},{5,13},{6,14},{7,15},{8,0},{9,1},... | collective-permute-start | bytes 49160 | tf_op jit(solution)/shard_map/ppermute | solution.py:436
  96.3 5.9 %copy-start.4 = (f32[64,64]{1,0:T(8,128)S(1)}, f32[64,64]{1,0:T(8,128)}, u32[]{:S(2)}) copy-start(f32[64,64]{1,0:T(8,128)} %param.7) | copy-start | bytes 49156

commit v10 on v9

--- a/solution.py
+++ b/solution.py
@@ -369,66 +369,59 @@
 
 
 def merge_kernel(
-    side, inverse, tip_tip, pivot_mine, pivot_other, pack_mine, pack_other, outer_mine, merged,
-    gh, gl, zh, zl,
+    start, side, inverse, pivot_mine, pivot_other, pack_mine, pack_other, outer_mine, *refs
 ):
-    width, tip = inverse.shape[0], tip_tip.shape[0]
+    merged, gh, gl, out, sem = refs[-5:]
+    width = inverse.shape[0]
+    tip = (pivot_mine.shape[0] - width) // 2
     two = 2 * width
-    half = merged.shape[0]
+    half = (two + tip) // 2
     spill = half - width
+    count = out.shape[0]
     is_left = side[0] == 0
-    for start, size in chunks(width):
-        rows = pl.ds(start, size)
+    for row, size in chunks(width):
+        rows = pl.ds(row, size)
         mine, other = split(pack_mine[rows, :]), split(pack_other[rows, :])
         gh[rows, :] = jnp.where(is_left, mine[0], other[0])
         gl[rows, :] = jnp.where(is_left, mine[1], other[1])
-        rows = pl.ds(width + start, size)
+        rows = pl.ds(width + row, size)
         gh[rows, :] = jnp.where(is_left, other[0], mine[0])
         gl[rows, :] = jnp.where(is_left, other[1], mine[1])
     at = pl.ds(width, tip)
     gh[two:, :], gl[two:, :] = split(pivot_mine[at, :] + pivot_other[at, :])
-    solver = split(inverse[...])
-    system = (None, None, gh, gl, zh, zl)
     outer_tip = pl.ds(width, tip)
-
-    def solve(start, size):
-        rows = pl.ds(start, size)
-        zh[rows, :], zl[rows, :] = split(dot3((gh[rows, :], gl[rows, :]), solver))
 
     @pl.when(is_left)
     def _():
-        for start, size in chunks(half):
-            solve(start, size)
-        for start, size in chunks(width):
-            rows = pl.ds(start, size)
-            merged[rows, :width] = outer_mine[rows, :] - update(system, start, size, 0, width)
-            merged[rows, width:two] = -update(system, start, size, width, width)
-            mine = pack_mine[outer_tip, start : start + size].T
-            merged[rows, two:] = mine - update(system, start, size, two, tip)
-        merged[width:, :width] = -update(system, width, spill, 0, width)
-        other = pack_other[width + tip :, :]
-        merged[width:, width:two] = other - update(system, width, spill, width, width)
-        other = pack_other[outer_tip, :LANES].T[:spill, :]
-        merged[width:, two:] = other - update(system, width, spill, two, tip)
+        size = min(count, width - start)
+        out[:size, :width] = outer_mine[start : start + size, :]
+        out[:size, width:two] = jnp.zeros((size, width), F32)
+        out[:size, two:] = pack_mine[outer_tip, start : start + size].T
+        if size < count:
+            out[size:, :width] = jnp.zeros((spill, width), F32)
+            out[size:, width:two] = pack_other[width + tip :, :]
+            out[size:, two:] = pack_other[outer_tip, :LANES].T[:spill, :]
 
     @pl.when(jnp.logical_not(is_left))
     def _():
-        for start, size in chunks(width + tip):
-            solve(width + start, size)
-        for start, size in chunks(width):
-            skip = spill if start == 0 else 0
-            rows = pl.ds(start + skip - spill, size - skip)
-            merged[rows, :width] = -update(system, width + start, size, 0, width)[skip:, :]
-            mine = outer_mine[pl.ds(start, size), :]
-            merged[rows, width:two] = (
-                mine - update(system, width + start, size, width, width)
-            )[skip:, :]
-            mine = pack_mine[outer_tip, start : start + size].T
-            merged[rows, two:] = (mine - update(system, width + start, size, two, tip))[skip:, :]
-        rows = pl.ds(half - tip, tip)
-        merged[rows, :width] = pack_other[outer_tip, :] - update(system, two, tip, 0, width)
-        merged[rows, width:two] = pack_mine[outer_tip, :] - update(system, two, tip, width, width)
-        merged[rows, two:] = tip_tip[...]
+        size = min(count, half - tip - start)
+        first = start + spill
+        out[:size, :width] = jnp.zeros((size, width), F32)
+        out[:size, width:two] = outer_mine[first : first + size, :]
+        out[:size, two:] = pack_mine[outer_tip, :].T[first : first + size, :]
+        if size < count:
+            out[size:, :width] = pack_other[outer_tip, :]
+            out[size:, width:two] = pack_mine[outer_tip, :]
+            at = pl.ds(width + tip, tip)
+            out[size:, two:] = pivot_mine[at, :tip] + pivot_other[at, :tip]
+
+    rows = pl.ds(pl.multiple_of(side[0] * half + start, PAIR), count)
+    solved = split(dot3((gh[rows, :], gl[rows, :]), split(inverse[...])))
+    for lanes in (pl.ds(0, two), pl.ds(two, tip)):
+        out[:, lanes] = out[:, lanes] - dot3(solved, (gh[lanes, :], gl[lanes, :]), NT)
+    copy = pltpu.make_async_copy(out, merged.at[pl.ds(start, count), :], sem)
+    copy.start()
+    copy.wait()
 
 
 def swapped(value, axis, mask):
@@ -499,16 +492,21 @@
         cost_estimate=pl.CostEstimate(flops=10**10, bytes_accessed=10**7, transcendentals=0),
         name="factor",
     )(pivot, pivot_other)
-    merged = pl.pallas_call(
-        merge_kernel,
-        out_shape=jax.ShapeDtypeStruct((half, front), F32),
-        in_specs=[smem] + [vmem] * 7,
-        out_specs=vmem,
-        scratch_shapes=parts,
-        compiler_params=pltpu.CompilerParams(vmem_limit_bytes=40 * 2**20),
-        cost_estimate=pl.CostEstimate(flops=5 * 10**9, bytes_accessed=10**7, transcendentals=0),
-        name="merge",
-    )(side, inverse, tip_tip, pivot, pivot_other, pack, pack_other, outer)
+    operands = [side, inverse, pivot, pivot_other, pack, pack_other, outer]
+    anywhere = pl.BlockSpec(memory_space=pl.ANY)
+    for start, size in ((0, HALF), (HALF, half - HALF)):
+        merged = pl.pallas_call(
+            functools.partial(merge_kernel, start),
+            out_shape=jax.ShapeDtypeStruct((half, front), F32),
+            in_specs=[smem] + [vmem] * 6 + [anywhere] * (start > 0),
+            out_specs=anywhere,
+            scratch_shapes=parts[:2] + [pltpu.VMEM((size, front), F32), pltpu.SemaphoreType.DMA],
+            input_output_aliases={7: 0} if start else {},
+            compiler_params=pltpu.CompilerParams(vmem_limit_bytes=40 * 2**20),
+            cost_estimate=pl.CostEstimate(flops=10**10, bytes_accessed=10**7, transcendentals=0),
+            name="merge",
+        )(*operands)
+        operands.append(merged)
     return merged, tip_block + sum_over_pairs(tip_tip, "tm")
 
 

time: 103 us -> 101 us (0.981)
  waiting for transfers between devices: 6.58 us -> 3.37 us
  Pallas kernels: 84 us -> 85.4 us
    ppermute x8, waiting for transfers between devices: 6.58 us -> 3.37 us  [swapped(): return lax.ppermute(value, axis, [(k, k ^ mask) for k in range(count)])]
    pallas_call x1 -> x2, Pallas kernels: 5.9 us -> 7.32 us  [local(): pl.pallas_call(functools.partial(merge_kernel, start), out_shape=jax.Shap...]
  transfers between devices with their start and end apart: 8 -> 8, of which waited for: 4 -> 3; matrix products, arithmetic and copies ran while one was open for 0% -> 0% of each run, Pallas kernels for 25% -> 27%
where the time goes in v10:
time: 101 us
  Pallas kernels  85.4 us (85%)
  starting transfers between devices  9.63 us (10%)
  waiting for transfers between devices  3.37 us (3%)
  local copies, waits for them, and re-layouts  1.33 us (1%)
    pallas_call x1, Pallas kernels, local(): pl.pallas_call(front_kernel, out_shape=[jax.ShapeDtypeStruct((width + 2 *...  58.3 us
    pallas_call x1, Pallas kernels, local(): pl.pallas_call(factor_kernel, out_shape=[jax.ShapeDtypeStruct((width, wid...  19.8 us
    ppermute x8, starting transfers between devices, swapped(): return lax.ppermute(value, axis, [(k, k ^ mask) for k in range(count)])  9.63 us
    pallas_call x2, Pallas kernels, local(): pl.pallas_call(functools.partial(merge_kernel, start), out_shape=jax.Shap...  7.32 us
    ppermute x8, waiting for transfers between devices, swapped(): return lax.ppermute(value, axis, [(k, k ^ mask) for k in range(count)])  3.37 us
  transfers between devices with their start and end apart: 8, of which 3 were waited for; matrix products, arithmetic and copies ran while one was open for 0% of the time, Pallas kernels for 27%

profile of v10, /device:TPU:0, one launch (start us, length us, event | category | flops | bytes accessed | tf_op | source)
XLA Modules:
  0.0 101.1 jit_solution(6480199745578177985)
XLA Ops:
  0.6 58.3 %front.1 = (f32[640,512]{1,0:T(8,128)}, f32[608,512]{1,0:T(8,128)}, f32[512,512]{1,0:T(8,128)}) custom-call(s32[1]{0:T(128)} %bitcast.side, f32[4,512,512]{2,1,0:T(8,128)} %diag.1, f32[4,512,512]{2,1,0:T(8,128)} %lower.1, f32[4,64,512]{2,1,0:T(8,128)} %arrow.1), custom_call_target="tpu_custom_call" | custom-call | tf_op jit(solution)/shard_map/front/pallas_call | solution.py:456
  58.9 0.5 collective-permute-start
  59.4 0.1 collective-permute-start.1
  59.5 2.8 %collective-permute-done.other.pivot_other = f32[640,512]{1,0:T(8,128)S(1)} collective-permute-done((f32[640,512]{1,0:T(8,128)}, f32[640,512]{1,0:T(8,128)S(1)}, u32[]{:S(2)}, u32[]{:S(2)}) %collective-permute-start) | collective-permute-done | bytes 1310752 | tf_op jit(solution)/shard_map/ppermute | solution.py:429
  62.3 1.3 %copy-done = f32[640,512]{1,0:T(8,128)S(1)} copy-done((f32[640,512]{1,0:T(8,128)S(1)}, f32[640,512]{1,0:T(8,128)}, u32[]{:S(2)}) %copy-start) | copy-done | bytes 1310744
  63.6 19.8 %factor.1 = (f32[512,512]{1,0:T(8,128)S(1)}, f32[64,64]{1,0:T(8,128)S(1)}) custom-call(f32[640,512]{1,0:T(8,128)S(1)} %copy-done, f32[640,512]{1,0:T(8,128)S(1)} %collective-permute-done.other.pivot_other), custom_call_target="tpu_custom_call" | custom-call | flops 10000000000 | bytes 10000000 | tf_op jit(solution)/shard_map/factor/pallas_call | solution.py:482
  83.5 3.9 %collective-permute-start.4 = (f32[64,64]{1,0:T(8,128)S(1)}, f32[64,64]{1,0:T(8,128)S(1)}, u32[]{:S(2)}, u32[]{:S(2)}) collective-permute-start(f32[64,64]{1,0:T(8,128)S(1)} %get-tuple-element.11), channel_id=1, source_target_pairs={{0,6},{1,7},{2,4},{3,5},{4,2},{5,3},{6,0},{7,1},{8,14},{9,15},{10,... | collective-permute-start | bytes 49160 | tf_op jit(solution)/shard_map/ppermute | solution.py:429
  87.3 0.5 collective-permute-start.3
  87.9 0.1 collective-permute-start.2
  88.0 0.0 collective-permute-done.1.pack_other
  88.0 0.0 copy-done.2
  88.0 3.5 %merge.2.refs_0_ = f32[544,1088]{1,0:T(8,128)} custom-call(s32[1]{0:T(128)} %bitcast.side, f32[512,512]{1,0:T(8,128)S(1)} %get-tuple-element.8.inverse, f32[640,512]{1,0:T(8,128)S(1)} %copy-done.1, f32[640,512]{1,0:T(8,128)S(1)} %collective-permute-done.other.pivot_other, f32[608,512]{1,0:T(8,128)S(1)} %copy-done.2, ...), custom_call_target="tpu_custom_call" | custom-call | flops 10000000000 | bytes 10000000 | tf_op jit(solution)/shard_map/merge/pallas_call | solution.py:498
  91.6 0.0 collective-permute-done.4
  91.6 0.0 collective-permute-done.3
  91.6 0.2 collective-permute-done.2
  91.8 0.0 copy-start.4
  91.8 3.9 %collective-permute-start.7 = (f32[64,64]{1,0:T(8,128)S(1)}, f32[64,64]{1,0:T(8,128)S(1)}, u32[]{:S(2)}, u32[]{:S(2)}) collective-permute-start(f32[64,64]{1,0:T(8,128)S(1)} %add_add_fusion.1), channel_id=1, source_target_pairs={{0,24},{1,25},{2,26},{3,27},{4,28},{5,29},{6,30},{7,31},{8,16},{9,... | collective-permute-start | bytes 49160 | tf_op jit(solution)/shard_map/ppermute | solution.py:429
  95.7 0.0 collective-permute-start.6
  95.7 0.6 collective-permute-start.5
  96.3 3.8 %merge.3 = f32[544,1088]{1,0:T(8,128)} custom-call(s32[1]{0:T(128)} %bitcast.side, f32[512,512]{1,0:T(8,128)S(1)} %get-tuple-element.8.inverse, f32[640,512]{1,0:T(8,128)S(1)} %copy-done.1, f32[640,512]{1,0:T(8,128)S(1)} %collective-permute-done.other.pivot_other, f32[608,512]{1,0:T(8,128)S(1)} %copy-done.2, ...), custom_call_target="tpu_custom_call", output_to_operand_aliasing={{}: (7, {})} | custom-call | flops 10000000000 | bytes 10000000 | tf_op jit(solution)/shard_map/merge/pallas_call | solution.py:498
  100.1 0.0 collective-permute-done.7
  100.1 0.4 collective-permute-done.6
  100.5 0.0 collective-permute-done.5
  100.5 0.6 add_add_fusion
  (8 shorter events, 0.0 us)
Async XLA Ops:
  58.9 3.4 %collective-permute-start = (f32[640,512]{1,0:T(8,128)}, f32[640,512]{1,0:T(8,128)S(1)}, u32[]{:S(2)}, u32[]{:S(2)}) collective-permute-start(f32[640,512]{1,0:T(8,128)} %get-tuple-element.7.mine.pivot_mine), channel_id=1, source_target_pairs={{0,1},{1,0},{2,3},{3,2},{4,5},{5,4},{6,7},{7,6},{8,9},{9,8},{10,11... | collective-permute-start | bytes 3932168 | tf_op jit(solution)/shard_map/ppermute | solution.py:429
  59.4 28.6 %collective-permute-start.1 = (f32[608,512]{1,0:T(8,128)}, f32[608,512]{1,0:T(8,128)S(1)}, u32[]{:S(2)}, u32[]{:S(2)}) collective-permute-start(f32[608,512]{1,0:T(8,128)} %get-tuple-element.9.pack_mine), channel_id=1, source_target_pairs={{0,1},{1,0},{2,3},{3,2},{4,5},{5,4},{6,7},{7,6},{8,9},{9,8},{10,11... | collective-permute-start | bytes 3735560 | tf_op jit(solution)/shard_map/ppermute | solution.py:429
  62.3 1.3 %copy-start = (f32[640,512]{1,0:T(8,128)S(1)}, f32[640,512]{1,0:T(8,128)}, u32[]{:S(2)}) copy-start(f32[640,512]{1,0:T(8,128)} %get-tuple-element.7.mine.pivot_mine) | copy-start | bytes 3932164
  63.6 24.4 %copy-start.1 = (f32[640,512]{1,0:T(8,128)S(1)}, f32[640,512]{1,0:T(8,128)}, u32[]{:S(2)}) copy-start(f32[640,512]{1,0:T(8,128)} %get-tuple-element.7.mine.pivot_mine) | copy-start | bytes 3932164
  63.6 24.4 %copy-start.2 = (f32[608,512]{1,0:T(8,128)S(1)}, f32[608,512]{1,0:T(8,128)}, u32[]{:S(2)}) copy-start(f32[608,512]{1,0:T(8,128)} %get-tuple-element.9.pack_mine) | copy-start | bytes 3735556
  63.6 24.4 %copy-start.3 = (f32[512,512]{1,0:T(8,128)S(1)}, f32[512,512]{1,0:T(8,128)}, u32[]{:S(2)}) copy-start(f32[512,512]{1,0:T(8,128)} %get-tuple-element.10.outer_mine) | copy-start | bytes 3145732
  83.5 8.1 %collective-permute-start.4 = (f32[64,64]{1,0:T(8,128)S(1)}, f32[64,64]{1,0:T(8,128)S(1)}, u32[]{:S(2)}, u32[]{:S(2)}) collective-permute-start(f32[64,64]{1,0:T(8,128)S(1)} %get-tuple-element.11), channel_id=1, source_target_pairs={{0,6},{1,7},{2,4},{3,5},{4,2},{5,3},{6,0},{7,1},{8,14},{9,15},{10,... | collective-permute-start | bytes 49160 | tf_op jit(solution)/shard_map/ppermute | solution.py:429
  87.3 4.2 %collective-permute-start.3 = (f32[64,64]{1,0:T(8,128)S(1)}, f32[64,64]{1,0:T(8,128)S(1)}, u32[]{:S(2)}, u32[]{:S(2)}) collective-permute-start(f32[64,64]{1,0:T(8,128)S(1)} %get-tuple-element.11), channel_id=1, source_target_pairs={{0,4},{1,5},{2,6},{3,7},{4,0},{5,1},{6,2},{7,3},{8,12},{9,13},{10,... | collective-permute-start | bytes 49160 | tf_op jit(solution)/shard_map/ppermute | solution.py:429
  87.9 3.9 %collective-permute-start.2 = (f32[64,64]{1,0:T(8,128)S(1)}, f32[64,64]{1,0:T(8,128)S(1)}, u32[]{:S(2)}, u32[]{:S(2)}) collective-permute-start(f32[64,64]{1,0:T(8,128)S(1)} %get-tuple-element.11), channel_id=1, source_target_pairs={{0,2},{1,3},{2,0},{3,1},{4,6},{5,7},{6,4},{7,5},{8,10},{9,11},{10,... | collective-permute-start | bytes 49160 | tf_op jit(solution)/shard_map/ppermute | solution.py:429
  91.8 8.7 %copy-start.4 = (f32[64,64]{1,0:T(8,128)S(1)}, f32[64,64]{1,0:T(8,128)}, u32[]{:S(2)}) copy-start(f32[64,64]{1,0:T(8,128)} %param.7) | copy-start | bytes 49156
  91.8 8.3 %collective-permute-start.7 = (f32[64,64]{1,0:T(8,128)S(1)}, f32[64,64]{1,0:T(8,128)S(1)}, u32[]{:S(2)}, u32[]{:S(2)}) collective-permute-start(f32[64,64]{1,0:T(8,128)S(1)} %add_add_fusion.1), channel_id=1, source_target_pairs={{0,24},{1,25},{2,26},{3,27},{4,28},{5,29},{6,30},{7,31},{8,16},{9,... | collective-permute-start | bytes 49160 | tf_op jit(solution)/shard_map/ppermute | solution.py:429
  95.7 4.8 %collective-permute-start.6 = (f32[64,64]{1,0:T(8,128)S(1)}, f32[64,64]{1,0:T(8,128)S(1)}, u32[]{:S(2)}, u32[]{:S(2)}) collective-permute-start(f32[64,64]{1,0:T(8,128)S(1)} %add_add_fusion.1), channel_id=1, source_target_pairs={{0,16},{1,17},{2,18},{3,19},{4,20},{5,21},{6,22},{7,23},{8,24},{9,... | collective-permute-start | bytes 49160 | tf_op jit(solution)/shard_map/ppermute | solution.py:429
  95.7 4.8 %collective-permute-start.5 = (f32[64,64]{1,0:T(8,128)S(1)}, f32[64,64]{1,0:T(8,128)S(1)}, u32[]{:S(2)}, u32[]{:S(2)}) collective-permute-start(f32[64,64]{1,0:T(8,128)S(1)} %add_add_fusion.1), channel_id=1, source_target_pairs={{0,8},{1,9},{2,10},{3,11},{4,12},{5,13},{6,14},{7,15},{8,0},{9,1},... | collective-permute-start | bytes 49160 | tf_op jit(solution)/shard_map/ppermute | solution.py:429
